TPU v7x, 32 devices: a whole 2x2x4 slice. The times are simulated.
32 devices in a mesh: seq: 8 (over z, x), stream: 4 (over y, core).
Axes of the slice: x: 2, y: 2, z: 4, core: 2. Of those that a mesh axis runs over, the one named last changes fastest.
Arguments:
- inputs: bfloat16 [4, 4096, 2304], P('stream', 'seq'), may hold values from -12 to 12
- boundary: int32 [4, 4096], P('stream', 'seq'), may hold values from 0 to 1, as said below
- start_state: float32 [4, 2304], P('stream'), may hold values from -3 to 3
- weight: float32 [2, 2304, 6912], P(None, ('seq', 'stream')), may hold values from -0.09375 to 0.09375
- gate_bias: float32 [6912], P(('seq', 'stream')), may hold values from -3 to 8
- first_weight: float32 [2, 2304, 6912], P(None, ('seq', 'stream')), may hold values from -1 to 1
- second_weight: float32 [2, 2304, 6912], P(None, ('seq', 'stream')), may hold values from 0 to 1
- first_bias: float32 [6912], P(('seq', 'stream')), may hold values from -1 to 1
- second_bias: float32 [6912], P(('seq', 'stream')), may hold values from 0 to 1
- cotangent: bfloat16 [4, 4096, 2304], P('stream', 'seq'), may hold values from -6 to 6
- final_cotangent: float32 [4, 2304], P('stream'), may hold values from -6 to 6
Outputs:
- hidden: bfloat16 [4, 4096, 2304], P('stream', 'seq')
- final_state: float32 [4, 2304], P('stream', 'seq')
- input_gradient: bfloat16 [4, 4096, 2304], P('stream', 'seq')
- weight_gradient: float32 [2, 2304, 6912], P(None, ('seq', 'stream'))
- bias_gradient: float32 [6912], P(('seq', 'stream'))
- gradient_norm: float32 [], replicated
- new_weight: float32 [2, 2304, 6912], P(None, ('seq', 'stream'))
- new_first_weight: float32 [2, 2304, 6912], P(None, ('seq', 'stream'))
- new_second_weight: float32 [2, 2304, 6912], P(None, ('seq', 'stream'))
- new_bias: float32 [6912], P(('seq', 'stream'))
- new_first_bias: float32 [6912], P(('seq', 'stream'))
- new_second_bias: float32 [6912], P(('seq', 'stream'))
Inputs may be any that keep to these rules, and one draw needn't show every extreme that they name: `boundary`: 1 marks the first token of a document; position 0 of every stream holds 0; in every draw one stream holds no 1 at all.
All inputs are finite; a program needn't handle non-finite values.
Results may differ from a plain program's by a relative error of at most 0.007.
Values may be sent and summed in bfloat16 or wider, within the bound.
No kernel may reach another device: no remote copies, remote signals or barrier semaphores. Data moves between devices by JAX's collectives and lax.ppermute only.
A program may use at most 640 MiB of HBM per device.

v0:
```python
import jax
import jax.numpy as jnp
from jax import lax
from jax.sharding import PartitionSpec as P

STEP = 10


BETA_ONE = 0.9
BETA_TWO = 0.95
EPSILON = 1e-08
RATE_WEIGHT = 0.01
RATE_BIAS = 1.0
DECAY_RATE = 0.1
CLIP_NORM = 1.0
FORGET_SHIFT = 6.0


def from_behind(block, axis, distance):
    devices = range(lax.axis_size(axis))
    route = [(i - distance, i) for i in devices if i - distance in devices]
    return lax.ppermute(block, axis, route)


def carried_in(value, axis, combine, identity, reverse):
    count, here = (lax.axis_size(axis), lax.axis_index(axis))
    everything = jax.tree.map(lambda part: lax.all_gather(part, axis), value)
    start = jax.tree.map(
        lambda part, zero: jnp.broadcast_to(jnp.asarray(zero, part.dtype), part.shape),
        value,
        identity,
    )

    def turn(k, before):
        at = count - 1 - k if reverse else k
        reached = at > here if reverse else at < here
        new = combine(before, jax.tree.map(lambda part: part[at], everything))
        return jax.tree.map(lambda a, b: jnp.where(reached, a, b), new, before)

    return lax.fori_loop(0, count, turn, start)


def from_root(value, axis, source):
    kept = jnp.where(lax.axis_index(axis) == source, value, 0).astype(value.dtype)
    return lax.psum(kept, axis)


def compose(earlier, latter):
    return (earlier[0] * latter[0], latter[0] * earlier[1] + latter[1])


def contract(left_side, right_side, left_axis, right_axis):
    return lax.dot_general(
        left_side,
        right_side,
        (((left_axis,), (right_axis,)), ((), ())),
        preferred_element_type=jnp.float32,
    )


def adamw(master, gradient, moment_one, moment_two, rate):
    moment_one = BETA_ONE * moment_one + (1.0 - BETA_ONE) * gradient
    moment_two = BETA_TWO * moment_two + (1.0 - BETA_TWO) * gradient * gradient
    step_size = (
        moment_one
        / (1.0 - BETA_ONE**STEP)
        / (jnp.sqrt(moment_two / (1.0 - BETA_TWO**STEP)) + EPSILON)
    )
    return (master - rate * (step_size + DECAY_RATE * master), moment_one, moment_two)


def on_device(
    inputs,
    boundary,
    start_state,
    weight,
    gate_bias,
    first_weight,
    second_weight,
    first_bias,
    second_bias,
    cotangent,
    final_cotangent,
):
    streams_here = inputs.shape[0]
    block_length = inputs.shape[1]
    model_width = inputs.shape[2]
    seq_devices = lax.axis_size("seq")
    position = lax.axis_index("seq")
    own_columns = model_width // seq_devices
    keeping = (1 - boundary).astype(jnp.float32)[:, :, None]
    weight_low = weight.astype(jnp.bfloat16)
    bias_low = gate_bias.astype(jnp.bfloat16)
    full_weight, full_bias = (
        lax.all_gather(weight_low, ("seq", "stream"), axis=1, tiled=True),
        lax.all_gather(bias_low, ("seq", "stream"), axis=0, tiled=True),
    )
    edge_values = from_behind(inputs[:, -1:, :], "seq", 1)
    previous = jnp.concatenate([edge_values, inputs[:, :-1, :]], axis=1)
    previous = jnp.where(boundary[:, :, None] == 1, jnp.zeros_like(previous), previous)
    token_rows = inputs.reshape(-1, model_width)
    prior_rows = previous.reshape(-1, model_width)
    gates = contract(token_rows, full_weight[0], 1, 0) + contract(prior_rows, full_weight[1], 1, 0)
    gates = (gates + full_bias.astype(jnp.float32)).reshape(
        streams_here, block_length, 3 * model_width
    )
    candidate = jnp.tanh(gates[..., :model_width])
    forget = jax.nn.sigmoid(gates[..., model_width : 2 * model_width] + FORGET_SHIFT)
    output_gate = jax.nn.sigmoid(gates[..., 2 * model_width :])
    retain = forget * keeping
    fresh = (1.0 - forget) * candidate
    running, local_memory = lax.associative_scan(compose, (retain, fresh), axis=1)
    summary = (running[:, -1], local_memory[:, -1])
    identity = (jnp.ones_like(summary[0]), jnp.zeros_like(summary[1]))
    before = carried_in(summary, "seq", compose, identity, False)
    entering = before[0] * start_state + before[1]
    memory = local_memory + running * entering[:, None]
    whole_final = from_root(memory[:, -1], "seq", seq_devices - 1)
    final_state = lax.dynamic_slice_in_dim(whole_final, position * own_columns, own_columns, 1)
    hidden = (output_gate * memory).astype(jnp.bfloat16)
    cot_values = cotangent.astype(jnp.float32)
    source = cot_values * output_gate
    factor = jnp.concatenate([retain[:, 1:], jnp.ones_like(retain[:, :1])], axis=1)
    trailing, local_adjoint = lax.associative_scan(compose, (factor, source), reverse=True, axis=1)
    back_summary = (retain[:, 0] * trailing[:, 0], retain[:, 0] * local_adjoint[:, 0])
    identity_back = (jnp.ones_like(back_summary[0]), jnp.zeros_like(back_summary[1]))
    after = carried_in(back_summary, "seq", compose, identity_back, True)
    arriving = after[0] * final_cotangent + after[1]
    adjoint = local_adjoint + trailing * arriving[:, None]
    memory_prior = jnp.concatenate([entering[:, None], memory[:, :-1]], axis=1)
    grad_candidate = adjoint * (1.0 - forget) * (1.0 - candidate * candidate)
    grad_forget = adjoint * (keeping * memory_prior - candidate) * forget * (1.0 - forget)
    grad_output = cot_values * memory * output_gate * (1.0 - output_gate)
    gate_grads = jnp.concatenate([grad_candidate, grad_forget, grad_output], axis=-1).astype(
        jnp.bfloat16
    )
    gate_grads = gate_grads.reshape(-1, 3 * model_width)
    back_weight = lax.all_gather(weight_low, ("seq", "stream"), axis=1, tiled=True)
    direct = contract(gate_grads, back_weight[0], 1, 1).reshape(
        streams_here, block_length, model_width
    )
    shifted = (
        contract(gate_grads, back_weight[1], 1, 1).reshape(streams_here, block_length, model_width)
        * keeping
    )
    from_next = from_behind(shifted[:, :1, :], "seq", -1)
    input_gradient = (direct + jnp.concatenate([shifted[:, 1:], from_next], axis=1)).astype(
        jnp.bfloat16
    )
    local_weight = jnp.stack(
        [contract(token_rows, gate_grads, 0, 0), contract(prior_rows, gate_grads, 0, 0)]
    )
    local_bias = jnp.sum(gate_grads.astype(jnp.float32), axis=0)
    weight_sum, bias_sum = (
        lax.psum_scatter(local_weight, ("seq", "stream"), scatter_dimension=1, tiled=True),
        lax.psum_scatter(local_bias, ("seq", "stream"), scatter_dimension=0, tiled=True),
    )
    squares = jnp.sum(weight_sum * weight_sum) + jnp.sum(bias_sum * bias_sum)
    gradient_norm = jnp.sqrt(lax.psum(squares, ("seq", "stream")))
    clip_factor = jnp.minimum(1.0, CLIP_NORM / (gradient_norm + 1e-06))
    weight_gradient = clip_factor * weight_sum
    bias_gradient = clip_factor * bias_sum
    new_weight, new_first_weight, new_second_weight = adamw(
        weight, weight_gradient, first_weight, second_weight, RATE_WEIGHT
    )
    new_bias, new_first_bias, new_second_bias = adamw(
        gate_bias, bias_gradient, first_bias, second_bias, RATE_BIAS
    )
    return (
        hidden,
        final_state,
        input_gradient,
        weight_gradient,
        bias_gradient,
        gradient_norm,
        new_weight,
        new_first_weight,
        new_second_weight,
        new_bias,
        new_first_bias,
        new_second_bias,
    )


def solution(mesh):
    placed = (
        P("stream", "seq", None),
        P("stream", "seq"),
        P("stream", None),
        P(None, ("seq", "stream"), None),
        P(("seq", "stream")),
        P(None, ("seq", "stream"), None),
        P(None, ("seq", "stream"), None),
        P(("seq", "stream")),
        P(("seq", "stream")),
        P("stream", "seq", None),
        P("stream", None),
    )
    return jax.shard_map(
        on_device,
        mesh=mesh,
        in_specs=placed,
        out_specs=(
            P("stream", "seq", None),
            P("stream", "seq"),
            P("stream", "seq", None),
            P(None, ("seq", "stream"), None),
            P(("seq", "stream")),
            P(),
            P(None, ("seq", "stream"), None),
            P(None, ("seq", "stream"), None),
            P(None, ("seq", "stream"), None),
            P(("seq", "stream")),
            P(("seq", "stream")),
            P(("seq", "stream")),
        ),
        check_vma=False,
    )
```

profile of v0, /device:TPU:0, one launch (start us, length us, event | category | flops | bytes accessed | tf_op | source)
XLA Modules:
  0.0 3473.2 jit_solution(9305383252589305236)
XLA Ops:
  16.3 43.1 %all-reduce.74 = bf16[6912]{0:T(1024)(128)(2,1)S(1)} all-reduce(bf16[6912]{0:T(1024)(128)(2,1)S(1)} %dynamic-update-slice), channel_id=1, replica_groups=mesh['seq'=8,'stream'=4] {'seq','stream'}, use_global_device_ids=true, to_apply=%add.74 | all-reduce | flops 6912 | bytes 27648
  61.9 293.2 %all-gather.2.cloned.1.call-done = bf16[2,2304,6912]{2,1,0:T(8,128)(2,1)} async-done(((bf16[2,72,6912]{2,1,0:T(8,128)(2,1)}), bf16[2,2304,6912]{2,1,0:T(8,128)(2,1)}) %all-gather.2.cloned.1.call-update) | async-done | bytes 63701008 | tf_op jit(solution)/shard_map/all_gather | solution.py:95
  355.1 23.1 fusion.1
  378.2 27.5 add_bitcast_fusion
  580.9 17.1 pad.257
  602.0 17.2 pad.239
  627.5 17.3 pad.256
  645.7 30.6 all_gather.23
  677.9 17.3 pad.238
  696.1 30.6 all_gather.24
  728.0 12.0 fusion.25
  805.8 18.8 slice.693
  836.2 18.8 slice.698
  961.3 12.2 slice.759
  973.6 19.2 slice.689
  1057.8 17.0 pad.274
  1084.4 17.3 pad.293
  1123.0 36.7 %rev.8 = f32[1,512,2304]{2,1,0:T(8,128)} reverse(f32[1,512,2304]{2,1,0:T(8,128)} %add.584), dimensions={1} | reverse | bytes 9437184 | tf_op jit(solution)/shard_map/rev | solution.py:124
  1159.7 36.7 %rev.9 = f32[1,512,2304]{2,1,0:T(8,128)} reverse(f32[1,512,2304]{2,1,0:T(8,128)} %add.593), dimensions={1} | reverse | bytes 9437184 | tf_op jit(solution)/shard_map/rev | solution.py:124
  1196.5 30.5 all_gather.26
  1227.0 30.5 all_gather.25
  1258.1 14.4 fusion.23
  1272.5 29.7 convolution_bitcast_fusion.1
  1302.2 29.5 convolution_bitcast_fusion
  1331.7 82.5 %pad_maximum_fusion = f32[2,2304,6912]{1,2,0:T(8,128)} fusion(f32[1,2304,6912]{1,2,0:T(8,128)} %convolution_bitcast_fusion, f32[1,2304,6912]{1,2,0:T(8,128)} %convolution_bitcast_fusion.1), kind=kLoop, calls=%fused_computation.12 | loop fusion | flops 31850496 | bytes 254803968 | tf_op jit(solution)/shard_map/stack | solution.py:150
  1414.1 181.3 %copy.43 = f32[2,2304,6912]{2,0,1:T(2,128)} copy(f32[2,2304,6912]{1,2,0:T(8,128)} %pad_maximum_fusion) | data formatting | bytes 254803968 | tf_op jit(solution)/shard_map/stack | solution.py:150
  1597.1 27.1 fusion.5
  1629.9 40.3 %all-reduce.76 = f32[6912]{0:T(1024)S(1)} all-reduce(f32[6912]{0:T(1024)S(1)} %convert_reduce_fusion), channel_id=3, replica_groups=mesh['seq'=8,'stream'=4] {'seq','stream'}, use_global_device_ids=true, to_apply=%region_8.9.clone | all-reduce | flops 6912 | bytes 55296
  1671.8 23.7 psum.14
  1701.4 1675.0 %all-reduce.79.cloned.1.call-done = f32[2,2304,6912]{2,0,1:T(2,128)} async-done(((f32[2,2304,6912]{2,0,1:T(2,128)}), f32[2,2304,6912]{2,0,1:T(2,128)}) %all-reduce.79.cloned.1.call-update) | async-done | bytes 127402000
  3386.5 27.4 fusion.24
  3413.8 39.0 %psum.15 = f32[]{:T(128)} all-reduce(f32[]{:T(128)S(6)} %add.597), channel_id=1, replica_groups=mesh['seq'=8,'stream'=4] {'seq','stream'}, use_global_device_ids=true, to_apply=%region_10.11 | all-reduce | flops 1 | bytes 8 | tf_op jit(solution)/shard_map/psum | solution.py:159
  (514 shorter events, 518.3 us)
Async XLA Ops:
  7.2 52.2 %copy-start.79 = (s32[1,512]{1,0:T(1,128)S(1)}, s32[1,512]{1,0:T(1,128)}, u32[]{:S(2)}) copy-start(s32[1,512]{1,0:T(1,128)} %param.16) | copy-start | bytes 6148
  7.2 347.9 %all-gather.2.cloned.1.call-start = ((), (), s32[]{:S(2)}) async-start(), calls=%async_computation | async-start | bytes 65691648 | tf_op jit(solution)/shard_map/all_gather | solution.py:95
  11.0 3365.4 %all-reduce.79.cloned.1.call-start = ((), (), s32[]{:S(2)}) async-start(), calls=%async_computation.1 | async-start | bytes 254803968
  11.1 367.1 %collective-permute-start = (bf16[1,1,2304]{2,1,0:T(2,128)(2,1)S(1)}, bf16[1,1,2304]{2,1,0:T(2,128)(2,1)S(1)}, u32[]{:S(2)}, u32[]{:S(2)}) collective-permute-start(bf16[1,1,2304]{2,1,0:T(2,128)(2,1)S(1)} %slice.593), channel_id=1, source_target_pairs={{0,4},{4,8},{8,12},{12,16},{16,20},{20,24},{24,28},{1,5},{5,9},{9,... | collective-permute-start | bytes 13832 | tf_op jit(solution)/shard_map/ppermute | solution.py:22
  59.4 318.8 %copy-start.84 = (pred[512]{0:T(512)(128)(4,1)}, pred[512]{0:T(512)(128)(4,1)S(1)}, u32[]{:S(2)}) copy-start(pred[512]{0:T(512)(128)(4,1)S(1)} %compare_reduce_fusion) | copy-start | bytes 1540
  59.4 346.3 %copy-start.74 = (f32[1,512]{1,0:T(1,128)}, f32[1,512]{1,0:T(1,128)S(1)}, u32[]{:S(2)}) copy-start(f32[1,512]{1,0:T(1,128)S(1)} %subtract_convert_fusion) | copy-start | bytes 6148
  378.2 27.5 copy-start.86
  627.5 48.8 %copy-start.12 = (f32[1,255,2304]{2,1,0:T(8,128)S(1)}, f32[1,255,2304]{2,1,0:T(8,128)}, u32[]{:S(2)}) copy-start(f32[1,255,2304]{2,1,0:T(8,128)} %get-tuple-element.401) | copy-start | bytes 7050244
  627.5 48.8 %copy-start.71 = (f32[1,1,2304]{2,1,0:T(1,128)S(1)}, f32[1,1,2304]{2,1,0:T(1,128)}, u32[]{:S(2)}) copy-start(f32[1,1,2304]{2,1,0:T(1,128)} %slice.786) | copy-start | bytes 27652
  677.9 48.8 %copy-start.43 = (f32[1,2304]{1,0:T(1,128)S(1)}, f32[1,2304]{1,0:T(1,128)}, u32[]{:S(2)}) copy-start(f32[1,2304]{1,0:T(1,128)} %custom-call) | copy-start | bytes 27652
  677.9 49.5 %copy-start.78 = (f32[1,2304]{1,0:T(1,128)S(1)}, f32[1,2304]{1,0:T(1,128)}, u32[]{:S(2)}) copy-start(f32[1,2304]{1,0:T(1,128)} %param.17) | copy-start | bytes 27652
  677.9 50.1 %copy-start.31 = (bf16[1,512,2304]{2,1,0:T(8,128)(2,1)S(1)}, bf16[1,512,2304]{2,1,0:T(8,128)(2,1)}, u32[]{:S(2)}) copy-start(bf16[1,512,2304]{2,1,0:T(8,128)(2,1)} %param.24) | copy-start | bytes 7077892
  915.2 46.1 %copy-start.16 = (f32[1,255,2304]{2,1,0:T(8,128)S(1)}, f32[1,255,2304]{2,1,0:T(8,128)}, u32[]{:S(2)}) copy-start(f32[1,255,2304]{2,1,0:T(8,128)} %slice.758) | copy-start | bytes 7050244
  973.5 19.5 copy-start.59
  973.5 19.6 copy-start.46
  973.5 19.6 copy-start.47
  973.5 19.6 copy-start.64
  973.6 19.7 copy-start.63
  973.6 19.8 copy-start.44
  973.6 19.8 copy-start.45
  1159.7 97.8 %copy-start.41 = (f32[1,2304]{1,0:T(1,128)S(1)}, f32[1,2304]{1,0:T(1,128)}, u32[]{:S(2)}) copy-start(f32[1,2304]{1,0:T(1,128)} %custom-call.3) | copy-start | bytes 27652
  1159.7 97.8 %copy-start.42 = (f32[1,2304]{1,0:T(1,128)S(1)}, f32[1,2304]{1,0:T(1,128)}, u32[]{:S(2)}) copy-start(f32[1,2304]{1,0:T(1,128)} %custom-call.2) | copy-start | bytes 27652
  1159.7 98.3 %copy-start.77 = (f32[1,2304]{1,0:T(1,128)S(1)}, f32[1,2304]{1,0:T(1,128)}, u32[]{:S(2)}) copy-start(f32[1,2304]{1,0:T(1,128)} %param.25) | copy-start | bytes 27652
  1159.7 98.4 %copy-start.52 = (f32[1,1,2304]{2,1,0:T(1,128)S(1)}, f32[1,1,2304]{2,1,0:T(1,128)}, u32[]{:S(2)}) copy-start(f32[1,1,2304]{2,1,0:T(1,128)} %get-tuple-element.461) | copy-start | bytes 27652
  1159.7 98.4 %copy-start.75 = (f32[1,512]{1,0:T(1,128)S(1)}, f32[1,512]{1,0:T(1,128)}, u32[]{:S(2)}) copy-start(f32[1,512]{1,0:T(1,128)} %copy-done.74) | copy-start | bytes 6148
  1272.5 29.7 copy-start.13
  1272.5 29.7 copy-start.85
  1272.5 29.7 copy-start.87
  1625.1 1761.4 %collective-permute-start.1 = (f32[1,1,2304]{2,1,0:T(1,128)S(1)}, f32[1,1,2304]{2,1,0:T(1,128)S(1)}, u32[]{:S(2)}, u32[]{:S(2)}) collective-permute-start(f32[1,1,2304]{2,1,0:T(1,128)S(1)} %slice.905), channel_id=1, source_target_pairs={{4,0},{8,4},{12,8},{16,12},{20,16},{24,20},{28,24},{5,1},{9,5},{13... | collective-permute-start | bytes 27656 | tf_op jit(solution)/shard_map/ppermute | solution.py:22
  3386.4 67.1 %copy-start.81 = (f32[216]{0:T(256)S(1)}, f32[216]{0:T(256)}, u32[]{:S(2)}) copy-start(f32[216]{0:T(256)} %param.19) | copy-start | bytes 2596
  3386.4 67.1 %copy-start.82 = (f32[216]{0:T(256)S(1)}, f32[216]{0:T(256)}, u32[]{:S(2)}) copy-start(f32[216]{0:T(256)} %param.22) | copy-start | bytes 2596
  3386.4 67.1 %copy-start.83 = (f32[216]{0:T(256)S(1)}, f32[216]{0:T(256)}, u32[]{:S(2)}) copy-start(f32[216]{0:T(256)} %param.23) | copy-start | bytes 2596
  (62 other events, 287.1 us)
Sparse Core Ops, SparseCore 0:
  11.5 343.5 all-gather.1
  1595.6 1780.7 all-reduce.78
where the time goes:
time: 3500 us; the launch traced here: 3470 us
  waiting for transfers between devices  1970 us (56%)
  local copies, waits for them, and re-layouts  810 us (23%)
  blocking collectives  268 us (8%)
  other arithmetic  237 us (7%)
  matrix products  164 us (5%)
    unnamed x3, waiting for transfers between devices  1680 us
    all_gather x1, waiting for transfers between devices, on_device(): lax.all_gather(weight_low, ('seq', 'stream'), axis=1, tiled=True)  293 us
    slice x65, local copies, waits for them, and re-layouts, on_device(): lax.associative_scan(compose, (factor, source), reverse=True, axis=1)  225 us
    another operation x1, local copies, waits for them, and re-layouts, on_device(): jnp.stack([contract(token_rows, gate_grads, 0, 0), contract(prior_rows, g...  181 us
    dot_general x6, matrix products, contract(): lax.dot_general(left_side, right_side, (((left_axis,), (right_axis,)), ((...  164 us
    all_gather x4, blocking collectives, carried_in(): everything = jax.tree.map(lambda part: lax.all_gather(part, axis), value)  122 us
    pad x32, local copies, waits for them, and re-layouts, on_device(): lax.associative_scan(compose, (retain, fresh), axis=1)  106 us
    slice x60, local copies, waits for them, and re-layouts, on_device(): lax.associative_scan(compose, (retain, fresh), axis=1)  100 us
  transfers between devices with their start and end apart: 4, of which 2 were waited for; matrix products, arithmetic and copies ran while one was open for 2% of the time, Pallas kernels for 0%

commit v1 on v0

v1 whole, which is shorter than its diff:
```python
import functools
import jax
import jax.numpy as jnp
from jax import lax
from jax.experimental import pallas as pl
from jax.experimental.pallas import tpu as pltpu
from jax.sharding import PartitionSpec as P

STEP = 10
BETA_ONE = 0.9
BETA_TWO = 0.95
EPSILON = 1e-08
RATE_WEIGHT = 0.01
RATE_BIAS = 1.0
DECAY_RATE = 0.1
CLIP_NORM = 1.0
FORGET_SHIFT = 6.0

AXES = ("seq", "stream")
LANES = 128
MEMBERS = 8
HEAD = 16
EDGE = HEAD - 1
BF16 = jnp.bfloat16
F32 = jnp.float32
VMEM_LIMIT = 60 * 1024 * 1024


def params():
    return pltpu.CompilerParams(vmem_limit_bytes=VMEM_LIMIT)


def in_vmem(count):
    return [pl.BlockSpec(memory_space=pltpu.VMEM)] * count


def dot_f32(a, b, dims):
    return lax.dot_general(a, b, (dims, ((), ())), preferred_element_type=F32)


class Place:
    def __init__(self):
        self.n_seq = lax.axis_size("seq")
        self.n_stream = lax.axis_size("stream")
        self.depth = self.n_seq // 2
        self.wide = self.n_stream // 4
        self.count = self.n_seq * self.n_stream
        self.seq = lax.axis_index("seq")
        self.stream = lax.axis_index("stream")
        self.linear = self.seq * self.n_stream + self.stream
        self.member = (self.seq % 2) * 4 + self.stream % 4
        self.high = self.seq // 2
        self.group_bits = [1, 2, self.n_stream]
        self.deep_bits = [self.n_stream * (2 << b) for b in range(self.depth.bit_length() - 1)]
        self.wide_bits = [4 << b for b in range(self.wide.bit_length() - 1)]

    def flip(self, block, mask):
        return lax.ppermute(block, AXES, [(n, n ^ mask) for n in range(self.count)])

    def member_mask(self, p):
        return (p & 3) | ((p >> 2) * self.n_stream)

    def gather_flips(self, block, bits):
        for bit in bits:
            block = jnp.concatenate([block, self.flip(block, bit)], axis=0)
        return block

    def sum_flips(self, value, bits):
        for bit in bits:
            value = value + self.flip(value, bit)
        return value

    def exchange(self, even, odd):
        sibling = self.flip(odd, 1)
        pairs = [jnp.stack([even[i], sibling[i]]) for i in range(4)]
        return [pairs[0]] + [self.flip(pairs[i], self.member_mask(2 * i)) for i in (1, 2, 3)]


def sizes(width):
    whole = width // (MEMBERS * LANES)
    rest = width // MEMBERS - whole * LANES
    assert whole == 2 and 0 < 3 * rest <= LANES and LANES % rest == 0
    return whole, rest


def lane_index(shape):
    return lax.broadcasted_iota(jnp.int32, shape, len(shape) - 1)


def pack_weight_kernel(width, member_ref, weight_ref, even_ref, odd_ref):
    rest = sizes(width)[1]
    taps, rows, _ = weight_ref.shape
    per_tile = LANES // rest
    lane = lane_index((rows, LANES))
    for p in range(MEMBERS):
        out = (even_ref, odd_ref)[p % 2]
        to = member_ref[0] ^ p
        column = 0
        for tile in range(2):
            for tap in range(taps):
                for gate in range(3):
                    start = pl.multiple_of(gate * width + (tile * MEMBERS + to) * LANES, LANES)
                    out[p // 2, :, pl.ds(column, LANES)] = weight_ref[tap, :, pl.ds(start, LANES)].astype(BF16)
                    column += LANES
                if tile == 1:
                    mixed = jnp.zeros((rows, LANES), F32)
                    for gate in range(3):
                        start = pl.multiple_of(gate * width + (2 * MEMBERS + to // per_tile) * LANES, LANES)
                        part = weight_ref[tap, :, pl.ds(start, LANES)]
                        part = pltpu.roll(part, lax.rem((gate - to % per_tile) * rest + LANES, LANES), 1)
                        inside = (lane >= gate * rest) & (lane < (gate + 1) * rest)
                        mixed = jnp.where(inside, part, mixed)
                    out[p // 2, :, pl.ds(column, LANES)] = mixed.astype(BF16)
                    column += LANES


def pack_weight(weight, member):
    taps, rows, columns = weight.shape
    shape = jax.ShapeDtypeStruct((4, rows, 14 * LANES), BF16)
    return pl.pallas_call(
        functools.partial(pack_weight_kernel, columns // 3),
        out_shape=(shape, shape),
        in_specs=[pl.BlockSpec(memory_space=pltpu.SMEM)] + in_vmem(1),
        out_specs=tuple(in_vmem(2)),
        compiler_params=params(),
        name="pack_weight",
    )(member, weight)


def place_weight_kernel(split, member_ref, own_ref, y_ref, x_ref, both_ref, first_ref, second_ref):
    for p in range(MEMBERS):
        block = (own_ref, y_ref, x_ref, both_ref)[p // 2][p % 2]
        first_ref[member_ref[0] ^ p] = block[:, :split]
        second_ref[member_ref[0] ^ p] = block[:, split:]


def place_weight(pairs, member, split):
    _, rows, columns = pairs[0].shape
    return pl.pallas_call(
        functools.partial(place_weight_kernel, split),
        out_shape=(
            jax.ShapeDtypeStruct((MEMBERS, rows, split), BF16),
            jax.ShapeDtypeStruct((MEMBERS, rows, columns - split), BF16),
        ),
        in_specs=[pl.BlockSpec(memory_space=pltpu.SMEM)] + in_vmem(4),
        out_specs=tuple(in_vmem(2)),
        compiler_params=params(),
        name="place_weight",
    )(member, *pairs)


def pick_gradient_kernel(member_ref, first_ref, second_ref, even_ref, odd_ref):
    split = first_ref.shape[-1]
    for p in range(MEMBERS):
        out = (even_ref, odd_ref)[p % 2]
        out[p // 2, :, pl.ds(0, split)] = first_ref[member_ref[0] ^ p]
        out[p // 2, :, pl.ds(split, second_ref.shape[-1])] = second_ref[member_ref[0] ^ p]


def pick_gradient(first, second, member):
    rows = first.shape[1]
    shape = jax.ShapeDtypeStruct((4, rows, first.shape[2] + second.shape[2]), BF16)
    return pl.pallas_call(
        pick_gradient_kernel,
        out_shape=(shape, shape),
        in_specs=[pl.BlockSpec(memory_space=pltpu.SMEM)] + in_vmem(2),
        out_specs=tuple(in_vmem(2)),
        compiler_params=params(),
        name="pick_gradient",
    )(member, first, second)


def place_gradient_kernel(width, member_ref, own_ref, y_ref, x_ref, both_ref, out_ref):
    rest = sizes(width)[1]
    taps, rows, _ = out_ref.shape
    per_tile = LANES // rest
    lane = lane_index((rows, LANES))
    for p in range(MEMBERS):
        block_ref = (own_ref, y_ref, x_ref, both_ref)[p // 2]
        source = member_ref[0] ^ p
        column = 0
        for tile in range(2):
            for tap in range(taps):
                for gate in range(3):
                    start = pl.multiple_of(gate * width + (tile * MEMBERS + source) * LANES, LANES)
                    out_ref[tap, :, pl.ds(start, LANES)] = block_ref[p % 2, :, pl.ds(column, LANES)].astype(F32)
                    column += LANES
                if tile == 1:
                    mixed = block_ref[p % 2, :, pl.ds(column, LANES)].astype(F32)
                    column += LANES
                    for gate in range(3):
                        start = pl.multiple_of(gate * width + (2 * MEMBERS + source // per_tile) * LANES, LANES)
                        first = (source % per_tile) * rest
                        part = pltpu.roll(mixed, lax.rem(first - gate * rest + LANES, LANES), 1)
                        inside = (lane >= first) & (lane < first + rest)
                        old = out_ref[tap, :, pl.ds(start, LANES)]
                        out_ref[tap, :, pl.ds(start, LANES)] = jnp.where(inside, part, old)


def place_gradient(pairs, member, shape):
    return pl.pallas_call(
        functools.partial(place_gradient_kernel, shape[2] // 3),
        out_shape=jax.ShapeDtypeStruct(shape, F32),
        in_specs=[pl.BlockSpec(memory_space=pltpu.SMEM)] + in_vmem(4),
        out_specs=pl.BlockSpec(memory_space=pltpu.VMEM),
        compiler_params=params(),
        name="place_gradient",
    )(member, *pairs)


def pack_channels_kernel(width, member_ref, values_ref, even_ref, odd_ref):
    rest = sizes(width)[1]
    per_tile = LANES // rest
    for p in range(MEMBERS):
        out = (even_ref, odd_ref)[p % 2]
        to = member_ref[0] ^ p
        for tile in range(2):
            start = pl.multiple_of((tile * MEMBERS + to) * LANES, LANES)
            out[p // 2, :, pl.ds(tile * LANES, LANES)] = values_ref[:, pl.ds(start, LANES)]
        start = pl.multiple_of((2 * MEMBERS + to // per_tile) * LANES, LANES)
        part = values_ref[:, pl.ds(start, LANES)].astype(F32)
        part = pltpu.roll(part, lax.rem(LANES - (to % per_tile) * rest, LANES), 1)
        out[p // 2, :, pl.ds(2 * LANES, LANES)] = part.astype(BF16)


def pack_channels(values, member):
    rows, width = values.shape
    shape = jax.ShapeDtypeStruct((4, rows, 3 * LANES), BF16)
    return pl.pallas_call(
        functools.partial(pack_channels_kernel, width),
        out_shape=(shape, shape),
        in_specs=[pl.BlockSpec(memory_space=pltpu.SMEM)] + in_vmem(1),
        out_specs=tuple(in_vmem(2)),
        compiler_params=params(),
        name="pack_channels",
    )(member, values)


def place_channels_kernel(width, member_ref, own_ref, y_ref, x_ref, both_ref, out_ref):
    rest = sizes(width)[1]
    rows, _ = out_ref.shape
    per_tile = LANES // rest
    lane = lane_index((rows, LANES))
    for p in range(MEMBERS):
        block_ref = (own_ref, y_ref, x_ref, both_ref)[p // 2]
        source = member_ref[0] ^ p
        for tile in range(2):
            start = pl.multiple_of((tile * MEMBERS + source) * LANES, LANES)
            out_ref[:, pl.ds(start, LANES)] = block_ref[p % 2, :, pl.ds(tile * LANES, LANES)]
        start = pl.multiple_of((2 * MEMBERS + source // per_tile) * LANES, LANES)
        first = (source % per_tile) * rest
        part = pltpu.roll(block_ref[p % 2, :, pl.ds(2 * LANES, LANES)].astype(F32), first, 1)
        inside = (lane >= first) & (lane < first + rest)
        old = out_ref[:, pl.ds(start, LANES)].astype(F32)
        out_ref[:, pl.ds(start, LANES)] = jnp.where(inside, part, old).astype(BF16)


def place_channels(pairs, member, width):
    return pl.pallas_call(
        functools.partial(place_channels_kernel, width),
        out_shape=jax.ShapeDtypeStruct((pairs[0].shape[1], width), BF16),
        in_specs=[pl.BlockSpec(memory_space=pltpu.SMEM)] + in_vmem(4),
        out_specs=pl.BlockSpec(memory_space=pltpu.VMEM),
        compiler_params=params(),
        name="place_channels",
    )(member, *pairs)


def row_block(rows):
    for block in (176, 48, 16):
        if rows % block == 0:
            return block
    return rows


def tile_columns(tiles, taps_first):
    return 3 * LANES if tiles == 1 else 4 * LANES


def forward_kernel(tiles, rest, x_ref, w_ref, bias_ref, keep_ref, cot_ref, act_ref, sum_ref, both, cot_f32, carry, before):
    step = pl.program_id(0)
    block = x_ref.shape[1]
    rows = MEMBERS * block
    half = w_ref.shape[1] // 2
    lane = lane_index((MEMBERS, LANES))

    x = x_ref[...].reshape(rows, x_ref.shape[2])

    def multiply(i, _):
        at = pl.ds(pl.multiple_of(i * 256, 256), 256)
        result = dot_f32(x, w_ref[:, at], ((1,), (0,)))
        both[2 * i] = result[:, :LANES]
        both[2 * i + 1] = result[:, LANES:]
        return 0

    lax.fori_loop(0, w_ref.shape[1] // 256, multiply, 0)
    for tile in range(tiles):
        cot_f32[tile] = cot_ref[:, :, pl.ds(tile * LANES, LANES)].reshape(rows, LANES).astype(F32)
    count = half // LANES

    @pl.when(step == 0)
    def _():
        for tile in range(tiles):
            carry[3 * tile] = jnp.ones((MEMBERS, LANES), F32)
            carry[3 * tile + 1] = jnp.zeros((MEMBERS, LANES), F32)
            carry[3 * tile + 2] = jnp.zeros((MEMBERS, LANES), F32)
        for i in range(count):
            before[i] = both[count + i, pl.ds(EDGE, MEMBERS, stride=block), :]

    act = act_ref

    def token(k, state):
        sums, earlier = state
        rows_at = pl.ds(k, MEMBERS, stride=block)
        keep = keep_ref[k]
        later = tuple(both[count + i, rows_at, :] for i in range(count))
        gates = [
            both[i, rows_at, :] + keep * earlier[i] + bias_ref[:, pl.ds(i * LANES, LANES)]
            for i in range(count)
        ]
        new = []
        outs = []
        for tile in range(tiles):
            at = lambda g: gates[3 * tile + g]
            if tile == 0:
                z = jnp.tanh(at(0))
                u = 1.0 / (1.0 + jnp.exp(at(1) + FORGET_SHIFT))
                o = 1.0 / (1.0 + jnp.exp(-at(2)))
                outs += [z, u, o]
            else:
                mixed = at(0)
                z = jnp.tanh(mixed)
                s = 1.0 / (1.0 + jnp.exp(jnp.where(lane < 2 * rest, mixed + FORGET_SHIFT, -mixed)))
                outs += [jnp.where(lane < rest, z, s)]
                u = pltpu.roll(s, LANES - rest, 1)
                o = pltpu.roll(s, LANES - 2 * rest, 1)
            a = keep * (1.0 - u)
            total, local, back = sums[3 * tile : 3 * tile + 3]
            cot = cot_f32[tile, rows_at, :]
            total = total * a
            new += [total, a * local + u * z, back + total * (cot * o)]
        for i, value in enumerate(outs):
            act[k, :, pl.ds(i * LANES, LANES)] = value
        return tuple(new), later

    start = (tuple(carry[i] for i in range(3 * tiles)), tuple(before[i] for i in range(count)))
    low = jnp.where(step == 0, HEAD, 0)
    sums, earlier = lax.fori_loop(low, block, token, start)
    for i in range(3 * tiles):
        carry[i] = sums[i]
        sum_ref[i] = sums[i]
    for i in range(count):
        before[i] = earlier[i]


def forward(x, w, bias, keep, cot, tiles, rest):
    members, length, width = x.shape
    block = row_block(length)
    half = w.shape[1] // 2
    lanes = cot.shape[2]
    return pl.pallas_call(
        functools.partial(forward_kernel, tiles, rest),
        grid=(length // block,),
        out_shape=(
            jax.ShapeDtypeStruct((length, members, half), F32),
            jax.ShapeDtypeStruct((3 * tiles, members, LANES), F32),
        ),
        in_specs=[
            pl.BlockSpec((members, block, width), lambda i: (0, i, 0)),
            pl.BlockSpec(memory_space=pltpu.VMEM),
            pl.BlockSpec(memory_space=pltpu.VMEM),
            pl.BlockSpec((block, members, LANES), lambda i: (i, 0, 0)),
            pl.BlockSpec((members, block, lanes), lambda i: (0, i, 0)),
        ],
        out_specs=(
            pl.BlockSpec((block, members, half), lambda i: (i, 0, 0)),
            pl.BlockSpec((3 * tiles, members, LANES), lambda i: (0, 0, 0)),
        ),
        scratch_shapes=[
            pltpu.VMEM((2 * half // LANES, members * block, LANES), F32),
            pltpu.VMEM((tiles, members * block, LANES), F32),
            pltpu.VMEM((3 * tiles, members, LANES), F32),
            pltpu.VMEM((half // LANES, members, LANES), F32),
        ],
        compiler_params=params(),
        cost_estimate=pl.CostEstimate(
            flops=4 * members * length * width * half,
            bytes_accessed=2 * x.size + 2 * w.size + 4 * members * length * half,
            transcendentals=members * length * half,
        ),
        name="forward",
    )(x, w, bias, keep, cot)


def backward_kernel(
    tiles, rest, blocks, act_ref, keep_ref, cot_ref, enter_ref, arrive_ref, final_ref,
    hidden_ref, grads_ref, bias_ref, memory, cot_f32, wide, hold, carry, after,
):
    step = pl.program_id(0)
    block = act_ref.shape[0]
    half = act_ref.shape[2]
    rows = MEMBERS * block
    lane = lane_index((MEMBERS, LANES))
    which = jnp.where(step < blocks, step, 2 * blocks - 1 - step)
    base = which * block
    for tile in range(tiles):
        cot_f32[tile] = cot_ref[:, :, pl.ds(tile * LANES, LANES)].reshape(rows, LANES).astype(F32)
    count = half // LANES
    low = jnp.where(which == 0, HEAD, 0)

    def values(k, tile):
        at = lambda i: act_ref[k, :, pl.ds(i * LANES, LANES)]
        if tile == 0:
            return at(0), at(1), at(2)
        mixed = at(3)
        return mixed, pltpu.roll(mixed, LANES - rest, 1), pltpu.roll(mixed, LANES - 2 * rest, 1)

    @pl.when(step == 0)
    def _():
        for tile in range(tiles):
            memory[EDGE, tile] = enter_ref[tile]
            carry[tile] = enter_ref[tile]

    @pl.when(step < blocks)
    def _():
        def token(k, state):
            keep = keep_ref[k]
            new = []
            for tile in range(tiles):
                z, u, o = values(k, tile)
                m = keep * (1.0 - u) * state[tile] + u * z
                memory[base + k, tile] = m
                hold[tile, pl.ds(k, MEMBERS, stride=block), :] = o * m
                new.append(m)
            return tuple(new)

        state = lax.fori_loop(low, block, token, tuple(carry[t] for t in range(tiles)))
        for tile in range(tiles):
            carry[tile] = state[tile]

        @pl.when(step == 0)
        def _():
            for tile in range(tiles):
                rest_of = final_ref[tile]
                for row in range(3):
                    part = rest_of.astype(BF16).astype(F32)
                    hold[tile, pl.ds(row, MEMBERS, stride=block), :] = part
                    rest_of = rest_of - part
                for row in range(3, HEAD):
                    hold[tile, pl.ds(row, MEMBERS, stride=block), :] = jnp.zeros_like(part)

        for tile in range(tiles):
            hidden_ref[:, :, pl.ds(tile * LANES, LANES)] = hold[tile].astype(BF16).reshape(MEMBERS, block, LANES)

    @pl.when(step == blocks)
    def _():
        for tile in range(tiles):
            carry[tile] = arrive_ref[tile]
        after[...] = jnp.zeros_like(after)
        bias_ref[...] = jnp.zeros_like(bias_ref)

    @pl.when(step >= blocks)
    def _():
        def token(i, state):
            k = block - 1 - i
            arriving, shifted, totals = state
            rows_at = pl.ds(k, MEMBERS, stride=block)
            keep = keep_ref[k]
            new, parts = [], []
            for tile in range(tiles):
                z, u, o = values(k, tile)
                f = 1.0 - u
                cot = cot_f32[tile, rows_at, :]
                held = keep * memory[base + k - 1, tile]
                m = memory[base + k, tile]
                grad = cot * o
                adjoint = grad + arriving[tile]
                new.append(keep * f * adjoint)
                scaled = adjoint * u
                one = [scaled * (1.0 - z * z), scaled * (held - z) * f, grad * m * (1.0 - o)]
                if tile == 1:
                    one = [
                        jnp.where(lane < rest, one[0], jnp.where(lane < 2 * rest, pltpu.roll(one[1], rest, 1), jnp.where(lane < 3 * rest, pltpu.roll(one[2], 2 * rest, 1), 0.0)))
                    ]
                parts += one
            for i, part in enumerate(parts):
                wide[i, rows_at, :] = part
                wide[count + i, rows_at, :] = shifted[i]
            return tuple(new), tuple(keep * part for part in parts), tuple(t + p for t, p in zip(totals, parts))

        state = (
            tuple(carry[t] for t in range(tiles)),
            tuple(after[i] for i in range(count)),
            tuple(bias_ref[:, pl.ds(i * LANES, LANES)] for i in range(count)),
        )
        arriving, shifted, totals = lax.fori_loop(0, block - low, token, state)
        for tile in range(tiles):
            carry[tile] = arriving[tile]
        for i in range(count):
            after[i] = shifted[i]
            bias_ref[:, pl.ds(i * LANES, LANES)] = totals[i]

        @pl.when(which == 0)
        def _():
            for row in range(HEAD):
                for i in range(2 * count):
                    wide[i, pl.ds(row, MEMBERS, stride=block), :] = jnp.zeros((MEMBERS, LANES), F32)
            for i in range(count):
                wide[count + i, pl.ds(EDGE, MEMBERS, stride=block), :] = shifted[i]

        for i in range(2 * count):
            grads_ref[:, :, pl.ds(i * LANES, LANES)] = wide[i].astype(BF16).reshape(MEMBERS, block, LANES)


def backward(act, keep, cot, enter, arrive, final, tiles, rest):
    length, members, half = act.shape
    block = row_block(length)
    blocks = length // block
    lanes = cot.shape[2]
    turn = lambda i: jnp.where(i < blocks, i, 2 * blocks - 1 - i)
    return pl.pallas_call(
        functools.partial(backward_kernel, tiles, rest, blocks),
        grid=(2 * blocks,),
        out_shape=(
            jax.ShapeDtypeStruct((members, length, lanes), BF16),
            jax.ShapeDtypeStruct((members, length, 2 * half), BF16),
            jax.ShapeDtypeStruct((members, half), F32),
        ),
        in_specs=[
            pl.BlockSpec((block, members, half), lambda i: (turn(i), 0, 0)),
            pl.BlockSpec((block, members, LANES), lambda i: (turn(i), 0, 0)),
            pl.BlockSpec((members, block, lanes), lambda i: (0, turn(i), 0)),
            *in_vmem(3),
        ],
        out_specs=(
            pl.BlockSpec((members, block, lanes), lambda i: (0, jnp.minimum(i, blocks - 1), 0)),
            pl.BlockSpec((members, block, 2 * half), lambda i: (0, jnp.minimum(2 * blocks - 1 - i, blocks - 1), 0)),
            pl.BlockSpec((members, half), lambda i: (0, 0)),
        ),
        scratch_shapes=[
            pltpu.VMEM((length, tiles, members, LANES), F32),
            pltpu.VMEM((tiles, members * block, LANES), F32),
            pltpu.VMEM((2 * half // LANES, members * block, LANES), F32),
            pltpu.VMEM((tiles, members * block, LANES), F32),
            pltpu.VMEM((tiles, members, LANES), F32),
            pltpu.VMEM((half // LANES, members, LANES), F32),
        ],
        compiler_params=params(),
        cost_estimate=pl.CostEstimate(
            flops=60 * members * length * half,
            bytes_accessed=8 * act.size + 4 * members * length * half,
            transcendentals=0,
        ),
        name="backward",
    )(act, keep, cot, enter, arrive, final)


def adamw(master, gradient, moment_one, moment_two, rate):
    moment_one = BETA_ONE * moment_one + (1.0 - BETA_ONE) * gradient
    moment_two = BETA_TWO * moment_two + (1.0 - BETA_TWO) * gradient * gradient
    step_size = (
        moment_one
        / (1.0 - BETA_ONE**STEP)
        / (jnp.sqrt(moment_two / (1.0 - BETA_TWO**STEP)) + EPSILON)
    )
    return (master - rate * (step_size + DECAY_RATE * master), moment_one, moment_two)


def three_parts(value):
    parts = []
    for _ in range(3):
        part = lax.reduce_precision(value, 8, 7)
        parts.append(part.astype(BF16))
        value = value - part
    return parts


def channel_tiles(vector, member, rest):
    width = vector.shape[-1]
    axis = vector.ndim - 1
    pieces = [
        lax.dynamic_slice_in_dim(vector, member * LANES, LANES, axis),
        lax.dynamic_slice_in_dim(vector, (MEMBERS + member) * LANES, LANES, axis),
        lax.dynamic_slice_in_dim(vector, 2 * MEMBERS * LANES + member * rest, rest, axis),
    ]
    return pieces


def widen(part):
    return jnp.pad(part, [(0, 0)] * (part.ndim - 1) + [(0, LANES - part.shape[-1])])


def on_device(
    inputs,
    boundary,
    start_state,
    weight,
    gate_bias,
    first_weight,
    second_weight,
    first_bias,
    second_bias,
    cotangent,
    final_cotangent,
):
    here = Place()
    tokens, width = inputs.shape[1:]
    rest = sizes(width)[1]
    member = here.member.astype(jnp.int32).reshape(1)
    taps, own_rows, columns = weight.shape
    split = 6 * LANES
    group_rows = MEMBERS * own_rows
    length = HEAD + tokens
    deep_groups = [[lo + 2 * h for h in range(here.depth)] for lo in range(2)]
    wide_groups = [[jl + 4 * h for h in range(here.wide)] for jl in range(4)]

    pairs = here.exchange(*pack_weight(weight, member))
    parts = place_weight(pairs, member, split)

    def all_rows(part):
        cols = part.shape[-1]
        if here.wide > 1:
            part = lax.all_gather(part, "stream", axis=0, axis_index_groups=wide_groups)
            part = part.reshape(here.wide, 2, 4 * own_rows, cols).swapaxes(0, 1)
        part = part.reshape(-1, cols)
        return lax.all_gather(part, "seq", axis=0, tiled=True, axis_index_groups=deep_groups)

    weights = [all_rows(part) for part in parts]

    edge = lax.ppermute(inputs[0, -1:, :], "seq", [(i, i + 1) for i in range(here.n_seq - 1)])
    keeping = (1 - boundary[0]).astype(BF16)
    head = jnp.concatenate(
        [jnp.pad(keeping, (0, width - tokens))[None]]
        + [part for part in three_parts(start_state)]
        + [part for part in three_parts(final_cotangent)]
        + [jnp.zeros((HEAD - 8, width), BF16), edge],
        axis=0,
    )
    own = jnp.concatenate([head, inputs[0]], axis=0)
    middle = (length // 32) * 16
    from_y = here.flip(own, here.member_mask(2))
    from_x = here.flip(own, here.member_mask(4))
    both_low = here.flip(from_y[:middle], here.member_mask(4))
    both_high = here.flip(from_x[middle:], here.member_mask(2))
    from_both = jnp.concatenate([both_low, both_high], axis=0)
    mine = [own, from_y, from_x, from_both]
    theirs = [here.flip(piece, 1) for piece in mine]
    x_all = jnp.stack([piece for pair in zip(mine, theirs) for piece in pair])

    cot_own = jnp.concatenate([jnp.zeros((HEAD, width), BF16), cotangent[0]], axis=0)
    cot_all = jnp.concatenate(here.exchange(*pack_channels(cot_own, member)), axis=0)
    cots = [cot_all[:, :, :LANES], cot_all[:, :, LANES:]]

    keep = x_all[:, 0, :tokens].astype(F32).T
    keep = jnp.pad(keep, ((HEAD, 0), (0, 0)))
    keep = jnp.broadcast_to(keep[:, :, None], (length, MEMBERS, LANES))
    head_all = x_all[:, 1:7].astype(F32)
    starts = channel_tiles(head_all[:, 0] + head_all[:, 1] + head_all[:, 2], here.member, rest)
    finals = channel_tiles(head_all[:, 3] + head_all[:, 4] + head_all[:, 5], here.member, rest)
    all_bits = [1 << b for b in range(here.count.bit_length() - 1)]
    bias_all = here.gather_flips(gate_bias.astype(BF16)[None], all_bits)
    order = here.linear ^ jnp.arange(here.count)
    bias_all = jnp.take(bias_all, order, axis=0).astype(F32).reshape(3, width)
    bias_parts = channel_tiles(bias_all, here.member, rest)
    biases = [
        bias_parts[0].reshape(1, 3 * LANES),
        jnp.concatenate([bias_parts[1].reshape(1, 3 * LANES), widen(bias_parts[2].reshape(1, 3 * rest))], axis=1),
    ]
    lower = ((jnp.arange(MEMBERS) >> 2) ^ (here.seq % 2)) == 0

    def both_halves(value):
        other = jnp.concatenate([value[4:], value[:4]], axis=0)
        mask = lower[:, None]
        return jnp.where(mask, value, other), jnp.where(mask, other, value)

    gradients, outs = [], []
    for chunk in range(2):
        tiles = chunk + 1
        act, summary = forward(x_all, weights[chunk], biases[chunk], keep, cots[chunk], tiles, rest)
        every = here.gather_flips(summary[None], here.deep_bits)
        enters, arrives, ends = [], [], []
        for tile in range(tiles):
            where = chunk + tile
            state, back = widen(starts[where]), widen(finals[where])
            enter, arrive = state, back
            for z in range(here.depth):
                part = jnp.take(every, z ^ here.high, axis=0)
                a_low, a_high = both_halves(part[3 * tile])
                b_low, b_high = both_halves(part[3 * tile + 1])
                between = a_low * state + b_low
                enter = jnp.where(z == here.high, jnp.where(lower[:, None], state, between), enter)
                state = a_high * between + b_high
            for z in reversed(range(here.depth)):
                part = jnp.take(every, z ^ here.high, axis=0)
                a_low, a_high = both_halves(part[3 * tile])
                c_low, c_high = both_halves(part[3 * tile + 2])
                between = a_high * back + c_high
                arrive = jnp.where(z == here.high, jnp.where(lower[:, None], between, back), arrive)
                back = a_low * between + c_low
            enters.append(enter)
            arrives.append(arrive)
            ends.append(state)
        hidden, grads, bias_grad = backward(
            act, keep, cots[chunk], jnp.stack(enters), jnp.stack(arrives), jnp.stack(ends), tiles, rest
        )
        flat = grads.reshape(MEMBERS * length, -1)
        local = dot_f32(x_all.reshape(MEMBERS * length, width), flat, ((0,), (0,))).astype(BF16)
        cols = local.shape[-1]
        summed = lax.psum_scatter(local, "seq", scatter_dimension=0, tiled=True, axis_index_groups=deep_groups)
        if here.wide > 1:
            summed = summed.reshape(2, here.wide, 4 * own_rows, cols).swapaxes(0, 1).reshape(-1, cols)
            summed = lax.psum_scatter(summed, "stream", scatter_dimension=0, tiled=True, axis_index_groups=wide_groups)
        gradients.append(summed.reshape(MEMBERS, own_rows, cols))
        outs.append((hidden, flat, jnp.sum(bias_grad, axis=0)))

    hidden_all = jnp.concatenate([outs[0][0], outs[1][0]], axis=-1)
    hidden_own = place_channels(here.exchange(hidden_all[0::2], hidden_all[1::2]), member, width)
    hidden = hidden_own[None, HEAD:]
    whole_final = jnp.sum(hidden_own[:3].astype(F32), axis=0, keepdims=True)
    own_columns = width // here.n_seq
    final_state = lax.dynamic_slice_in_dim(whole_final, here.seq * own_columns, own_columns, 1)

    back_all = dot_f32(outs[0][1], weights[0], ((1,), (1,))) + dot_f32(outs[1][1], weights[1], ((1,), (1,)))
    back_all = back_all.astype(BF16).reshape(4, 2, length, width)
    even, odd = back_all[:, 0], back_all[:, 1]
    pair_sum = even.astype(F32) + here.flip(odd, 1).astype(F32)
    sent = pair_sum.astype(BF16)
    input_sum = pair_sum[0]
    for i in (1, 2, 3):
        input_sum = input_sum + here.flip(sent[i], here.member_mask(2 * i)).astype(F32)
    from_next = lax.ppermute(input_sum[EDGE:HEAD], "seq", [(i + 1, i) for i in range(here.n_seq - 1)])
    last = lax.broadcasted_iota(jnp.int32, (tokens, 1), 0) == tokens - 1
    input_gradient = (input_sum[HEAD:] + jnp.where(last, from_next, 0.0)).astype(BF16)[None]

    bias_sum = jnp.concatenate([outs[0][2], outs[1][2]])[None]
    bias_sum = here.sum_flips(bias_sum, here.deep_bits + here.wide_bits)
    bias_squares = jnp.sum(bias_sum * bias_sum)
    bias_every = here.gather_flips(bias_sum, here.group_bits)
    bias_every = jnp.take(bias_every, here.member ^ jnp.arange(MEMBERS), axis=0)
    tile_a = bias_every[:, : 3 * LANES].reshape(MEMBERS, 3, LANES)
    tile_b = bias_every[:, 3 * LANES : 6 * LANES].reshape(MEMBERS, 3, LANES)
    tile_c = bias_every[:, 6 * LANES : 6 * LANES + 3 * rest].reshape(MEMBERS, 3, rest)
    natural = jnp.concatenate([t.swapaxes(0, 1).reshape(3, -1) for t in (tile_a, tile_b, tile_c)], axis=1)
    own_bias = gate_bias.shape[0]
    bias_raw = lax.dynamic_slice_in_dim(natural.reshape(-1), here.linear * own_bias, own_bias, 0)

    squares = sum(jnp.sum(jnp.square(g.astype(F32))) for g in gradients)
    first_plane = (here.high == 0) & (here.stream // 4 == 0)
    squares = squares + jnp.where(first_plane, bias_squares, 0.0)
    squares = here.sum_flips(jnp.broadcast_to(squares, (8, LANES)), all_bits)
    gradient_norm = jnp.sqrt(squares[0, 0])
    clip_factor = jnp.minimum(1.0, CLIP_NORM / (gradient_norm + 1e-06))
    raw = place_gradient(here.exchange(*pick_gradient(*gradients, member)), member, weight.shape)
    weight_gradient = clip_factor * raw
    bias_gradient = clip_factor * bias_raw
    new_weight, new_first_weight, new_second_weight = adamw(
        weight, weight_gradient, first_weight, second_weight, RATE_WEIGHT
    )
    new_bias, new_first_bias, new_second_bias = adamw(
        gate_bias, bias_gradient, first_bias, second_bias, RATE_BIAS
    )
    return (
        hidden,
        final_state,
        input_gradient,
        weight_gradient,
        bias_gradient,
        gradient_norm,
        new_weight,
        new_first_weight,
        new_second_weight,
        new_bias,
        new_first_bias,
        new_second_bias,
    )


def solution(mesh):
    placed = (
        P("stream", "seq", None),
        P("stream", "seq"),
        P("stream", None),
        P(None, ("seq", "stream"), None),
        P(("seq", "stream")),
        P(None, ("seq", "stream"), None),
        P(None, ("seq", "stream"), None),
        P(("seq", "stream")),
        P(("seq", "stream")),
        P("stream", "seq", None),
        P("stream", None),
    )
    return jax.shard_map(
        on_device,
        mesh=mesh,
        in_specs=placed,
        out_specs=(
            P("stream", "seq", None),
            P("stream", "seq"),
            P("stream", "seq", None),
            P(None, ("seq", "stream"), None),
            P(("seq", "stream")),
            P(),
            P(None, ("seq", "stream"), None),
            P(None, ("seq", "stream"), None),
            P(None, ("seq", "stream"), None),
            P(("seq", "stream")),
            P(("seq", "stream")),
            P(("seq", "stream")),
        ),
        check_vma=False,
    )
```

time: 3500 us -> 886 us (0.25)
  waiting for transfers between devices: 1970 us -> 270 us
  local copies, waits for them, and re-layouts: 810 us -> 83.8 us
  Pallas kernels: 0 us -> 292 us
  blocking collectives: 268 us -> 0 us
  other arithmetic: 237 us -> 57.7 us
  matrix products: 164 us -> 107 us
  starting transfers between devices: 6.2 us -> 49 us
    unnamed x3 -> x4, waiting for transfers between devices: 1680 us -> 0.07 us
    slice x128 -> x25, local copies, waits for them, and re-layouts: 329 us -> 22.7 us  [the longest x8 9.63 us: exchange(): pairs = [jnp.stack([even[i], sibling[i]]) for i in range(4)]]
    all_gather x1 -> x2, waiting for transfers between devices: 293 us -> 0.02 us  [all_rows(): lax.all_gather(part, 'seq', axis=0, tiled=True, axis_index_groups=deep_gr...]
    pallas_call x0 -> x10, Pallas kernels: none -> 292 us  [the longest x2 141 us: backward(): pl.pallas_call(functools.partial(backward_kernel, tiles, rest, blocks), g...]
    ppermute x2 -> x49, waiting for transfers between devices: 0.01 us -> 270 us  [the longest x47 270 us: flip(): return lax.ppermute(block, AXES, [(n, n ^ mask) for n in range(self.count)])]
    pad x64 -> x2, local copies, waits for them, and re-layouts: 195 us -> 0.14 us  [the longest x1 0.13 us: on_device(): keep = jnp.pad(keep, ((HEAD, 0), (0, 0)))]
    another operation x1 -> x2, local copies, waits for them, and re-layouts: 181 us -> 1.65 us  [the longest x1 1.57 us: on_device(): x_all = jnp.stack([piece for pair in zip(mine, theirs) for piece in pair])]
    all_gather x4 -> x0, blocking collectives: 122 us -> none  [carried_in(): everything = jax.tree.map(lambda part: lax.all_gather(part, axis), value)]
  transfers between devices with their start and end apart: 4 -> 53, of which waited for: 2 -> 23; matrix products, arithmetic and copies ran while one was open for 2% -> 27% of each run, Pallas kernels for 0% -> 23%
where the time goes in v1:
time: 886 us; the launch traced here: 878 us
  Pallas kernels  292 us (33%)
  waiting for transfers between devices  270 us (30%)
  matrix products  107 us (12%)
  local copies, waits for them, and re-layouts  83.8 us (9%)
  other arithmetic  57.7 us (7%)
  starting transfers between devices  49 us (6%)
  between operations  18.8 us (2%)
    ppermute x47, waiting for transfers between devices, flip(): return lax.ppermute(block, AXES, [(n, n ^ mask) for n in range(self.count)])  270 us
    pallas_call x2, Pallas kernels, backward(): pl.pallas_call(functools.partial(backward_kernel, tiles, rest, blocks), g...  141 us
    pallas_call x2, Pallas kernels, forward(): pl.pallas_call(functools.partial(forward_kernel, tiles, rest), grid=(leng...  129 us
    dot_general x4, matrix products, dot_f32(): return lax.dot_general(a, b, (dims, ((), ())), preferred_element_type=F32)  107 us
    ppermute x47, starting transfers between devices, flip(): return lax.ppermute(block, AXES, [(n, n ^ mask) for n in range(self.count)])  43.7 us
    unnamed x70, local copies, waits for them, and re-layouts  28.3 us
  transfers between devices with their start and end apart: 53, of which 23 were waited for; matrix products, arithmetic and copies ran while one was open for 27% of the time, Pallas kernels for 23%

profile of v1, /device:TPU:0, one launch (start us, length us, event | category | flops | bytes accessed | tf_op | source)
XLA Modules:
  0.0 877.8 jit_solution(3543179348288880702)
XLA Ops:
  7.2 3.9 pack_weight.1
  19.7 9.5 %collective-permute-done.10.y_ref = bf16[2,72,1792]{2,1,0:T(8,128)(2,1)S(1)} collective-permute-done((bf16[2,72,1792]{2,1,0:T(8,128)(2,1)S(1)}, bf16[2,72,1792]{2,1,0:T(8,128)(2,1)S(1)}, u32[]{:S(2)}, u32[]{:S(2)}) %collective-permute-start.10) | collective-permute-done | bytes 516128 | tf_op jit(solution)/shard_map/ppermute | solution.py:58
  31.9 9.7 %collective-permute-done.12.both_ref = bf16[2,72,1792]{2,1,0:T(8,128)(2,1)S(1)} collective-permute-done((bf16[2,72,1792]{2,1,0:T(8,128)(2,1)S(1)}, bf16[2,72,1792]{2,1,0:T(8,128)(2,1)S(1)}, u32[]{:S(2)}, u32[]{:S(2)}) %collective-permute-start.12) | collective-permute-done | bytes 516128 | tf_op jit(solution)/shard_map/ppermute | solution.py:58
  46.3 3.6 collective-permute-start
  51.5 3.9 pack_channels.1
  67.3 8.8 concatenate.188
  93.4 53.4 %collective-permute-done.19 = bf16[2,528,384]{2,1,0:T(8,128)(2,1)} collective-permute-done((bf16[2,528,384]{2,1,0:T(8,128)(2,1)}, bf16[2,528,384]{2,1,0:T(8,128)(2,1)}, u32[]{:S(2)}, u32[]{:S(2)}) %collective-permute-start.19) | collective-permute-done | bytes 811040 | tf_op jit(solution)/shard_map/ppermute | solution.py:58
  155.1 10.4 %collective-permute-done.21 = bf16[2,528,384]{2,1,0:T(8,128)(2,1)S(1)} collective-permute-done((bf16[2,528,384]{2,1,0:T(8,128)(2,1)}, bf16[2,528,384]{2,1,0:T(8,128)(2,1)S(1)}, u32[]{:S(2)}, u32[]{:S(2)}) %collective-permute-start.21) | collective-permute-done | bytes 811040 | tf_op jit(solution)/shard_map/ppermute | solution.py:58
  184.5 16.1 %collective-permute-done.6 = bf16[256,2304]{1,0:T(8,128)(2,1)S(1)} collective-permute-done((bf16[256,2304]{1,0:T(8,128)(2,1)S(1)}, bf16[256,2304]{1,0:T(8,128)(2,1)S(1)}, u32[]{:S(2)}, u32[]{:S(2)}) %collective-permute-start.6) | collective-permute-done | bytes 1179680 | tf_op jit(solution)/shard_map/ppermute | solution.py:58
  215.1 42.9 %forward.2 = (f32[528,8,384]{2,1,0:T(8,128)}, f32[3,8,128]{2,1,0:T(8,128)}) custom-call(bf16[8,528,2304]{2,1,0:T(8,128)(2,1)} %bitcast_dynamic-update-slice_fusion.x_ref, bf16[2304,768]{1,0:T(8,128)(2,1)} %all-gather.3.cloned.1.call-done.w_ref, f32[1,384]{1,0:T(1,128)} %bitcast.774, f32[528,8,128]{2,1,0:T(8,128)} %broadcast_in_dim.519.keep_ref, ...), custom_call_target="tpu_custom_call" | custom-call | flops 14948499456 | bytes 29491200 | tf_op jit(solution)/shard_map/forward/pallas_call | solution.py:361
  269.6 86.3 %forward.3 = (f32[528,8,512]{2,1,0:T(8,128)}, f32[6,8,128]{2,1,0:T(8,128)}) custom-call(bf16[8,528,2304]{2,1,0:T(8,128)(2,1)} %bitcast_dynamic-update-slice_fusion.x_ref, bf16[2304,1024]{1,0:T(8,128)(2,1)} %all-gather.5.cloned.1.call-done.w_ref, f32[1,512]{1,0:T(1,128)} %fusion.66.bias_ref, f32[528,8,128]{2,1,0:T(8,128)} %broadcast_in_dim.519.keep_ref, ...), custom_call_target="tpu_custom_call" | custom-call | flops 19931332608 | bytes 32833536 | tf_op jit(solution)/shard_map/forward/pallas_call | solution.py:361
  356.9 17.8 %backward.2 = (bf16[8,528,128]{2,1,0:T(8,128)(2,1)}, bf16[8,528,768]{2,1,0:T(8,128)(2,1)}, f32[8,384]{1,0:T(8,128)}) custom-call(f32[528,8,384]{2,1,0:T(8,128)} %get-tuple-element.37.act_ref, f32[528,8,128]{2,1,0:T(8,128)} %broadcast_in_dim.519.keep_ref, bf16[8,528,128]{2,1,0:T(8,128)(2,1)} %slice.1109.cot_ref, f32[1,8,128]{2,1,0:T(8,128)} %fusion.13.enter_ref, ...), custom_call_target="tpu_custom_call" | custom-call | flops 97320960 | bytes 19464192 | tf_op jit(solution)/shard_map/backward/pallas_call | solution.py:521
  377.0 22.1 %bitcast_convert_fusion.1 = bf16[2304,768]{1,0:T(8,128)(2,1)} fusion(bf16[8,528,2304]{2,1,0:T(8,128)(2,1)} %bitcast_dynamic-update-slice_fusion.x_ref, bf16[8,528,768]{2,1,0:T(8,128)(2,1)} %get-tuple-element.44), kind=kOutput, calls=%fused_computation.7 | convolution fusion | flops 14950268928 | bytes 29491200 | tf_op jit(solution)/shard_map/dot_general | solution.py:38
  401.6 122.8 %backward.3 = (bf16[8,528,256]{2,1,0:T(8,128)(2,1)}, bf16[8,528,1024]{2,1,0:T(8,128)(2,1)}, f32[8,512]{1,0:T(8,128)}) custom-call(f32[528,8,512]{2,1,0:T(8,128)} %get-tuple-element.41.act_ref, f32[528,8,128]{2,1,0:T(8,128)} %broadcast_in_dim.519.keep_ref, bf16[8,528,256]{2,1,0:T(8,128)(2,1)} %slice.1153.cot_ref, f32[2,8,128]{2,1,0:T(8,128)} %pad_maximum_fusion.22.enter_ref, ...), custom_call_target="tpu_custom_call" | custom-call | flops 129761280 | bytes 25952256 | tf_op jit(solution)/shard_map/backward/pallas_call | solution.py:521
  524.4 28.0 %bitcast_convert_fusion = bf16[2304,1024]{1,0:T(8,128)(2,1)} fusion(bf16[8,528,2304]{2,1,0:T(8,128)(2,1)} %bitcast_dynamic-update-slice_fusion.x_ref, bf16[8,528,1024]{2,1,0:T(8,128)(2,1)} %get-tuple-element.45), kind=kOutput, calls=%fused_computation.6 | convolution fusion | flops 19933691904 | bytes 32833536 | tf_op jit(solution)/shard_map/dot_general | solution.py:38
  552.4 27.8 %fusion.82 = f32[4224,2304]{1,0:T(8,128)} fusion(bf16[4224,1024]{1,0:T(8,128)(2,1)} %bitcast.775, bf16[2304,1024]{1,0:T(8,128)(2,1)} %all-gather.5.cloned.1.call-done.w_ref), kind=kOutput, calls=%fused_computation.378 | convolution fusion | flops 19931332608 | bytes 52297728 | tf_op jit(solution)/shard_map/dot_general | solution.py:38
  580.3 29.2 %add_convert_fusion = bf16[4224,2304]{1,0:T(8,128)(2,1)} fusion(f32[4224,2304]{1,0:T(8,128)} %fusion.82, bf16[4224,768]{1,0:T(8,128)(2,1)} %bitcast.776, bf16[2304,768]{1,0:T(8,128)(2,1)S(1)} %copy-done.25), kind=kOutput, calls=%fused_computation.2 | convolution fusion | flops 14967963648 | bytes 68419584 | tf_op jit(solution)/shard_map/dot_general | solution.py:38
  609.5 8.2 slice_bitcast_fusion
  622.3 3.5 fusion.73
  626.3 4.8 collective-permute-done.36
  635.2 3.6 collective-permute-done.47
  647.0 3.5 collective-permute-start.29
  658.8 6.6 collective-permute-done.27.y_ref
  668.2 15.5 %collective-permute-done.29.both_ref = bf16[2,528,384]{2,1,0:T(8,128)(2,1)} collective-permute-done((bf16[2,528,384]{2,1,0:T(8,128)(2,1)S(1)}, bf16[2,528,384]{2,1,0:T(8,128)(2,1)}, u32[]{:S(2)}, u32[]{:S(2)}) %collective-permute-start.29) | collective-permute-done | bytes 811040 | tf_op jit(solution)/shard_map/ppermute | solution.py:58
  683.6 4.1 place_channels.1
  694.4 15.0 %fusion.70 = (bf16[4,528,2304]{2,1,0:T(8,128)(2,1)S(1)}, f32[4,528,2304]{2,1,0:T(8,128)}) fusion(bf16[4,528,2304]{2,1,0:T(8,128)(2,1)} %collective-permute-done.30, bf16[4,2,528,2304]{3,2,1,0:T(8,128)(2,1)} %bitcast.747), kind=kLoop, calls=%fused_computation.368 | loop fusion | flops 19464192 | bytes 48660480 | tf_op jit(solution)/shard_map/convert_element_type | solution.py:727
  723.8 105.7 %collective-permute-done.43.y_ref = bf16[2,72,1792]{2,1,0:T(8,128)(2,1)S(1)} collective-permute-done((bf16[2,72,1792]{2,1,0:T(8,128)(2,1)S(1)}, bf16[2,72,1792]{2,1,0:T(8,128)(2,1)S(1)}, u32[]{:S(2)}, u32[]{:S(2)}) %collective-permute-start.43) | collective-permute-done | bytes 516128 | tf_op jit(solution)/shard_map/ppermute | solution.py:58
  834.4 8.6 collective-permute-done.45.both_ref
  843.0 4.0 place_gradient.1
  848.4 5.6 fusion.2
  859.3 6.2 multiply_subtract_fusion
  865.5 4.2 fusion.5
  (298 shorter events, 163.9 us)
Async XLA Ops:
  7.2 205.9 %all-gather.3.cloned.1.call-start = ((), (), s32[]{:S(2)}) async-start(), calls=%async_computation.2 | async-start | bytes 4423680 | tf_op jit(solution)/shard_map/all_gather | solution.py:626
  18.8 22.8 %collective-permute-start.12 = (bf16[2,72,1792]{2,1,0:T(8,128)(2,1)S(1)}, bf16[2,72,1792]{2,1,0:T(8,128)(2,1)S(1)}, u32[]{:S(2)}, u32[]{:S(2)}) collective-permute-start(bf16[2,72,1792]{2,1,0:T(8,128)(2,1)S(1)} %pad_maximum_fusion.10), channel_id=1, source_target_pairs={{0,6},{1,7},{2,4},{3,5},{4,2},{5,3},{6,0},{7,1},{8,14},{9,15},{10,... | collective-permute-start | bytes 1548296 | tf_op jit(solution)/shard_map/ppermute | solution.py:58
  45.3 224.2 %all-gather.5.cloned.1.call-start = ((), (), s32[]{:S(2)}) async-start(), calls=%async_computation.3 | async-start | bytes 5898240 | tf_op jit(solution)/shard_map/all_gather | solution.py:626
  46.3 21.0 %collective-permute-start = (bf16[1,2304]{1,0:T(2,128)(2,1)S(1)}, bf16[1,2304]{1,0:T(2,128)(2,1)S(1)}, u32[]{:S(2)}, u32[]{:S(2)}) collective-permute-start(bf16[1,2304]{1,0:T(2,128)(2,1)S(1)} %slice_bitcast_fusion.9), channel_id=1, source_target_pairs={{0,4},{4,8},{8,12},{12,16},{16,20},{20,24},{24,28},{1,5},{5,9},{9,... | collective-permute-start | bytes 13832 | tf_op jit(solution)/shard_map/ppermute | solution.py:630
  55.4 25.0 %collective-permute-start.18 = (bf16[4,528,384]{2,1,0:T(8,128)(2,1)}, bf16[4,528,384]{2,1,0:T(8,128)(2,1)}, u32[]{:S(2)}, u32[]{:S(2)}) collective-permute-start(bf16[4,528,384]{2,1,0:T(8,128)(2,1)} %get-tuple-element.36), channel_id=1, source_target_pairs={{0,1},{1,0},{2,3},{3,2},{4,5},{5,4},{6,7},{7,6},{8,9},{9,8},{10,11... | collective-permute-start | bytes 4866056 | tf_op jit(solution)/shard_map/ppermute | solution.py:58
  76.0 79.1 %collective-permute-start.2 = (bf16[528,2304]{1,0:T(8,128)(2,1)S(1)}, bf16[528,2304]{1,0:T(8,128)(2,1)}, u32[]{:S(2)}, u32[]{:S(2)}) collective-permute-start(bf16[528,2304]{1,0:T(8,128)(2,1)S(1)} %concatenate.188), channel_id=1, source_target_pairs={{0,2},{1,3},{2,0},{3,1},{4,6},{5,7},{6,4},{7,5},{8,10},{9,11},{10,... | collective-permute-start | bytes 7299080 | tf_op jit(solution)/shard_map/ppermute | solution.py:58
  77.6 94.3 %collective-permute-start.4 = (bf16[528,2304]{1,0:T(8,128)(2,1)S(1)}, bf16[528,2304]{1,0:T(8,128)(2,1)}, u32[]{:S(2)}, u32[]{:S(2)}) collective-permute-start(bf16[528,2304]{1,0:T(8,128)(2,1)S(1)} %concatenate.188), channel_id=1, source_target_pairs={{0,4},{1,5},{2,6},{3,7},{4,0},{5,1},{6,2},{7,3},{8,12},{9,13},{10,... | collective-permute-start | bytes 7299080 | tf_op jit(solution)/shard_map/ppermute | solution.py:58
  79.2 98.6 %collective-permute-start.1 = (bf16[528,2304]{1,0:T(8,128)(2,1)S(1)}, bf16[528,2304]{1,0:T(8,128)(2,1)}, u32[]{:S(2)}, u32[]{:S(2)}) collective-permute-start(bf16[528,2304]{1,0:T(8,128)(2,1)S(1)} %concatenate.188), channel_id=1, source_target_pairs={{0,1},{1,0},{2,3},{3,2},{4,5},{5,4},{6,7},{7,6},{8,9},{9,8},{10,11... | collective-permute-start | bytes 7299080 | tf_op jit(solution)/shard_map/ppermute | solution.py:58
  84.8 62.0 %collective-permute-start.19 = (bf16[2,528,384]{2,1,0:T(8,128)(2,1)}, bf16[2,528,384]{2,1,0:T(8,128)(2,1)}, u32[]{:S(2)}, u32[]{:S(2)}) collective-permute-start(bf16[2,528,384]{2,1,0:T(8,128)(2,1)} %pad_maximum_fusion), channel_id=1, source_target_pairs={{0,2},{1,3},{2,0},{3,1},{4,6},{5,7},{6,4},{7,5},{8,10},{9,11},{10,... | collective-permute-start | bytes 2433032 | tf_op jit(solution)/shard_map/ppermute | solution.py:58
  89.5 63.5 %collective-permute-start.20 = (bf16[2,528,384]{2,1,0:T(8,128)(2,1)}, bf16[2,528,384]{2,1,0:T(8,128)(2,1)}, u32[]{:S(2)}, u32[]{:S(2)}) collective-permute-start(bf16[2,528,384]{2,1,0:T(8,128)(2,1)} %pad_maximum_fusion.1), channel_id=1, source_target_pairs={{0,4},{1,5},{2,6},{3,7},{4,0},{5,1},{6,2},{7,3},{8,12},{9,13},{10,... | collective-permute-start | bytes 2433032 | tf_op jit(solution)/shard_map/ppermute | solution.py:58
  146.9 18.7 %collective-permute-start.21 = (bf16[2,528,384]{2,1,0:T(8,128)(2,1)}, bf16[2,528,384]{2,1,0:T(8,128)(2,1)S(1)}, u32[]{:S(2)}, u32[]{:S(2)}) collective-permute-start(bf16[2,528,384]{2,1,0:T(8,128)(2,1)} %pad_maximum_fusion.2), channel_id=1, source_target_pairs={{0,6},{1,7},{2,4},{3,5},{4,2},{5,3},{6,0},{7,1},{8,14},{9,15},{10,... | collective-permute-start | bytes 2433032 | tf_op jit(solution)/shard_map/ppermute | solution.py:58
  150.9 499.7 %reduce-scatter.3.cloned.1.call-start = ((), (), s32[]{:S(2)}) async-start(), calls=%async_computation.4 | async-start | bytes 4423680 | tf_op jit(solution)/shard_map/reduce_scatter | solution.py:709
  155.1 45.7 %collective-permute-start.3 = (bf16[528,2304]{1,0:T(8,128)(2,1)}, bf16[528,2304]{1,0:T(8,128)(2,1)S(1)}, u32[]{:S(2)}, u32[]{:S(2)}) collective-permute-start(bf16[528,2304]{1,0:T(8,128)(2,1)} %collective-permute-done.2), channel_id=1, source_target_pairs={{0,1},{1,0},{2,3},{3,2},{4,5},{5,4},{6,7},{7,6},{8,9},{9,8},{10,11... | collective-permute-start | bytes 7299080 | tf_op jit(solution)/shard_map/ppermute | solution.py:58
  173.3 27.3 %collective-permute-start.7 = (bf16[272,2304]{1,0:T(8,128)(2,1)S(1)}, bf16[272,2304]{1,0:T(8,128)(2,1)S(1)}, u32[]{:S(2)}, u32[]{:S(2)}) collective-permute-start(bf16[272,2304]{1,0:T(8,128)(2,1)S(1)} %slice.1099), channel_id=1, source_target_pairs={{0,2},{1,3},{2,0},{3,1},{4,6},{5,7},{6,4},{7,5},{8,10},{9,11},{10,... | collective-permute-start | bytes 3760136 | tf_op jit(solution)/shard_map/ppermute | solution.py:58
  176.2 24.3 %collective-permute-start.6 = (bf16[256,2304]{1,0:T(8,128)(2,1)S(1)}, bf16[256,2304]{1,0:T(8,128)(2,1)S(1)}, u32[]{:S(2)}, u32[]{:S(2)}) collective-permute-start(bf16[256,2304]{1,0:T(8,128)(2,1)S(1)} %slice.1098), channel_id=1, source_target_pairs={{0,4},{1,5},{2,6},{3,7},{4,0},{5,1},{6,2},{7,3},{8,12},{9,13},{10,... | collective-permute-start | bytes 3538952 | tf_op jit(solution)/shard_map/ppermute | solution.py:58
  177.8 28.1 %collective-permute-start.5 = (bf16[528,2304]{1,0:T(8,128)(2,1)}, bf16[528,2304]{1,0:T(8,128)(2,1)S(1)}, u32[]{:S(2)}, u32[]{:S(2)}) collective-permute-start(bf16[528,2304]{1,0:T(8,128)(2,1)} %collective-permute-done.4), channel_id=1, source_target_pairs={{0,1},{1,0},{2,3},{3,2},{4,5},{5,4},{6,7},{7,6},{8,9},{9,8},{10,11... | collective-permute-start | bytes 7299080 | tf_op jit(solution)/shard_map/ppermute | solution.py:58
  355.9 18.8 %collective-permute-start.24 = (f32[1,6,8,128]{3,2,1,0:T(8,128)}, f32[1,6,8,128]{3,2,1,0:T(8,128)S(1)}, u32[]{:S(2)}, u32[]{:S(2)}) collective-permute-start(f32[1,6,8,128]{3,2,1,0:T(8,128)} %bitcast.754), channel_id=1, source_target_pairs={{0,8},{1,9},{2,10},{3,11},{4,12},{5,13},{6,14},{7,15},{8,0},{9,1},... | collective-permute-start | bytes 73736 | tf_op jit(solution)/shard_map/ppermute | solution.py:58
  374.7 24.5 %collective-permute-start.25 = (f32[2,6,8,128]{3,2,1,0:T(8,128)S(1)}, f32[2,6,8,128]{3,2,1,0:T(8,128)S(1)}, u32[]{:S(2)}, u32[]{:S(2)}) collective-permute-start(f32[2,6,8,128]{3,2,1,0:T(8,128)S(1)} %pad_maximum_fusion.17), channel_id=1, source_target_pairs={{0,16},{1,17},{2,18},{3,19},{4,20},{5,21},{6,22},{7,23},{8,24},{9,... | collective-permute-start | bytes 147464 | tf_op jit(solution)/shard_map/ppermute | solution.py:58
  399.1 253.7 %reduce-scatter.5.cloned.1.call-start = ((), (), s32[]{:S(2)}) async-start(), calls=%async_computation.5 | async-start | bytes 5898240 | tf_op jit(solution)/shard_map/reduce_scatter | solution.py:709
  617.7 76.8 %collective-permute-start.30 = (bf16[4,528,2304]{2,1,0:T(8,128)(2,1)}, bf16[4,528,2304]{2,1,0:T(8,128)(2,1)}, u32[]{:S(2)}, u32[]{:S(2)}) collective-permute-start(bf16[4,528,2304]{2,1,0:T(8,128)(2,1)} %slice_bitcast_fusion), channel_id=1, source_target_pairs={{0,1},{1,0},{2,3},{3,2},{4,5},{5,4},{6,7},{7,6},{8,9},{9,8},{10,11... | collective-permute-start | bytes 29196296 | tf_op jit(solution)/shard_map/ppermute | solution.py:58
  625.8 17.6 %collective-permute-start.26 = (bf16[4,528,384]{2,1,0:T(8,128)(2,1)}, bf16[4,528,384]{2,1,0:T(8,128)(2,1)}, u32[]{:S(2)}, u32[]{:S(2)}) collective-permute-start(bf16[4,528,384]{2,1,0:T(8,128)(2,1)} %get-tuple-element.94), channel_id=1, source_target_pairs={{0,1},{1,0},{2,3},{3,2},{4,5},{5,4},{6,7},{7,6},{8,9},{9,8},{10,11... | collective-permute-start | bytes 4866056 | tf_op jit(solution)/shard_map/ppermute | solution.py:58
  646.0 19.5 %collective-permute-start.27 = (bf16[2,528,384]{2,1,0:T(8,128)(2,1)}, bf16[2,528,384]{2,1,0:T(8,128)(2,1)}, u32[]{:S(2)}, u32[]{:S(2)}) collective-permute-start(bf16[2,528,384]{2,1,0:T(8,128)(2,1)} %pad_maximum_fusion.4), channel_id=1, source_target_pairs={{0,2},{1,3},{2,0},{3,1},{4,6},{5,7},{6,4},{7,5},{8,10},{9,11},{10,... | collective-permute-start | bytes 2433032 | tf_op jit(solution)/shard_map/ppermute | solution.py:58
  646.9 21.2 %collective-permute-start.28 = (bf16[2,528,384]{2,1,0:T(8,128)(2,1)}, bf16[2,528,384]{2,1,0:T(8,128)(2,1)S(1)}, u32[]{:S(2)}, u32[]{:S(2)}) collective-permute-start(bf16[2,528,384]{2,1,0:T(8,128)(2,1)} %pad_maximum_fusion.5), channel_id=1, source_target_pairs={{0,4},{1,5},{2,6},{3,7},{4,0},{5,1},{6,2},{7,3},{8,12},{9,13},{10,... | collective-permute-start | bytes 2433032 | tf_op jit(solution)/shard_map/ppermute | solution.py:58
  647.0 36.6 %collective-permute-start.29 = (bf16[2,528,384]{2,1,0:T(8,128)(2,1)S(1)}, bf16[2,528,384]{2,1,0:T(8,128)(2,1)}, u32[]{:S(2)}, u32[]{:S(2)}) collective-permute-start(bf16[2,528,384]{2,1,0:T(8,128)(2,1)S(1)} %pad_maximum_fusion.6), channel_id=1, source_target_pairs={{0,6},{1,7},{2,4},{3,5},{4,2},{5,3},{6,0},{7,1},{8,14},{9,15},{10,... | collective-permute-start | bytes 2433032 | tf_op jit(solution)/shard_map/ppermute | solution.py:58
  657.8 32.9 %collective-permute-start.38 = (f32[8,128]{1,0:T(8,128)S(1)}, f32[8,128]{1,0:T(8,128)S(1)}, u32[]{:S(2)}, u32[]{:S(2)}) collective-permute-start(f32[8,128]{1,0:T(8,128)S(1)} %broadcast_add_fusion), channel_id=1, source_target_pairs={{0,2},{1,3},{2,0},{3,1},{4,6},{5,7},{6,4},{7,5},{8,10},{9,11},{10,... | collective-permute-start | bytes 12296 | tf_op jit(solution)/shard_map/ppermute | solution.py:58
  692.5 23.6 %collective-permute-start.42 = (bf16[4,72,1792]{2,1,0:T(8,128)(2,1)}, bf16[4,72,1792]{2,1,0:T(8,128)(2,1)S(1)}, u32[]{:S(2)}, u32[]{:S(2)}) collective-permute-start(bf16[4,72,1792]{2,1,0:T(8,128)(2,1)} %get-tuple-element.49), channel_id=1, source_target_pairs={{0,1},{1,0},{2,3},{3,2},{4,5},{5,4},{6,7},{7,6},{8,9},{9,8},{10,11... | collective-permute-start | bytes 3096584 | tf_op jit(solution)/shard_map/ppermute | solution.py:58
  694.4 23.8 %collective-permute-start.40 = (f32[8,128]{1,0:T(8,128)S(1)}, f32[8,128]{1,0:T(8,128)S(1)}, u32[]{:S(2)}, u32[]{:S(2)}) collective-permute-start(f32[8,128]{1,0:T(8,128)S(1)} %add.411), channel_id=1, source_target_pairs={{0,8},{1,9},{2,10},{3,11},{4,12},{5,13},{6,14},{7,15},{8,0},{9,1},... | collective-permute-start | bytes 12296 | tf_op jit(solution)/shard_map/ppermute | solution.py:58
  712.6 134.4 %collective-permute-start.31 = (bf16[528,2304]{1,0:T(8,128)(2,1)}, bf16[528,2304]{1,0:T(8,128)(2,1)S(1)}, u32[]{:S(2)}, u32[]{:S(2)}) collective-permute-start(bf16[528,2304]{1,0:T(8,128)(2,1)} %get-tuple-element.90), channel_id=1, source_target_pairs={{0,2},{1,3},{2,0},{3,1},{4,6},{5,7},{6,4},{7,5},{8,10},{9,11},{10,... | collective-permute-start | bytes 7299080 | tf_op jit(solution)/shard_map/ppermute | solution.py:58
  712.9 134.1 %collective-permute-start.33 = (bf16[528,2304]{1,0:T(8,128)(2,1)}, bf16[528,2304]{1,0:T(8,128)(2,1)}, u32[]{:S(2)}, u32[]{:S(2)}) collective-permute-start(bf16[528,2304]{1,0:T(8,128)(2,1)} %get-tuple-element.91), channel_id=1, source_target_pairs={{0,6},{1,7},{2,4},{3,5},{4,2},{5,3},{6,0},{7,1},{8,14},{9,15},{10,... | collective-permute-start | bytes 7299080 | tf_op jit(solution)/shard_map/ppermute | solution.py:58
  714.4 132.6 %collective-permute-start.32 = (bf16[528,2304]{1,0:T(8,128)(2,1)}, bf16[528,2304]{1,0:T(8,128)(2,1)}, u32[]{:S(2)}, u32[]{:S(2)}) collective-permute-start(bf16[528,2304]{1,0:T(8,128)(2,1)} %get-tuple-element.92), channel_id=1, source_target_pairs={{0,4},{1,5},{2,6},{3,7},{4,0},{5,1},{6,2},{7,3},{8,12},{9,13},{10,... | collective-permute-start | bytes 7299080 | tf_op jit(solution)/shard_map/ppermute | solution.py:58
  716.3 113.2 %collective-permute-start.43 = (bf16[2,72,1792]{2,1,0:T(8,128)(2,1)S(1)}, bf16[2,72,1792]{2,1,0:T(8,128)(2,1)S(1)}, u32[]{:S(2)}, u32[]{:S(2)}) collective-permute-start(bf16[2,72,1792]{2,1,0:T(8,128)(2,1)S(1)} %pad_maximum_fusion.12), channel_id=1, source_target_pairs={{0,2},{1,3},{2,0},{3,1},{4,6},{5,7},{6,4},{7,5},{8,10},{9,11},{10,... | collective-permute-start | bytes 1548296 | tf_op jit(solution)/shard_map/ppermute | solution.py:58
  722.7 111.7 %collective-permute-start.44 = (bf16[2,72,1792]{2,1,0:T(8,128)(2,1)}, bf16[2,72,1792]{2,1,0:T(8,128)(2,1)}, u32[]{:S(2)}, u32[]{:S(2)}) collective-permute-start(bf16[2,72,1792]{2,1,0:T(8,128)(2,1)} %pad_maximum_fusion.13), channel_id=1, source_target_pairs={{0,4},{1,5},{2,6},{3,7},{4,0},{5,1},{6,2},{7,3},{8,12},{9,13},{10,... | collective-permute-start | bytes 1548296 | tf_op jit(solution)/shard_map/ppermute | solution.py:58
  (47 other events, 772.2 us)
Sparse Core Ops, SparseCore 0:
  45.4 71.7 all-gather.2
  151.0 87.6 all-gather.4
  399.2 64.9 reduce-scatter.2
  552.5 83.5 reduce-scatter.4

commit v2 on v1

v2 whole, which is shorter than its diff:
```python
import functools
import jax
import jax.numpy as jnp
from jax import lax
from jax.experimental import pallas as pl
from jax.experimental.pallas import tpu as pltpu
from jax.sharding import PartitionSpec as P

STEP = 10
BETA_ONE = 0.9
BETA_TWO = 0.95
EPSILON = 1e-08
RATE_WEIGHT = 0.01
RATE_BIAS = 1.0
DECAY_RATE = 0.1
CLIP_NORM = 1.0
FORGET_SHIFT = 6.0

AXES = ("seq", "stream")
LANES = 128
MEMBERS = 8
TAIL = 16
BF16 = jnp.bfloat16
F32 = jnp.float32
VMEM_LIMIT = 60 * 1024 * 1024


def params():
    return pltpu.CompilerParams(vmem_limit_bytes=VMEM_LIMIT)


def in_vmem(count):
    return [pl.BlockSpec(memory_space=pltpu.VMEM)] * count


def dot_f32(a, b, dims):
    return lax.dot_general(a, b, (dims, ((), ())), preferred_element_type=F32)


class Place:
    def __init__(self):
        self.n_seq = lax.axis_size("seq")
        self.n_stream = lax.axis_size("stream")
        self.depth = self.n_seq // 2
        self.wide = self.n_stream // 4
        self.count = self.n_seq * self.n_stream
        self.seq = lax.axis_index("seq")
        self.stream = lax.axis_index("stream")
        self.linear = self.seq * self.n_stream + self.stream
        self.member = (self.seq % 2) * 4 + self.stream % 4
        self.high = self.seq // 2
        self.group_bits = [1, 2, self.n_stream]
        self.deep_bits = [self.n_stream * (2 << b) for b in range(self.depth.bit_length() - 1)]
        self.wide_bits = [4 << b for b in range(self.wide.bit_length() - 1)]

    def flip(self, block, mask):
        return lax.ppermute(block, AXES, [(n, n ^ mask) for n in range(self.count)])

    def member_mask(self, p):
        return (p & 3) | ((p >> 2) * self.n_stream)

    def gather_flips(self, block, bits):
        for bit in bits:
            block = jnp.concatenate([block, self.flip(block, bit)], axis=0)
        return block

    def sum_flips(self, value, bits):
        for bit in bits:
            value = value + self.flip(value, bit)
        return value

    def pair_up(self, even, odd):
        sibling = self.flip(odd, 1)
        return [jnp.stack([even[i], sibling[i]]) for i in range(4)]

    def send_pairs(self, pairs):
        return [pairs[0]] + [self.flip(pairs[i], self.member_mask(2 * i)) for i in (1, 2, 3)]

    def exchange(self, even, odd):
        return self.send_pairs(self.pair_up(even, odd))


def after(value, *others):
    return pl.pallas_call(
        lambda *refs: None,
        out_shape=jax.ShapeDtypeStruct(value.shape, value.dtype),
        in_specs=[pl.BlockSpec(memory_space=pl.ANY)] * (1 + len(others)),
        out_specs=pl.BlockSpec(memory_space=pl.ANY),
        input_output_aliases={0: 0},
        name="after",
    )(value, *others)


def copy_kernel(in_ref, out_ref):
    out_ref[...] = in_ref[...]


def copied(value):
    rows, width = value.shape
    spec = pl.BlockSpec((rows // 4, width), lambda i: (i, 0))
    return pl.pallas_call(
        copy_kernel,
        grid=(4,),
        out_shape=jax.ShapeDtypeStruct(value.shape, value.dtype),
        in_specs=[spec],
        out_specs=spec,
        name="copied",
    )(value)


def blank(shape, dtype):
    return pl.pallas_call(
        lambda out_ref: None,
        out_shape=jax.ShapeDtypeStruct(shape, dtype),
        out_specs=pl.BlockSpec(memory_space=pl.ANY),
        name="blank",
    )()


def waiting(kernel, operands, others):
    skip = operands + len(others)
    return lambda *refs: kernel(*refs[:operands], *refs[skip:])


def unseen(others):
    return [pl.BlockSpec(memory_space=pl.ANY)] * len(others)


def sizes(width):
    whole = width // (MEMBERS * LANES)
    rest = width // MEMBERS - whole * LANES
    assert whole == 2 and 0 < 3 * rest <= LANES and LANES % rest == 0
    return whole, rest


def lane_index(shape):
    return lax.broadcasted_iota(jnp.int32, shape, len(shape) - 1)


def pack_weight_kernel(width, member_ref, weight_ref, even_ref, odd_ref):
    rest = sizes(width)[1]
    taps, rows, _ = weight_ref.shape
    per_tile = LANES // rest
    lane = lane_index((rows, LANES))
    for p in range(MEMBERS):
        to = member_ref[0] ^ p
        out = (even_ref, odd_ref)[p % 2]
        column = 0
        for tile in range(2):
            for tap in range(taps):
                for gate in range(3):
                    start = pl.multiple_of(gate * width + (tile * MEMBERS + to) * LANES, LANES)
                    out[p // 2, :, pl.ds(column, LANES)] = weight_ref[tap, :, pl.ds(start, LANES)].astype(BF16)
                    column += LANES
                if tile == 0:
                    mixed = jnp.zeros((rows, LANES), F32)
                    for gate in range(3):
                        start = pl.multiple_of(gate * width + (2 * MEMBERS + to // per_tile) * LANES, LANES)
                        part = weight_ref[tap, :, pl.ds(start, LANES)]
                        part = pltpu.roll(part, lax.rem((gate - to % per_tile) * rest + LANES, LANES), 1)
                        inside = (lane >= gate * rest) & (lane < (gate + 1) * rest)
                        mixed = jnp.where(inside, part, mixed)
                    out[p // 2, :, pl.ds(column, LANES)] = mixed.astype(BF16)
                    column += LANES


def pack_weight(weight, member):
    taps, rows, columns = weight.shape
    shape = jax.ShapeDtypeStruct((4, rows, 14 * LANES), BF16)
    return pl.pallas_call(
        functools.partial(pack_weight_kernel, columns // 3),
        out_shape=(shape, shape),
        in_specs=[pl.BlockSpec(memory_space=pltpu.SMEM)] + in_vmem(1),
        out_specs=tuple(in_vmem(2)),
        compiler_params=params(),
        name="pack_weight",
    )(member, weight)


def place_weight_kernel(split, member_ref, own_ref, y_ref, x_ref, both_ref, first_ref, second_ref):
    for p in range(MEMBERS):
        block = (own_ref, y_ref, x_ref, both_ref)[p // 2][p % 2]
        first_ref[member_ref[0] ^ p] = block[:, :split]
        second_ref[member_ref[0] ^ p] = block[:, split:]


def place_weight(pairs, member, split, *others):
    _, rows, columns = pairs[0].shape
    return pl.pallas_call(
        waiting(functools.partial(place_weight_kernel, split), 5, others),
        out_shape=(
            jax.ShapeDtypeStruct((MEMBERS, rows, split), BF16),
            jax.ShapeDtypeStruct((MEMBERS, rows, columns - split), BF16),
        ),
        in_specs=[pl.BlockSpec(memory_space=pltpu.SMEM)] + in_vmem(4) + unseen(others),
        out_specs=tuple(in_vmem(2)),
        compiler_params=params(),
        name="place_weight",
    )(member, *pairs, *others)


def pick_rows_kernel(member_ref, first_ref, second_ref, even_ref, odd_ref):
    split = first_ref.shape[-1]
    for p in range(MEMBERS):
        out = (even_ref, odd_ref)[p % 2]
        out[p // 2, :, pl.ds(0, split)] = first_ref[member_ref[0] ^ p]
        out[p // 2, :, pl.ds(split, second_ref.shape[-1])] = second_ref[member_ref[0] ^ p]


def pick_rows(first, second, member):
    shape = jax.ShapeDtypeStruct((4, first.shape[1], first.shape[2] + second.shape[2]), BF16)
    return pl.pallas_call(
        pick_rows_kernel,
        out_shape=(shape, shape),
        in_specs=[pl.BlockSpec(memory_space=pltpu.SMEM)] + in_vmem(2),
        out_specs=tuple(in_vmem(2)),
        compiler_params=params(),
        name="pick_rows",
    )(member, first, second)


def place_gradient_kernel(width, member_ref, *refs):
    rest = sizes(width)[1]
    out_ref = refs[4]
    taps, rows, _ = out_ref.shape
    per_tile = LANES // rest
    lane = lane_index((rows, LANES))
    for p in range(MEMBERS):
        source = member_ref[0] ^ p
        block_ref = refs[p // 2]
        column = 0
        for tile in range(2):
            for tap in range(taps):
                for gate in range(3):
                    start = pl.multiple_of(gate * width + (tile * MEMBERS + source) * LANES, LANES)
                    out_ref[tap, :, pl.ds(start, LANES)] = block_ref[p % 2, :, pl.ds(column, LANES)].astype(F32)
                    column += LANES
                if tile == 0:
                    mixed = block_ref[p % 2, :, pl.ds(column, LANES)].astype(F32)
                    column += LANES
                    for gate in range(3):
                        start = pl.multiple_of(gate * width + (2 * MEMBERS + source // per_tile) * LANES, LANES)
                        first = (source % per_tile) * rest
                        part = pltpu.roll(mixed, lax.rem(first - gate * rest + LANES, LANES), 1)
                        inside = (lane >= first) & (lane < first + rest)
                        old = out_ref[tap, :, pl.ds(start, LANES)]
                        out_ref[tap, :, pl.ds(start, LANES)] = jnp.where(inside, part, old)


def place_gradient(pairs, member, shape):
    return pl.pallas_call(
        functools.partial(place_gradient_kernel, shape[2] // 3),
        out_shape=jax.ShapeDtypeStruct(shape, F32),
        in_specs=[pl.BlockSpec(memory_space=pltpu.SMEM)] + in_vmem(4),
        out_specs=pl.BlockSpec(memory_space=pltpu.VMEM),
        compiler_params=params(),
        name="place_gradient",
    )(member, *pairs)


SMALL = 48


def small_rows(width, tokens, biases):
    edge = width // LANES
    keep = edge + tokens // LANES
    bias = keep + -(-biases // LANES)
    return edge, keep, bias, bias + 18


def pack_channels_kernel(width, marks, member_ref, values_ref, small_ref, even_first, odd_first, even_second, odd_second, rows):
    rest = sizes(width)[1]
    per_tile = LANES // rest
    count = values_ref.shape[0]
    tokens = pl.ds(0, count)
    edge, keep, bias, end = marks
    assert end <= SMALL
    for i in range(edge):
        rows[pl.ds(i, 1), :] = small_ref[pl.ds(0, 1), pl.ds(i * LANES, LANES)]
    for i in range(edge, keep):
        rows[pl.ds(i, 1), :] = small_ref[pl.ds(1, 1), pl.ds((i - edge) * LANES, LANES)]
    for i in range(keep, bias):
        rows[pl.ds(i, 1), :] = small_ref[pl.ds(2, 1), pl.ds((i - keep) * LANES, LANES)]
    for i in range(end, SMALL):
        rows[pl.ds(i, 1), :] = jnp.zeros((1, LANES), F32)
    fold = LANES // rest
    folded = pl.ds(count, count // fold)
    lane = lane_index((count // fold, LANES))
    for out in (even_second, odd_second):
        out[:, pl.ds(count, TAIL), :] = jnp.zeros((4, TAIL, LANES), BF16)
    for p in range(MEMBERS):
        first, second = ((even_first, even_second), (odd_first, odd_second))[p % 2]
        to = member_ref[0] ^ p
        for tile, out in enumerate((first, second)):
            start = pl.multiple_of((tile * MEMBERS + to) * LANES, LANES)
            out[p // 2, tokens, pl.ds(0, LANES)] = values_ref[:, pl.ds(start, LANES)]
        start = pl.multiple_of((2 * MEMBERS + to // per_tile) * LANES, LANES)
        part = values_ref[:, pl.ds(start, LANES)].astype(F32)
        total = jnp.zeros((count // fold, LANES), F32)
        for g in range(fold):
            group = pltpu.roll(part[g * (count // fold) : (g + 1) * (count // fold)], lax.rem(LANES + (g - to % per_tile) * rest, LANES), 1)
            total = jnp.where((lane >= g * rest) & (lane < (g + 1) * rest), group, total)
        first[p // 2, folded, :] = total.astype(BF16)
        at = bias
        for vector in (3, 4):
            for tile in range(3):
                start = (tile * MEMBERS + to) * LANES if tile < 2 else (2 * MEMBERS + to // per_tile) * LANES
                value = small_ref[pl.ds(vector, 1), pl.ds(pl.multiple_of(start, LANES), LANES)]
                if tile == 2:
                    value = pltpu.roll(value, lax.rem(LANES - (to % per_tile) * rest, LANES), 1)
                for _ in range(3):
                    piece = value.astype(BF16).astype(F32)
                    rows[pl.ds(at, 1), :] = piece
                    value = value - piece
                    at += 1
        first[p // 2, pl.ds(count + count // fold, SMALL), :] = rows[...].astype(BF16)


def pack_channels(values, small, marks, member, *others):
    rows, width = values.shape
    folded = rows * sizes(width)[1] // LANES
    first = jax.ShapeDtypeStruct((4, rows + folded + SMALL, LANES), BF16)
    second = jax.ShapeDtypeStruct((4, rows + TAIL, LANES), BF16)
    return pl.pallas_call(
        waiting(functools.partial(pack_channels_kernel, width, marks), 3, others),
        out_shape=(first, first, second, second),
        in_specs=[pl.BlockSpec(memory_space=pltpu.SMEM)] + in_vmem(2) + unseen(others),
        out_specs=tuple(in_vmem(4)),
        scratch_shapes=[pltpu.VMEM((SMALL, LANES), F32)],
        compiler_params=params(),
        name="pack_channels",
    )(member, values, small, *others)


def place_channels_kernel(width, member_ref, *refs):
    rest = sizes(width)[1]
    out_ref = refs[8]
    rows, _ = out_ref.shape
    per_tile = LANES // rest
    lane = lane_index((rows, LANES))
    for p in range(MEMBERS):
        source = member_ref[0] ^ p
        for tile in range(2):
            block_ref = refs[4 * tile + p // 2]
            start = pl.multiple_of((tile * MEMBERS + source) * LANES, LANES)
            out_ref[:, pl.ds(start, LANES)] = block_ref[p % 2, :, pl.ds(0, LANES)]
        start = pl.multiple_of((2 * MEMBERS + source // per_tile) * LANES, LANES)
        first = (source % per_tile) * rest
        part = pltpu.roll(refs[p // 2][p % 2, :, pl.ds(LANES, LANES)].astype(F32), first, 1)
        inside = (lane >= first) & (lane < first + rest)
        old = out_ref[:, pl.ds(start, LANES)].astype(F32)
        out_ref[:, pl.ds(start, LANES)] = jnp.where(inside, part, old).astype(BF16)


def place_channels(pairs, member, width):
    return pl.pallas_call(
        functools.partial(place_channels_kernel, width),
        out_shape=jax.ShapeDtypeStruct((pairs[0].shape[1], width), BF16),
        in_specs=[pl.BlockSpec(memory_space=pltpu.SMEM)] + in_vmem(8),
        out_specs=pl.BlockSpec(memory_space=pltpu.VMEM),
        compiler_params=params(),
        name="place_channels",
    )(member, *pairs)


UNROLL = 16


def token_loop(low, high, token, state, reverse):
    def several(i, state):
        for j in range(UNROLL):
            k = high - 1 - (i * UNROLL + j) if reverse else low + i * UNROLL + j
            state = token(k, state)
        return state

    return lax.fori_loop(0, (high - low) // UNROLL, several, state)


def row_block(rows):
    for block in (176, 48, 16):
        if rows % block == 0:
            return block
    return rows


def forward_kernel(tiles, rest, half_steps, *refs):
    gather = half_steps > 0
    x_refs, refs = (refs[:10], refs[10:]) if gather else (refs[:1], refs[1:])
    edge_ref, w_ref, bias_ref, keep_ref, cot_ref, *refs = refs
    if tiles == 2:
        folded_ref, *refs = refs
    act_ref, sum_ref, *refs = refs
    if gather:
        all_ref, *refs = refs
    both, cot_f32, carry, before = refs
    step = pl.program_id(0)
    block = act_ref.shape[0]
    rows = MEMBERS * block
    half = w_ref.shape[1] // 2
    count = half // LANES
    lane = lane_index((MEMBERS, LANES))

    if gather:
        for p in range(6):
            all_ref[p] = x_refs[p][...]

        @pl.when(step < half_steps)
        def _():
            all_ref[6] = x_refs[6][...]
            all_ref[7] = x_refs[7][...]

        @pl.when(step >= half_steps)
        def _():
            all_ref[6] = x_refs[8][...]
            all_ref[7] = x_refs[9][...]

        x = all_ref[...].reshape(rows, all_ref.shape[2])
    else:
        x = x_refs[0][...].reshape(rows, x_refs[0].shape[2])
    result = dot_f32(x, w_ref[...], ((1,), (0,)))
    for i in range(2 * count):
        both[i] = result[:, i * LANES : (i + 1) * LANES]
    cot_f32[0] = cot_ref[...].reshape(rows, LANES).astype(F32)
    if tiles == 2:
        folded = folded_ref[...].reshape(rows, LANES).astype(F32)
        cot_f32[1] = pltpu.roll(folded, lax.rem(LANES - step * rest, LANES), 1)

    @pl.when(step == 0)
    def _():
        for tile in range(tiles):
            carry[3 * tile] = jnp.ones((MEMBERS, LANES), F32)
            carry[3 * tile + 1] = jnp.zeros((MEMBERS, LANES), F32)
            carry[3 * tile + 2] = jnp.zeros((MEMBERS, LANES), F32)
        edges = dot_f32(edge_ref[...], w_ref[:, pl.ds(half, half)], ((1,), (0,)))
        for i in range(count):
            before[i] = edges[:MEMBERS, i * LANES : (i + 1) * LANES]

    def token(k, state):
        sums, earlier = state
        rows_at = pl.ds(k, MEMBERS, stride=block)
        keep = keep_ref[k]
        later = tuple(both[count + i, rows_at, :] for i in range(count))
        gates = [
            both[i, rows_at, :] + keep * earlier[i] + bias_ref[:, pl.ds(i * LANES, LANES)]
            for i in range(count)
        ]
        new = []
        outs = []
        for tile in range(tiles):
            if tile == 0:
                z = jnp.tanh(gates[0])
                u = 1.0 / (1.0 + jnp.exp(gates[1] + FORGET_SHIFT))
                o = 1.0 / (1.0 + jnp.exp(-gates[2]))
                outs += [z, u, o]
            else:
                mixed = gates[3]
                z = jnp.tanh(mixed)
                s = 1.0 / (1.0 + jnp.exp(jnp.where(lane < 2 * rest, mixed + FORGET_SHIFT, -mixed)))
                outs += [jnp.where(lane < rest, z, s)]
                u = pltpu.roll(s, LANES - rest, 1)
                o = pltpu.roll(s, LANES - 2 * rest, 1)
            a = keep * (1.0 - u)
            total, local, back = sums[3 * tile : 3 * tile + 3]
            cot = cot_f32[tile, rows_at, :]
            total = total * a
            new += [total, a * local + u * z, back + total * (cot * o)]
        for i, value in enumerate(outs):
            act_ref[k, :, pl.ds(i * LANES, LANES)] = value
        return tuple(new), later

    start = (tuple(carry[i] for i in range(3 * tiles)), tuple(before[i] for i in range(count)))
    sums, earlier = token_loop(0, block, token, start, False)
    for i in range(3 * tiles):
        carry[i] = sums[i]
        sum_ref[i] = sums[i]
    for i in range(count):
        before[i] = earlier[i]


def forward(pieces, edges, w, bias, keep, cot, tiles, rest, *others):
    gather = len(pieces) > 1
    width = w.shape[0]
    length = keep.shape[0]
    tokens = length - TAIL
    block = tokens // 4
    half = w.shape[1] // 2
    assert LANES // rest == 4
    cot_specs = [pl.BlockSpec((MEMBERS, block, LANES), lambda i: (0, i, 0))]
    if tiles == 2:
        cot_specs += [pl.BlockSpec((MEMBERS, block, LANES), lambda i: (0, 4, 0))]
    if gather:
        x_specs = [pl.BlockSpec((block, width), lambda i: (i, 0))] * 6
        x_specs += [pl.BlockSpec((block, width), lambda i: (jnp.minimum(i, 1), 0))] * 2
        x_specs += [pl.BlockSpec((block, width), lambda i: (jnp.maximum(i - 2, 0), 0))] * 2
    else:
        x_specs = [pl.BlockSpec((MEMBERS, block, width), lambda i: (0, i, 0))]
    whole = [jax.ShapeDtypeStruct((MEMBERS, length, width), BF16)] if gather else []
    return pl.pallas_call(
        waiting(
            functools.partial(forward_kernel, tiles, rest, 2 if gather else 0), len(pieces) + 4 + tiles, others
        ),
        grid=(4,),
        out_shape=(
            jax.ShapeDtypeStruct((length, MEMBERS, half), F32),
            jax.ShapeDtypeStruct((3 * tiles, MEMBERS, LANES), F32),
            *whole,
        ),
        in_specs=[
            *x_specs,
            *in_vmem(3),
            pl.BlockSpec((block, MEMBERS, LANES), lambda i: (i, 0, 0)),
            *cot_specs,
            *unseen(others),
        ],
        out_specs=(
            pl.BlockSpec((block, MEMBERS, half), lambda i: (i, 0, 0)),
            pl.BlockSpec((3 * tiles, MEMBERS, LANES), lambda i: (0, 0, 0)),
            *[pl.BlockSpec((MEMBERS, block, width), lambda i: (0, i, 0)) for _ in whole],
        ),
        scratch_shapes=[
            pltpu.VMEM((2 * half // LANES, MEMBERS * block, LANES), F32),
            pltpu.VMEM((tiles, MEMBERS * block, LANES), F32),
            pltpu.VMEM((3 * tiles, MEMBERS, LANES), F32),
            pltpu.VMEM((half // LANES, MEMBERS, LANES), F32),
        ],
        compiler_params=params(),
        name="forward",
    )(*pieces, edges, w, bias, keep, *[cot] * tiles, *others)


def backward_kernel(
    tiles, rest, blocks, act_ref, keep_ref, enter_ref, arrive_ref, final_ref, cot_ref, folded_ref,
    even_ref, odd_ref, grads_ref, bias_ref, edge_ref, memory, cot_f32, wide, hold, carry, after, unfolded=None,
):
    step = pl.program_id(0)
    block = act_ref.shape[0]
    half = act_ref.shape[2]
    rows = MEMBERS * block
    lane = lane_index((MEMBERS, LANES))
    which = jnp.where(step < blocks, step, 2 * blocks - 1 - step)
    base = which * block
    cot_f32[...] = cot_ref[...].reshape(rows, LANES).astype(F32)
    count = half // LANES
    top = jnp.where(which == blocks - 1, block - TAIL, block)

    def values(k, tile):
        at = lambda i: act_ref[k, :, pl.ds(i * LANES, LANES)]
        if tile == 0:
            return at(0), at(1), at(2)
        mixed = at(3)
        return mixed, pltpu.roll(mixed, LANES - rest, 1), pltpu.roll(mixed, LANES - 2 * rest, 1)

    if tiles == 2:
        long, short = unfolded.shape[0] // MEMBERS, folded_ref.shape[1]

        @pl.when(step == 0)
        def _():
            for p in range(MEMBERS):
                folded = folded_ref[p].astype(F32)
                for g in range(LANES // rest):
                    part = pltpu.roll(folded, LANES - g * rest, 1) if g else folded
                    unfolded[pl.ds(p * long + g * short, short), :] = part

    @pl.when(step == 0)
    def _():
        for tile in range(tiles):
            memory[0, tile] = enter_ref[tile]
            carry[tile] = enter_ref[tile]

    @pl.when(step < blocks)
    def _():
        def token(k, state):
            keep = keep_ref[k]
            new = []
            for tile in range(tiles):
                z, u, o = values(k, tile)
                m = keep * (1.0 - u) * state[tile] + u * z
                memory[base + k + 1, tile] = m
                hold[tile, pl.ds(k, MEMBERS, stride=block), :] = o * m
                new.append(m)
            return tuple(new)

        state = token_loop(0, top, token, tuple(carry[t] for t in range(tiles)), False)
        for tile in range(tiles):
            carry[tile] = state[tile]

        @pl.when(which == blocks - 1)
        def _():
            for tile in range(tiles):
                rest_of = final_ref[tile]
                for row in range(3):
                    part = rest_of.astype(BF16).astype(F32)
                    hold[tile, pl.ds(block - TAIL + row, MEMBERS, stride=block), :] = part
                    rest_of = rest_of - part
                for row in range(3, TAIL):
                    hold[tile, pl.ds(block - TAIL + row, MEMBERS, stride=block), :] = jnp.zeros_like(part)

        for tile in range(tiles):
            for p in range(MEMBERS):
                part = hold[tile, pl.ds(p * block, block), :].astype(BF16)
                (even_ref, odd_ref)[p % 2][p // 2, :, pl.ds(tile * LANES, LANES)] = part

    @pl.when(step == blocks)
    def _():
        for tile in range(tiles):
            carry[tile] = arrive_ref[tile]
        after[...] = jnp.zeros_like(after)
        bias_ref[...] = jnp.zeros_like(bias_ref)

    @pl.when(step >= blocks)
    def _():
        def token(k, state):
            arriving, shifted, totals = state
            rows_at = pl.ds(k, MEMBERS, stride=block)
            keep = keep_ref[k]
            new, parts = [], []
            for tile in range(tiles):
                z, u, o = values(k, tile)
                f = 1.0 - u
                if tile == 0:
                    cot = cot_f32[rows_at, :]
                else:
                    cot = unfolded[pl.ds(base + k, MEMBERS, stride=long), :]
                held = keep * memory[base + k, tile]
                m = memory[base + k + 1, tile]
                grad = cot * o
                adjoint = grad + arriving[tile]
                new.append(keep * f * adjoint)
                scaled = adjoint * u
                one = [scaled * (1.0 - z * z), scaled * (held - z) * f, grad * m * (1.0 - o)]
                if tile == 1:
                    one = [
                        jnp.where(lane < rest, one[0], jnp.where(lane < 2 * rest, pltpu.roll(one[1], rest, 1), jnp.where(lane < 3 * rest, pltpu.roll(one[2], 2 * rest, 1), 0.0)))
                    ]
                parts += one
            for i, part in enumerate(parts):
                wide[i, rows_at, :] = part
                wide[count + i, rows_at, :] = shifted[i]
            return tuple(new), tuple(keep * part for part in parts), tuple(t + p for t, p in zip(totals, parts))

        state = (
            tuple(carry[t] for t in range(tiles)),
            tuple(after[i] for i in range(count)),
            tuple(bias_ref[:, pl.ds(i * LANES, LANES)] for i in range(count)),
        )
        arriving, shifted, totals = token_loop(0, top, token, state, True)
        for tile in range(tiles):
            carry[tile] = arriving[tile]
        for i in range(count):
            after[i] = shifted[i]
            edge_ref[:, pl.ds(i * LANES, LANES)] = shifted[i]
            bias_ref[:, pl.ds(i * LANES, LANES)] = totals[i]

        @pl.when(which == blocks - 1)
        def _():
            for row in range(block - TAIL, block):
                for i in range(2 * count):
                    wide[i, pl.ds(row, MEMBERS, stride=block), :] = jnp.zeros((MEMBERS, LANES), F32)

        for i in range(2 * count):
            grads_ref[:, :, pl.ds(i * LANES, LANES)] = wide[i].astype(BF16).reshape(MEMBERS, block, LANES)


def backward(act, keep, cot, enter, arrive, final, tiles, rest, *others):
    length, members, half = act.shape
    block = row_block(length)
    blocks = length // block
    lanes = tiles * LANES
    turn = lambda i: jnp.where(i < blocks, i, 2 * blocks - 1 - i)
    return pl.pallas_call(
        waiting(functools.partial(backward_kernel, tiles, rest, blocks), 7, others),
        grid=(2 * blocks,),
        out_shape=(
            jax.ShapeDtypeStruct((members // 2, length, lanes), BF16),
            jax.ShapeDtypeStruct((members // 2, length, lanes), BF16),
            jax.ShapeDtypeStruct((members, length, 2 * half), BF16),
            jax.ShapeDtypeStruct((members, half), F32),
            jax.ShapeDtypeStruct((members, half), F32),
        ),
        in_specs=[
            pl.BlockSpec((block, members, half), lambda i: (turn(i), 0, 0)),
            pl.BlockSpec((block, members, LANES), lambda i: (turn(i), 0, 0)),
            *in_vmem(3),
            pl.BlockSpec((members, block, LANES), lambda i: (0, turn(i), 0)),
            pl.BlockSpec((members, (length - TAIL) // 4, LANES), lambda i: (0, 4 if tiles == 2 else 0, 0)),
            *unseen(others),
        ],
        out_specs=(
            pl.BlockSpec((members // 2, block, lanes), lambda i: (0, jnp.minimum(i, blocks - 1), 0)),
            pl.BlockSpec((members // 2, block, lanes), lambda i: (0, jnp.minimum(i, blocks - 1), 0)),
            pl.BlockSpec((members, block, 2 * half), lambda i: (0, jnp.minimum(2 * blocks - 1 - i, blocks - 1), 0)),
            pl.BlockSpec((members, half), lambda i: (0, 0)),
            pl.BlockSpec((members, half), lambda i: (0, 0)),
        ),
        scratch_shapes=[
            pltpu.VMEM((length, tiles, members, LANES), F32),
            pltpu.VMEM((members * block, LANES), F32),
            pltpu.VMEM((2 * half // LANES, members * block, LANES), F32),
            pltpu.VMEM((tiles, members * block, LANES), F32),
            pltpu.VMEM((tiles, members, LANES), F32),
            pltpu.VMEM((half // LANES, members, LANES), F32),
            *[pltpu.VMEM((members * (length - TAIL), LANES), F32) for _ in range(tiles - 1)],
        ],
        compiler_params=params(),
        name="backward",
    )(act, keep, enter, arrive, final, cot, cot, *others)


def input_gradient_kernel(first_ref, second_ref, w_first, w_second, even_ref, odd_ref):
    for p, out in enumerate((even_ref, odd_ref)):
        out[0] = (
            dot_f32(first_ref[p], w_first[...], ((1,), (1,)))
            + dot_f32(second_ref[p], w_second[...], ((1,), (1,)))
        ).astype(BF16)


def input_gradients(first, second, w_first, w_second, start, count, *others):
    _, length, _ = first.shape
    width = w_first.shape[0]
    shape = jax.ShapeDtypeStruct((count, length, width), BF16)
    return pl.pallas_call(
        waiting(input_gradient_kernel, 4, others),
        grid=(count,),
        out_shape=(shape, shape),
        in_specs=[
            pl.BlockSpec((2, length, first.shape[2]), lambda i: (start + i, 0, 0)),
            pl.BlockSpec((2, length, second.shape[2]), lambda i: (start + i, 0, 0)),
            *in_vmem(2),
            *unseen(others),
        ],
        out_specs=(pl.BlockSpec((1, length, width), lambda i: (i, 0, 0)),) * 2,
        compiler_params=params(),
        name="input_gradient",
    )(first, second, w_first, w_second, *others)


def far_sum_kernel(even_ref, odd_ref, low_ref, high_ref):
    total = even_ref[0].astype(F32) + odd_ref[0].astype(F32)
    middle = low_ref.shape[0]
    low_ref[...] = total[:middle].astype(BF16)
    high_ref[...] = total[middle:].astype(BF16)


def far_sum(even, odd, middle):
    _, length, width = even.shape
    block = 384
    sums = [jax.ShapeDtypeStruct((rows, width), BF16) for rows in (middle, length - middle)]
    spec = pl.BlockSpec((1, length, block), lambda i: (0, 0, i))
    return pl.pallas_call(
        far_sum_kernel,
        grid=(width // block,),
        out_shape=sums,
        in_specs=[spec, spec],
        out_specs=[pl.BlockSpec((rows, block), lambda i: (0, i)) for rows in (middle, length - middle)],
        compiler_params=params(),
        name="far_sum",
    )(even, odd)


def near_sums_kernel(even_ref, odd_ref, low_ref, high_ref, to_y, to_x):
    middle = low_ref.shape[0]
    total = even_ref[0].astype(F32) + odd_ref[0].astype(F32)
    to_y[pl.ds(0, middle), :] = (total[:middle] + low_ref[...].astype(F32)).astype(BF16)
    to_y[pl.ds(middle, high_ref.shape[0]), :] = total[middle:].astype(BF16)
    total = even_ref[1].astype(F32) + odd_ref[1].astype(F32)
    to_x[pl.ds(0, middle), :] = total[:middle].astype(BF16)
    to_x[pl.ds(middle, high_ref.shape[0]), :] = (total[middle:] + high_ref[...].astype(F32)).astype(BF16)


def near_sums(even, odd, low, high):
    _, length, width = even.shape
    block = 384
    spec = pl.BlockSpec((2, length, block), lambda i: (0, 0, i))
    out = pl.BlockSpec((length, block), lambda i: (0, i))
    return pl.pallas_call(
        near_sums_kernel,
        grid=(width // block,),
        out_shape=[jax.ShapeDtypeStruct((length, width), BF16)] * 2,
        in_specs=[spec, spec] + [pl.BlockSpec((part.shape[0], block), lambda i: (0, i)) for part in (low, high)],
        out_specs=[out, out],
        compiler_params=params(),
        name="near_sums",
    )(even, odd, low, high)


def adamw(master, gradient, moment_one, moment_two, rate):
    moment_one = BETA_ONE * moment_one + (1.0 - BETA_ONE) * gradient
    moment_two = BETA_TWO * moment_two + (1.0 - BETA_TWO) * gradient * gradient
    step_size = (
        moment_one
        / (1.0 - BETA_ONE**STEP)
        / (jnp.sqrt(moment_two / (1.0 - BETA_TWO**STEP)) + EPSILON)
    )
    return (master - rate * (step_size + DECAY_RATE * master), moment_one, moment_two)


def channel_tiles(vector, member, rest):
    width = vector.shape[-1]
    axis = vector.ndim - 1
    pieces = [
        lax.dynamic_slice_in_dim(vector, member * LANES, LANES, axis),
        lax.dynamic_slice_in_dim(vector, (MEMBERS + member) * LANES, LANES, axis),
        lax.dynamic_slice_in_dim(vector, 2 * MEMBERS * LANES + member * rest, rest, axis),
    ]
    return pieces


def widen(part):
    return jnp.pad(part, [(0, 0)] * (part.ndim - 1) + [(0, LANES - part.shape[-1])])


def on_device(
    inputs,
    boundary,
    start_state,
    weight,
    gate_bias,
    first_weight,
    second_weight,
    first_bias,
    second_bias,
    cotangent,
    final_cotangent,
):
    here = Place()
    tokens, width = inputs.shape[1:]
    rest = sizes(width)[1]
    member = here.member.astype(jnp.int32).reshape(1)
    taps, own_rows, columns = weight.shape
    length = tokens + TAIL
    deep_groups = [[lo + 2 * h for h in range(here.depth)] for lo in range(2)]
    wide_groups = [[jl + 4 * h for h in range(here.wide)] for jl in range(4)]

    weight_pairs = here.pair_up(*pack_weight(weight, member))
    weight_got = here.send_pairs(weight_pairs)

    def all_rows(part):
        cols = part.shape[-1]
        if here.wide > 1:
            part = lax.all_gather(part, "stream", axis=0, axis_index_groups=wide_groups)
            part = part.reshape(here.wide, 2, 4 * own_rows, cols).swapaxes(0, 1)
        part = part.reshape(-1, cols)
        return lax.all_gather(part, "seq", axis=0, tiled=True, axis_index_groups=deep_groups)

    own_bias = gate_bias.shape[0]
    marks = small_rows(width, tokens, own_bias)
    pad_to = lambda row: jnp.pad(row.astype(F32).reshape(1, -1), ((0, 0), (0, width - row.size)))
    small = [inputs[0, -1:].astype(F32), pad_to(1 - boundary[0]), pad_to(gate_bias.astype(BF16))]
    small = jnp.concatenate(small + [start_state, final_cotangent])

    own = inputs[0]
    own_copy = copied(own)
    packed_cot = pack_channels(cotangent[0], small, marks, member, own_copy, weight_pairs[3])
    cot_first, cot_second = here.pair_up(*packed_cot[:2]), here.pair_up(*packed_cot[2:])
    got_first = here.send_pairs(cot_first)
    placed = place_weight(weight_got, member, 8 * LANES, *cot_first[1:])
    weights = [all_rows(part) for part in placed]
    own_sibling = here.flip(own, 1)
    sent = after(own_copy, *placed, *got_first[1:])
    middle = (tokens // 32) * 16
    from_y = here.flip(sent, here.member_mask(2))
    from_x = here.flip(sent, here.member_mask(4))
    low_part, high_part = from_y[:middle], from_x[middle:]
    both_low = here.flip(low_part, here.member_mask(4))
    both_high = here.flip(high_part, here.member_mask(2))
    y_sibling, x_sibling = here.flip(from_y, 1), here.flip(from_x, 1)
    cots = [jnp.concatenate(got_first, axis=0)]
    pieces = [own, own_sibling, from_y, y_sibling, from_x, x_sibling]
    pieces += [both_low, here.flip(both_low, 1), both_high, here.flip(both_high, 1)]

    smalls = cots[0][:, tokens + tokens * rest // LANES :].astype(F32)
    lower = ((jnp.arange(MEMBERS) >> 2) ^ (here.seq % 2)) == 0
    lasts = smalls[:, : marks[0]].reshape(MEMBERS, width).astype(BF16)
    plane = 2 * here.n_stream
    behind = lax.ppermute(lasts, AXES, [(n, n + plane) for n in range(here.count - plane)])
    swap = lambda rows: jnp.concatenate([rows[4:], rows[:4]], axis=0)
    edges = jnp.where(lower[:, None], swap(behind), swap(lasts))
    edges = jnp.pad(edges, ((0, TAIL - MEMBERS), (0, 0)))
    keep = smalls[:, marks[0] : marks[1]].reshape(MEMBERS, tokens).T
    keep = jnp.pad(keep, ((0, TAIL), (0, 0)))
    keep = jnp.broadcast_to(keep[:, :, None], (length, MEMBERS, LANES))
    states = jnp.sum(smalls[:, marks[2] : marks[3]].reshape(MEMBERS, 2, 3, 3, LANES), axis=3)
    starts, finals = ([states[:, i, tile] for tile in range(3)] for i in range(2))
    all_bits = [1 << b for b in range(here.count.bit_length() - 1)]
    bias_all = smalls[:, marks[1] : marks[2]].reshape(1, MEMBERS, -1)[:, :, :own_bias].astype(BF16)
    bias_all = here.gather_flips(bias_all, here.deep_bits + here.wide_bits).astype(F32)
    bias_all = bias_all.reshape(here.wide, here.depth, MEMBERS, own_bias)
    every_member = here.member ^ jnp.arange(MEMBERS)
    bias_all = jnp.take(bias_all, (here.stream // 4) ^ jnp.arange(here.wide), axis=0)
    bias_all = jnp.take(bias_all, here.high ^ jnp.arange(here.depth), axis=1)
    bias_all = jnp.take(bias_all, every_member, axis=2)
    bias_all = bias_all.reshape(here.wide, here.depth, 2, 4, own_bias).transpose(1, 2, 0, 3, 4).reshape(3, width)
    bias_parts = channel_tiles(bias_all, here.member, rest)
    biases = [
        jnp.concatenate([bias_parts[0].reshape(1, 3 * LANES), widen(bias_parts[2].reshape(1, 3 * rest))], axis=1),
        bias_parts[1].reshape(1, 3 * LANES),
    ]

    def both_halves(value):
        other = jnp.concatenate([value[4:], value[:4]], axis=0)
        mask = lower[:, None]
        return jnp.where(mask, value, other), jnp.where(mask, other, value)

    def back_pairs(first, second, start, count, *others):
        even, odd = input_gradients(first, second, weights[0], weights[1], start, count, *others)
        return even, here.flip(odd, 1)

    halfway = (length // 32) * 16
    gradients, outs, hidden_got = [], [], []
    for chunk in range(2):
        tiles = 2 - chunk
        others = (outs[0][4],) if chunk else ()
        source = [x_all] if chunk else pieces
        act, summary, *whole = forward(source, edges, weights[chunk], biases[chunk], keep, cots[chunk], tiles, rest, *others)
        if whole:
            got_second = here.send_pairs([after(pair, summary) for pair in cot_second])
            cots.append(jnp.concatenate(got_second, axis=0))
            behind = jnp.pad(edges[:MEMBERS, None], ((0, 0), (0, TAIL - 1), (0, 0)))
            x_all = lax.dynamic_update_slice(whole[0], behind, (0, tokens, 0))
        every = here.gather_flips(summary[None], here.deep_bits)
        enters, arrives, ends = [], [], []
        for tile in range(tiles):
            where = (0, 2, 1)[2 * chunk + tile]
            state, back = starts[where], finals[where]
            enter, arrive = state, back
            for z in range(here.depth):
                part = jnp.take(every, z ^ here.high, axis=0)
                a_low, a_high = both_halves(part[3 * tile])
                b_low, b_high = both_halves(part[3 * tile + 1])
                between = a_low * state + b_low
                enter = jnp.where(z == here.high, jnp.where(lower[:, None], state, between), enter)
                state = a_high * between + b_high
            for z in reversed(range(here.depth)):
                part = jnp.take(every, z ^ here.high, axis=0)
                a_low, a_high = both_halves(part[3 * tile])
                c_low, c_high = both_halves(part[3 * tile + 2])
                between = a_high * back + c_high
                arrive = jnp.where(z == here.high, jnp.where(lower[:, None], between, back), arrive)
                back = a_low * between + c_low
            enters.append(enter)
            arrives.append(arrive)
            ends.append(state)
        others = () if chunk else (weights[1], cots[1])
        even, odd, grads, bias_grad, edge_grad = backward(
            act, keep, cots[chunk], jnp.stack(enters), jnp.stack(arrives), jnp.stack(ends), tiles, rest, *others
        )
        half = edge_grad.shape[1]
        edge_grad = jnp.pad(edge_grad.astype(BF16)[:, None], ((0, 0), (0, TAIL - 1), (half, 0)))
        grads = lax.dynamic_update_slice(grads, edge_grad, (0, tokens, 0))
        hidden_pairs = here.pair_up(even, odd)
        hidden_got += here.send_pairs(hidden_pairs)
        if chunk == 1:
            far_low, far_high = far_sum(*back_pairs(outs[0][2], grads, 3, 1, *hidden_got[1:4]), halfway)
            grads = after(grads, far_low, gradients[0])
        flat = grads.reshape(MEMBERS * length, -1)
        local = dot_f32(x_all.reshape(MEMBERS * length, width), flat, ((0,), (0,))).astype(BF16)
        cols = local.shape[-1]
        ordered = after(local, gradients[0]) if gradients else local
        summed = lax.psum_scatter(ordered, "seq", scatter_dimension=0, tiled=True, axis_index_groups=deep_groups)
        if here.wide > 1:
            summed = summed.reshape(2, here.wide, 4 * own_rows, cols).swapaxes(0, 1).reshape(-1, cols)
            summed = lax.psum_scatter(summed, "stream", scatter_dimension=0, tiled=True, axis_index_groups=wide_groups)
        gradients.append(summed.reshape(MEMBERS, own_rows, cols))
        outs.append((even, odd, grads, jnp.sum(bias_grad, axis=0), local))

    hidden_own = place_channels(hidden_got, member, width)
    hidden = hidden_own[None, :tokens]
    whole_final = jnp.sum(hidden_own[tokens : tokens + 3].astype(F32), axis=0, keepdims=True)
    own_columns = width // here.n_seq
    final_state = lax.dynamic_slice_in_dim(whole_final, here.seq * own_columns, own_columns, 1)

    low_half = here.flip(far_low, here.member_mask(4))
    high_half = here.flip(far_high, here.member_mask(2))
    grads = outs[0][2], outs[1][2]
    even, odd = back_pairs(*grads, 1, 2, low_half, high_half, outs[1][4], *hidden_got[5:])
    to_y, to_x = near_sums(even, odd, low_half, high_half)
    got_y = here.flip(to_y, here.member_mask(2))
    got_x = here.flip(to_x, here.member_mask(4))
    even, odd = back_pairs(*grads, 0, 1, to_y, to_x)
    gradients = [after(gradient, even, got_y, got_x) for gradient in gradients]
    add_up = lambda rows: sum(part[rows].astype(F32) for part in (even[0], odd[0], got_y, got_x))
    from_next = lax.ppermute(
        add_up(slice(tokens, tokens + 1)), "seq", [(i + 1, i) for i in range(here.n_seq - 1)]
    )
    last = lax.broadcasted_iota(jnp.int32, (tokens, 1), 0) == tokens - 1
    input_gradient = (add_up(slice(0, tokens)) + jnp.where(last, from_next, 0.0)).astype(BF16)[None]

    squares = sum(jnp.sum(jnp.square(g.astype(F32))) for g in gradients)
    vector = jnp.concatenate([outs[0][3], outs[1][3], jnp.broadcast_to(squares, (LANES,))]).reshape(1, -1)
    vector = here.sum_flips(vector, here.deep_bits + here.wide_bits)
    vectors = here.gather_flips(vector, here.group_bits)
    bias_every = jnp.take(vectors[:, :-LANES], every_member, axis=0)
    gradient_norm = jnp.sqrt(jnp.sum(vectors[:, -1]) + jnp.sum(jnp.square(vectors[:, :-LANES])))
    tile_a = bias_every[:, : 3 * LANES].reshape(MEMBERS, 3, LANES)
    tile_b = bias_every[:, 4 * LANES : 7 * LANES].reshape(MEMBERS, 3, LANES)
    tile_c = bias_every[:, 3 * LANES : 3 * LANES + 3 * rest].reshape(MEMBERS, 3, rest)
    natural = jnp.concatenate([t.swapaxes(0, 1).reshape(3, -1) for t in (tile_a, tile_b, tile_c)], axis=1)
    bias_raw = lax.dynamic_slice_in_dim(natural.reshape(-1), here.linear * own_bias, own_bias, 0)

    clip_factor = jnp.minimum(1.0, CLIP_NORM / (gradient_norm + 1e-06))
    received = here.exchange(*pick_rows(*gradients, member))
    raw = place_gradient(received, member, weight.shape)
    weight_gradient = clip_factor * raw
    bias_gradient = clip_factor * bias_raw
    new_weight, new_first_weight, new_second_weight = adamw(
        weight, weight_gradient, first_weight, second_weight, RATE_WEIGHT
    )
    new_bias, new_first_bias, new_second_bias = adamw(
        gate_bias, bias_gradient, first_bias, second_bias, RATE_BIAS
    )
    return (
        hidden,
        final_state,
        input_gradient,
        weight_gradient,
        bias_gradient,
        gradient_norm,
        new_weight,
        new_first_weight,
        new_second_weight,
        new_bias,
        new_first_bias,
        new_second_bias,
    )


def solution(mesh):
    placed = (
        P("stream", "seq", None),
        P("stream", "seq"),
        P("stream", None),
        P(None, ("seq", "stream"), None),
        P(("seq", "stream")),
        P(None, ("seq", "stream"), None),
        P(None, ("seq", "stream"), None),
        P(("seq", "stream")),
        P(("seq", "stream")),
        P("stream", "seq", None),
        P("stream", None),
    )
    return jax.shard_map(
        on_device,
        mesh=mesh,
        in_specs=placed,
        out_specs=(
            P("stream", "seq", None),
            P("stream", "seq"),
            P("stream", "seq", None),
            P(None, ("seq", "stream"), None),
            P(("seq", "stream")),
            P(),
            P(None, ("seq", "stream"), None),
            P(None, ("seq", "stream"), None),
            P(None, ("seq", "stream"), None),
            P(("seq", "stream")),
            P(("seq", "stream")),
            P(("seq", "stream")),
        ),
        check_vma=False,
    )
```

time: 886 us -> 603 us (0.68)
  waiting for transfers between devices: 270 us -> 182 us
  Pallas kernels: 292 us -> 210 us
  matrix products: 107 us -> 50.5 us
  local copies, waits for them, and re-layouts: 83.8 us -> 32.7 us
  other arithmetic: 57.7 us -> 48.6 us
    ppermute x47 -> x51, waiting for transfers between devices: 270 us -> 181 us  [flip(): return lax.ppermute(block, AXES, [(n, n ^ mask) for n in range(self.count)])]
    pallas_call x7 -> x22, Pallas kernels: 280 us -> 198 us  [the longest x2 75.7 us: forward(): pl.pallas_call(waiting(functools.partial(forward_kernel, tiles, rest, 2 i...]
    dot_general x4 -> x2, matrix products: 107 us -> 50.5 us  [dot_f32(): return lax.dot_general(a, b, (dims, ((), ())), preferred_element_type=F32)]
    unnamed x70 -> x113, local copies, waits for them, and re-layouts: 28.3 us -> 7.22 us
    convert_element_type x6 -> x4, other arithmetic: 16.2 us -> 0.8 us  [the longest x1 0.78 us: on_device(): inputs[0, -1:].astype(F32)]
    squeeze x3 -> x0, local copies, waits for them, and re-layouts: 12.2 us -> none  [the longest x1 8.18 us: on_device(): even, odd = (back_all[:, 0], back_all[:, 1])]
    concatenate x5, local copies, waits for them, and re-layouts: 12.9 us -> 0.8 us  [the longest x1 0.69 us: on_device(): small = jnp.concatenate(small + [start_state, final_cotangent])]
    slice x17 -> x20, local copies, waits for them, and re-layouts: 22.6 us -> 13.3 us  [the longest x12 8.5 us: pair_up(): return [jnp.stack([even[i], sibling[i]]) for i in range(4)]]
  transfers between devices with their start and end apart: 53 -> 57, of which waited for: 23 -> 28; matrix products, arithmetic and copies ran while one was open for 27% -> 14% of each run, Pallas kernels for 23% -> 25%
where the time goes in v2:
time: 603 us; the launch traced here: 596 us
  Pallas kernels  210 us (35%)
  waiting for transfers between devices  182 us (30%)
  starting transfers between devices  54.3 us (9%)
  matrix products  50.5 us (8%)
  other arithmetic  48.6 us (8%)
  local copies, waits for them, and re-layouts  32.7 us (5%)
  between operations  19.1 us (3%)
    ppermute x51, waiting for transfers between devices, flip(): return lax.ppermute(block, AXES, [(n, n ^ mask) for n in range(self.count)])  181 us
    pallas_call x2, Pallas kernels, forward(): pl.pallas_call(waiting(functools.partial(forward_kernel, tiles, rest, 2 i...  75.7 us
    pallas_call x3, Pallas kernels, input_gradients(): pl.pallas_call(waiting(input_gradient_kernel, 4, others), grid=(count,),...  54.3 us
    dot_general x2, matrix products, dot_f32(): return lax.dot_general(a, b, (dims, ((), ())), preferred_element_type=F32)  50.5 us
    ppermute x51, starting transfers between devices, flip(): return lax.ppermute(block, AXES, [(n, n ^ mask) for n in range(self.count)])  50.2 us
    pallas_call x2, Pallas kernels, backward(): pl.pallas_call(waiting(functools.partial(backward_kernel, tiles, rest, bl...  40.7 us
    another operation x23, other arithmetic, pair_up(): return [jnp.stack([even[i], sibling[i]]) for i in range(4)]  14.3 us
  transfers between devices with their start and end apart: 57, of which 28 were waited for; matrix products, arithmetic and copies ran while one was open for 14% of the time, Pallas kernels for 25%

profile of v2, /device:TPU:0, one launch (start us, length us, event | category | flops | bytes accessed | tf_op | source)
XLA Modules:
  0.0 596.3 jit_solution(5575365684391286918)
XLA Ops:
  7.3 3.9 pack_weight.1
  11.7 4.0 copied.1.refs_3_.refs_0_
  22.2 3.6 pack_channels.1
  30.6 13.8 %collective-permute-done.2.refs_2_ = bf16[2,72,1792]{2,1,0:T(8,128)(2,1)} collective-permute-done((bf16[2,72,1792]{2,1,0:T(8,128)(2,1)}, bf16[2,72,1792]{2,1,0:T(8,128)(2,1)}, u32[]{:S(2)}, u32[]{:S(2)}) %collective-permute-start.2) | collective-permute-done | bytes 516128 | tf_op jit(solution)/shard_map/ppermute | solution.py:57
  56.0 4.6 collective-permute-done.6.refs_3_
  62.9 6.2 %collective-permute-done.8.refs_5_ = bf16[2,688,128]{2,1,0:T(8,128)(2,1)S(1)} collective-permute-done((bf16[2,688,128]{2,1,0:T(8,128)(2,1)S(1)}, bf16[2,688,128]{2,1,0:T(8,128)(2,1)S(1)}, u32[]{:S(2)}, u32[]{:S(2)}) %collective-permute-start.8) | collective-permute-done | bytes 352288 | tf_op jit(solution)/shard_map/ppermute | solution.py:57
  84.3 38.3 %collective-permute-done.11.refs_4_ = bf16[512,2304]{1,0:T(8,128)(2,1)} collective-permute-done((bf16[512,2304]{1,0:T(8,128)(2,1)}, bf16[512,2304]{1,0:T(8,128)(2,1)}, u32[]{:S(2)}, u32[]{:S(2)}) %collective-permute-start.11) | collective-permute-done | bytes 2359328 | tf_op jit(solution)/shard_map/ppermute | solution.py:57
  133.6 17.8 %collective-permute-done.15.refs_8_ = bf16[256,2304]{1,0:T(8,128)(2,1)} collective-permute-done((bf16[256,2304]{1,0:T(8,128)(2,1)}, bf16[256,2304]{1,0:T(8,128)(2,1)}, u32[]{:S(2)}, u32[]{:S(2)}) %collective-permute-start.15) | collective-permute-done | bytes 1179680 | tf_op jit(solution)/shard_map/ppermute | solution.py:57
  151.4 3.6 collective-permute-done.13.refs_6_
  160.1 45.4 %forward.2 = (f32[528,8,512]{2,1,0:T(8,128)}, f32[6,8,128]{2,1,0:T(8,128)}, bf16[8,528,2304]{2,1,0:T(8,128)(2,1)}) custom-call(bf16[512,2304]{1,0:T(8,128)(2,1)} %bitcast.190, bf16[512,2304]{1,0:T(8,128)(2,1)} %collective-permute-done.refs_1_, bf16[512,2304]{1,0:T(8,128)(2,1)} %collective-permute-done.9.refs_2_, ...), custom_call_target="tpu_custom_call" | custom-call | tf_op jit(solution)/shard_map/forward/pallas_call | solution.py:498
  224.6 25.9 %backward.2 = (bf16[4,528,256]{2,1,0:T(8,128)(2,1)}, bf16[4,528,256]{2,1,0:T(8,128)(2,1)}, bf16[8,528,1024]{2,1,0:T(8,128)(2,1)}, f32[8,512]{1,0:T(8,128)}, f32[8,512]{1,0:T(8,128)}) custom-call(f32[528,8,512]{2,1,0:T(8,128)} %get-tuple-element.55.refs_0_, f32[528,8,128]{2,1,0:T(8,128)} %broadcast_in_dim.549.refs_13_.refs_1_.refs_4_, ...), custom_call_target="tpu_custom_call" | custom-call | tf_op jit(solution)/shard_map/backward/pallas_call | solution.py:670
  252.0 28.0 %bitcast_convert_fusion.refs_6_ = bf16[2304,1024]{1,0:T(8,128)(2,1)} fusion(bf16[8,528,2304]{2,1,0:T(8,128)(2,1)} %pad_dynamic-update-slice_fusion.refs_0_, bf16[8,528,1024]{2,1,0:T(8,128)(2,1)} %pad_dynamic-update-slice_fusion.1.refs_0_), kind=kOutput, calls=%fused_computation.3 | convolution fusion | flops 19933691904 | bytes 32833536 | tf_op jit(solution)/shard_map/dot_general | solution.py:37
  280.9 30.3 %forward.3 = (f32[528,8,384]{2,1,0:T(8,128)}, f32[3,8,128]{2,1,0:T(8,128)}) custom-call(bf16[8,528,2304]{2,1,0:T(8,128)(2,1)} %pad_dynamic-update-slice_fusion.refs_0_, bf16[16,2304]{1,0:T(8,128)(2,1)} %pad.38.refs_10_.refs_1_, bf16[2304,768]{1,0:T(8,128)(2,1)} %all-gather.5.cloned.1.call-done.refs_7_.refs_2_.refs_3_, f32[1,384]{1,0:T(1,128)} %bitcast.212, ...), custom_call_target="tpu_custom_call" | custom-call | tf_op jit(solution)/shard_map/forward/pallas_call | solution.py:498
  311.8 6.3 %collective-permute-done.30 = f32[1,3,8,128]{3,2,1,0:T(8,128)S(1)} collective-permute-done((f32[1,3,8,128]{3,2,1,0:T(8,128)}, f32[1,3,8,128]{3,2,1,0:T(8,128)S(1)}, u32[]{:S(2)}, u32[]{:S(2)}) %collective-permute-start.30) | collective-permute-done | bytes 12320 | tf_op jit(solution)/shard_map/ppermute | solution.py:57
  319.9 6.4 %collective-permute-done.31 = f32[2,3,8,128]{3,2,1,0:T(8,128)S(1)} collective-permute-done((f32[2,3,8,128]{3,2,1,0:T(8,128)S(1)}, f32[2,3,8,128]{3,2,1,0:T(8,128)S(1)}, u32[]{:S(2)}, u32[]{:S(2)}) %collective-permute-start.31) | collective-permute-done | bytes 24608 | tf_op jit(solution)/shard_map/ppermute | solution.py:57
  333.8 14.8 %backward.3 = (bf16[4,528,128]{2,1,0:T(8,128)(2,1)}, bf16[4,528,128]{2,1,0:T(8,128)(2,1)}, bf16[8,528,768]{2,1,0:T(8,128)(2,1)}, f32[8,384]{1,0:T(8,128)}, f32[8,384]{1,0:T(8,128)}) custom-call(f32[528,8,384]{2,1,0:T(8,128)} %get-tuple-element.64.refs_0_, f32[528,8,128]{2,1,0:T(8,128)} %broadcast_in_dim.549.refs_13_.refs_1_.refs_4_, ...), custom_call_target="tpu_custom_call" | custom-call | tf_op jit(solution)/shard_map/backward/pallas_call | solution.py:670
  351.9 15.1 %input_gradient.3 = (bf16[1,528,2304]{2,1,0:T(8,128)(2,1)}, bf16[1,528,2304]{2,1,0:T(8,128)(2,1)}) custom-call(bf16[8,528,1024]{2,1,0:T(8,128)(2,1)} %pad_dynamic-update-slice_fusion.1.refs_0_, bf16[8,528,768]{2,1,0:T(8,128)(2,1)} %pad_dynamic-update-slice_fusion.2.refs_1_.refs_0_, bf16[2304,1024]{1,0:T(8,128)(2,1)} %all-gather.3.cloned.1.call-done.refs_11_.refs_2_, ...), custom_call_target="tpu_custom_call" | custom-call | tf_op jit(solution)/shard_map/input_gradient/pallas_call | solution.py:721
  368.6 4.0 collective-permute-done.32
  379.7 5.4 far_sum.1
  386.8 22.5 %bitcast_convert_fusion.1.refs_6_.refs_0_ = bf16[2304,768]{1,0:T(8,128)(2,1)} fusion(bf16[8,528,2304]{2,1,0:T(8,128)(2,1)} %pad_dynamic-update-slice_fusion.refs_0_, bf16[8,528,768]{2,1,0:T(8,128)(2,1)} %after.14.refs_1_), kind=kOutput, calls=%fused_computation.4 | convolution fusion | flops 14950268928 | bytes 29491200 | tf_op jit(solution)/shard_map/dot_general | solution.py:37
  409.3 4.6 collective-permute-done.37.refs_4_.low_ref
  417.7 24.2 %input_gradient.4 = (bf16[2,528,2304]{2,1,0:T(8,128)(2,1)}, bf16[2,528,2304]{2,1,0:T(8,128)(2,1)}) custom-call(bf16[8,528,1024]{2,1,0:T(8,128)(2,1)} %pad_dynamic-update-slice_fusion.1.refs_0_, bf16[8,528,768]{2,1,0:T(8,128)(2,1)} %after.14.refs_1_, bf16[2304,1024]{1,0:T(8,128)(2,1)} %all-gather.3.cloned.1.call-done.refs_11_.refs_2_, ...), custom_call_target="tpu_custom_call" | custom-call | tf_op jit(solution)/shard_map/input_gradient/pallas_call | solution.py:721
  441.9 8.4 %collective-permute-done.39.odd_ref = bf16[2,528,2304]{2,1,0:T(8,128)(2,1)} collective-permute-done((bf16[2,528,2304]{2,1,0:T(8,128)(2,1)}, bf16[2,528,2304]{2,1,0:T(8,128)(2,1)}, u32[]{:S(2)}, u32[]{:S(2)}) %collective-permute-start.39) | collective-permute-done | bytes 4866080 | tf_op jit(solution)/shard_map/ppermute | solution.py:57
  450.3 7.9 %near_sums.1 = (bf16[528,2304]{1,0:T(8,128)(2,1)}, bf16[528,2304]{1,0:T(8,128)(2,1)}) custom-call(bf16[2,528,2304]{2,1,0:T(8,128)(2,1)} %get-tuple-element.74.even_ref, bf16[2,528,2304]{2,1,0:T(8,128)(2,1)} %collective-permute-done.39.odd_ref, bf16[256,2304]{1,0:T(8,128)(2,1)} %copy-done.8, bf16[272,2304]{1,0:T(8,128)(2,1)} %copy-done.7), custom_call_target="tpu_custom_call" | custom-call | tf_op jit(solution)/shard_map/near_sums/pallas_call | solution.py:775
  460.2 15.1 %input_gradient.5 = (bf16[1,528,2304]{2,1,0:T(8,128)(2,1)}, bf16[1,528,2304]{2,1,0:T(8,128)(2,1)}) custom-call(bf16[8,528,1024]{2,1,0:T(8,128)(2,1)} %pad_dynamic-update-slice_fusion.1.refs_0_, bf16[8,528,768]{2,1,0:T(8,128)(2,1)} %after.14.refs_1_, bf16[2304,1024]{1,0:T(8,128)(2,1)} %all-gather.3.cloned.1.call-done.refs_11_.refs_2_, ...), custom_call_target="tpu_custom_call" | custom-call | tf_op jit(solution)/shard_map/input_gradient/pallas_call | solution.py:721
  477.0 4.2 place_channels.1
  481.1 32.3 %collective-permute-done.41.refs_2_ = bf16[528,2304]{1,0:T(8,128)(2,1)S(1)} collective-permute-done((bf16[528,2304]{1,0:T(8,128)(2,1)}, bf16[528,2304]{1,0:T(8,128)(2,1)S(1)}, u32[]{:S(2)}, u32[]{:S(2)}) %collective-permute-start.41) | collective-permute-done | bytes 2433056 | tf_op jit(solution)/shard_map/ppermute | solution.py:57
  540.0 5.2 fusion.4
  556.4 5.4 collective-permute-done.50.refs_1_
  565.0 9.9 %collective-permute-done.52.refs_3_ = bf16[2,72,1792]{2,1,0:T(8,128)(2,1)} collective-permute-done((bf16[2,72,1792]{2,1,0:T(8,128)(2,1)}, bf16[2,72,1792]{2,1,0:T(8,128)(2,1)}, u32[]{:S(2)}, u32[]{:S(2)}) %collective-permute-start.52) | collective-permute-done | bytes 516128 | tf_op jit(solution)/shard_map/ppermute | solution.py:57
  574.9 4.0 place_gradient.1
  578.9 9.5 %multiply_subtract_fusion = (f32[2,72,6912]{2,1,0:T(8,128)}, f32[2,72,6912]{2,1,0:T(8,128)}, f32[2,72,6912]{2,1,0:T(8,128)}, f32[2,72,6912]{2,1,0:T(8,128)}) fusion(f32[2,72,6912]{2,1,0:T(8,128)S(1)} %copy-done.4, f32[2,72,6912]{2,1,0:T(8,128)} %param.20, f32[2,72,6912]{2,1,0:T(8,128)} %param.21, f32[2,72,6912]{2,1,0:T(8,128)} %place_gradient.1, f32[]{:T(128)S(6)} %min.3), kind=kLoop, calls=%fused_computation.11 | loop fusion | flops 15925248 | bytes 31850500 | tf_op jit(solution)/shard_map/sub | solution.py:794
  (375 shorter events, 146.7 us)
Async XLA Ops:
  7.2 150.9 %all-gather.3.cloned.1.call-start = ((), (), s32[]{:S(2)}) async-start(), calls=%async_computation.2 | async-start | bytes 5898240 | tf_op jit(solution)/shard_map/all_gather | solution.py:843
  18.1 26.3 %collective-permute-start.2 = (bf16[2,72,1792]{2,1,0:T(8,128)(2,1)}, bf16[2,72,1792]{2,1,0:T(8,128)(2,1)}, u32[]{:S(2)}, u32[]{:S(2)}) collective-permute-start(bf16[2,72,1792]{2,1,0:T(8,128)(2,1)} %pad_maximum_fusion.6), channel_id=1, source_target_pairs={{0,2},{1,3},{2,0},{3,1},{4,6},{5,7},{6,4},{7,5},{8,10},{9,11},{10,... | collective-permute-start | bytes 1548296 | tf_op jit(solution)/shard_map/ppermute | solution.py:57
  20.7 25.6 %collective-permute-start.4 = (bf16[2,72,1792]{2,1,0:T(8,128)(2,1)S(1)}, bf16[2,72,1792]{2,1,0:T(8,128)(2,1)}, u32[]{:S(2)}, u32[]{:S(2)}) collective-permute-start(bf16[2,72,1792]{2,1,0:T(8,128)(2,1)S(1)} %pad_maximum_fusion.8.refs_4_), channel_id=1, source_target_pairs={{0,6},{1,7},{2,4},{3,5},{4,2},{5,3},{6,0},{7,1},{8,14},{9,15},{10,... | collective-permute-start | bytes 1548296 | tf_op jit(solution)/shard_map/ppermute | solution.py:57
  25.9 19.6 %collective-permute-start.3 = (bf16[2,72,1792]{2,1,0:T(8,128)(2,1)S(1)}, bf16[2,72,1792]{2,1,0:T(8,128)(2,1)S(1)}, u32[]{:S(2)}, u32[]{:S(2)}) collective-permute-start(bf16[2,72,1792]{2,1,0:T(8,128)(2,1)S(1)} %pad_maximum_fusion.7), channel_id=1, source_target_pairs={{0,4},{1,5},{2,6},{3,7},{4,0},{5,1},{6,2},{7,3},{8,12},{9,13},{10,... | collective-permute-start | bytes 1548296 | tf_op jit(solution)/shard_map/ppermute | solution.py:57
  49.3 175.4 %all-gather.5.cloned.1.call-start = ((), (), s32[]{:S(2)}) async-start(), calls=%async_computation.3 | async-start | bytes 4423680 | tf_op jit(solution)/shard_map/all_gather | solution.py:843
  49.3 106.5 %collective-permute-start = (bf16[512,2304]{1,0:T(8,128)(2,1)}, bf16[512,2304]{1,0:T(8,128)(2,1)}, u32[]{:S(2)}, u32[]{:S(2)}) collective-permute-start(bf16[512,2304]{1,0:T(8,128)(2,1)} %bitcast.189), channel_id=1, source_target_pairs={{0,1},{1,0},{2,3},{3,2},{4,5},{5,4},{6,7},{7,6},{8,9},{9,8},{10,11... | collective-permute-start | bytes 7077896 | tf_op jit(solution)/shard_map/ppermute | solution.py:57
  49.6 23.6 %collective-permute-start.22 = (bf16[4,528,128]{2,1,0:T(8,128)(2,1)}, bf16[4,528,128]{2,1,0:T(8,128)(2,1)}, u32[]{:S(2)}, u32[]{:S(2)}) collective-permute-start(bf16[4,528,128]{2,1,0:T(8,128)(2,1)} %get-tuple-element.58), channel_id=1, source_target_pairs={{0,1},{1,0},{2,3},{3,2},{4,5},{5,4},{6,7},{7,6},{8,9},{9,8},{10,11... | collective-permute-start | bytes 1622024 | tf_op jit(solution)/shard_map/ppermute | solution.py:57
  53.3 15.9 %collective-permute-start.8 = (bf16[2,688,128]{2,1,0:T(8,128)(2,1)S(1)}, bf16[2,688,128]{2,1,0:T(8,128)(2,1)S(1)}, u32[]{:S(2)}, u32[]{:S(2)}) collective-permute-start(bf16[2,688,128]{2,1,0:T(8,128)(2,1)S(1)} %copy-done.18), channel_id=1, source_target_pairs={{0,6},{1,7},{2,4},{3,5},{4,2},{5,3},{6,0},{7,1},{8,14},{9,15},{10,... | collective-permute-start | bytes 1056776 | tf_op jit(solution)/shard_map/ppermute | solution.py:57
  69.9 52.7 %collective-permute-start.11 = (bf16[512,2304]{1,0:T(8,128)(2,1)}, bf16[512,2304]{1,0:T(8,128)(2,1)}, u32[]{:S(2)}, u32[]{:S(2)}) collective-permute-start(bf16[512,2304]{1,0:T(8,128)(2,1)} %after.9), channel_id=1, source_target_pairs={{0,4},{1,5},{2,6},{3,7},{4,0},{5,1},{6,2},{7,3},{8,12},{9,13},{10,... | collective-permute-start | bytes 7077896 | tf_op jit(solution)/shard_map/ppermute | solution.py:57
  71.6 55.0 %collective-permute-start.9 = (bf16[512,2304]{1,0:T(8,128)(2,1)}, bf16[512,2304]{1,0:T(8,128)(2,1)}, u32[]{:S(2)}, u32[]{:S(2)}) collective-permute-start(bf16[512,2304]{1,0:T(8,128)(2,1)} %after.9), channel_id=1, source_target_pairs={{0,2},{1,3},{2,0},{3,1},{4,6},{5,7},{6,4},{7,5},{8,10},{9,11},{10,... | collective-permute-start | bytes 7077896 | tf_op jit(solution)/shard_map/ppermute | solution.py:57
  77.3 309.5 %reduce-scatter.3.cloned.1.call-start = ((), (), s32[]{:S(2)}) async-start(), calls=%async_computation.4 | async-start | bytes 5898240 | tf_op jit(solution)/shard_map/reduce_scatter | solution.py:959
  79.2 51.4 %collective-permute-start.17 = (bf16[8,2304]{1,0:T(8,128)(2,1)S(1)}, bf16[8,2304]{1,0:T(8,128)(2,1)S(1)}, u32[]{:S(2)}, u32[]{:S(2)}) collective-permute-start(bf16[8,2304]{1,0:T(8,128)(2,1)S(1)} %bitcast.207), channel_id=1, source_target_pairs={{0,8},{1,9},{2,10},{3,11},{4,12},{5,13},{6,14},{7,15},{8,16},{9,17... | collective-permute-start | bytes 110600 | tf_op jit(solution)/shard_map/ppermute | solution.py:875
  83.1 47.4 %collective-permute-start.19 = (bf16[2,8,216]{2,1,0:T(8,128)(2,1)S(1)}, bf16[2,8,216]{2,1,0:T(8,128)(2,1)S(1)}, u32[]{:S(2)}, u32[]{:S(2)}) collective-permute-start(bf16[2,8,216]{2,1,0:T(8,128)(2,1)S(1)} %pad_maximum_fusion.36), channel_id=1, source_target_pairs={{0,16},{1,17},{2,18},{3,19},{4,20},{5,21},{6,22},{7,23},{8,24},{9,... | collective-permute-start | bytes 20744 | tf_op jit(solution)/shard_map/ppermute | solution.py:57
  125.0 26.4 %collective-permute-start.15 = (bf16[256,2304]{1,0:T(8,128)(2,1)}, bf16[256,2304]{1,0:T(8,128)(2,1)}, u32[]{:S(2)}, u32[]{:S(2)}) collective-permute-start(bf16[256,2304]{1,0:T(8,128)(2,1)} %slice.999), channel_id=1, source_target_pairs={{0,2},{1,3},{2,0},{3,1},{4,6},{5,7},{6,4},{7,5},{8,10},{9,11},{10,... | collective-permute-start | bytes 3538952 | tf_op jit(solution)/shard_map/ppermute | solution.py:57
  128.9 26.1 %collective-permute-start.13 = (bf16[256,2304]{1,0:T(8,128)(2,1)}, bf16[256,2304]{1,0:T(8,128)(2,1)}, u32[]{:S(2)}, u32[]{:S(2)}) collective-permute-start(bf16[256,2304]{1,0:T(8,128)(2,1)} %slice.998), channel_id=1, source_target_pairs={{0,4},{1,5},{2,6},{3,7},{4,0},{5,1},{6,2},{7,3},{8,12},{9,13},{10,... | collective-permute-start | bytes 3538952 | tf_op jit(solution)/shard_map/ppermute | solution.py:57
  130.5 25.3 %collective-permute-start.12 = (bf16[512,2304]{1,0:T(8,128)(2,1)}, bf16[512,2304]{1,0:T(8,128)(2,1)}, u32[]{:S(2)}, u32[]{:S(2)}) collective-permute-start(bf16[512,2304]{1,0:T(8,128)(2,1)} %collective-permute-done.11.refs_4_), channel_id=1, source_target_pairs={{0,1},{1,0},{2,3},{3,2},{4,5},{5,4},{6,7},{7,6},{8,9},{9,8},{10,11... | collective-permute-start | bytes 7077896 | tf_op jit(solution)/shard_map/ppermute | solution.py:57
  130.6 27.5 %collective-permute-start.10 = (bf16[512,2304]{1,0:T(8,128)(2,1)}, bf16[512,2304]{1,0:T(8,128)(2,1)}, u32[]{:S(2)}, u32[]{:S(2)}) collective-permute-start(bf16[512,2304]{1,0:T(8,128)(2,1)} %collective-permute-done.9.refs_2_), channel_id=1, source_target_pairs={{0,1},{1,0},{2,3},{3,2},{4,5},{5,4},{6,7},{7,6},{8,9},{9,8},{10,11... | collective-permute-start | bytes 7077896 | tf_op jit(solution)/shard_map/ppermute | solution.py:57
  280.1 234.8 %reduce-scatter.5.cloned.1.call-start = ((), (), s32[]{:S(2)}) async-start(), calls=%async_computation.5 | async-start | bytes 4423680 | tf_op jit(solution)/shard_map/reduce_scatter | solution.py:959
  329.3 20.7 %collective-permute-start.27 = (bf16[2,528,256]{2,1,0:T(8,128)(2,1)S(1)}, bf16[2,528,256]{2,1,0:T(8,128)(2,1)S(1)}, u32[]{:S(2)}, u32[]{:S(2)}) collective-permute-start(bf16[2,528,256]{2,1,0:T(8,128)(2,1)S(1)} %pad_maximum_fusion.2), channel_id=1, source_target_pairs={{0,2},{1,3},{2,0},{3,1},{4,6},{5,7},{6,4},{7,5},{8,10},{9,11},{10,... | collective-permute-start | bytes 1622024 | tf_op jit(solution)/shard_map/ppermute | solution.py:57
  329.4 20.6 %collective-permute-start.28 = (bf16[2,528,256]{2,1,0:T(8,128)(2,1)S(1)}, bf16[2,528,256]{2,1,0:T(8,128)(2,1)S(1)}, u32[]{:S(2)}, u32[]{:S(2)}) collective-permute-start(bf16[2,528,256]{2,1,0:T(8,128)(2,1)S(1)} %pad_maximum_fusion.3), channel_id=1, source_target_pairs={{0,4},{1,5},{2,6},{3,7},{4,0},{5,1},{6,2},{7,3},{8,12},{9,13},{10,... | collective-permute-start | bytes 1622024 | tf_op jit(solution)/shard_map/ppermute | solution.py:57
  331.0 19.7 %collective-permute-start.29 = (bf16[2,528,256]{2,1,0:T(8,128)(2,1)S(1)}, bf16[2,528,256]{2,1,0:T(8,128)(2,1)S(1)}, u32[]{:S(2)}, u32[]{:S(2)}) collective-permute-start(bf16[2,528,256]{2,1,0:T(8,128)(2,1)S(1)} %pad_maximum_fusion.4), channel_id=1, source_target_pairs={{0,6},{1,7},{2,4},{3,5},{4,2},{5,3},{6,0},{7,1},{8,14},{9,15},{10,... | collective-permute-start | bytes 1622024 | tf_op jit(solution)/shard_map/ppermute | solution.py:57
  373.3 35.9 %collective-permute-start.33 = (bf16[2,528,128]{2,1,0:T(8,128)(2,1)}, bf16[2,528,128]{2,1,0:T(8,128)(2,1)S(1)}, u32[]{:S(2)}, u32[]{:S(2)}) collective-permute-start(bf16[2,528,128]{2,1,0:T(8,128)(2,1)} %pad_maximum_fusion.21), channel_id=1, source_target_pairs={{0,2},{1,3},{2,0},{3,1},{4,6},{5,7},{6,4},{7,5},{8,10},{9,11},{10,... | collective-permute-start | bytes 811016 | tf_op jit(solution)/shard_map/ppermute | solution.py:57
  374.2 35.1 %collective-permute-start.34 = (bf16[2,528,128]{2,1,0:T(8,128)(2,1)}, bf16[2,528,128]{2,1,0:T(8,128)(2,1)S(1)}, u32[]{:S(2)}, u32[]{:S(2)}) collective-permute-start(bf16[2,528,128]{2,1,0:T(8,128)(2,1)} %pad_maximum_fusion.22), channel_id=1, source_target_pairs={{0,4},{1,5},{2,6},{3,7},{4,0},{5,1},{6,2},{7,3},{8,12},{9,13},{10,... | collective-permute-start | bytes 811016 | tf_op jit(solution)/shard_map/ppermute | solution.py:57
  376.4 32.8 %collective-permute-start.35 = (bf16[2,528,128]{2,1,0:T(8,128)(2,1)}, bf16[2,528,128]{2,1,0:T(8,128)(2,1)S(1)}, u32[]{:S(2)}, u32[]{:S(2)}) collective-permute-start(bf16[2,528,128]{2,1,0:T(8,128)(2,1)} %pad_maximum_fusion.23), channel_id=1, source_target_pairs={{0,6},{1,7},{2,4},{3,5},{4,2},{5,3},{6,0},{7,1},{8,14},{9,15},{10,... | collective-permute-start | bytes 811016 | tf_op jit(solution)/shard_map/ppermute | solution.py:57
  385.1 28.7 %collective-permute-start.37 = (bf16[256,2304]{1,0:T(8,128)(2,1)}, bf16[256,2304]{1,0:T(8,128)(2,1)S(1)}, u32[]{:S(2)}, u32[]{:S(2)}) collective-permute-start(bf16[256,2304]{1,0:T(8,128)(2,1)} %get-tuple-element.72.refs_1_), channel_id=1, source_target_pairs={{0,4},{1,5},{2,6},{3,7},{4,0},{5,1},{6,2},{7,3},{8,12},{9,13},{10,... | collective-permute-start | bytes 3538952 | tf_op jit(solution)/shard_map/ppermute | solution.py:57
  386.6 30.0 %collective-permute-start.38 = (bf16[272,2304]{1,0:T(8,128)(2,1)}, bf16[272,2304]{1,0:T(8,128)(2,1)S(1)}, u32[]{:S(2)}, u32[]{:S(2)}) collective-permute-start(bf16[272,2304]{1,0:T(8,128)(2,1)} %get-tuple-element.73), channel_id=1, source_target_pairs={{0,2},{1,3},{2,0},{3,1},{4,6},{5,7},{6,4},{7,5},{8,10},{9,11},{10,... | collective-permute-start | bytes 3760136 | tf_op jit(solution)/shard_map/ppermute | solution.py:57
  458.2 55.2 %collective-permute-start.41 = (bf16[528,2304]{1,0:T(8,128)(2,1)}, bf16[528,2304]{1,0:T(8,128)(2,1)S(1)}, u32[]{:S(2)}, u32[]{:S(2)}) collective-permute-start(bf16[528,2304]{1,0:T(8,128)(2,1)} %get-tuple-element.76.refs_4_), channel_id=1, source_target_pairs={{0,2},{1,3},{2,0},{3,1},{4,6},{5,7},{6,4},{7,5},{8,10},{9,11},{10,... | collective-permute-start | bytes 7299080 | tf_op jit(solution)/shard_map/ppermute | solution.py:57
  458.7 55.0 %collective-permute-start.42 = (bf16[528,2304]{1,0:T(8,128)(2,1)}, bf16[528,2304]{1,0:T(8,128)(2,1)}, u32[]{:S(2)}, u32[]{:S(2)}) collective-permute-start(bf16[528,2304]{1,0:T(8,128)(2,1)} %get-tuple-element.77.refs_5_), channel_id=1, source_target_pairs={{0,4},{1,5},{2,6},{3,7},{4,0},{5,1},{6,2},{7,3},{8,12},{9,13},{10,... | collective-permute-start | bytes 7299080 | tf_op jit(solution)/shard_map/ppermute | solution.py:57
  475.3 52.9 %collective-permute-start.40 = (bf16[1,528,2304]{2,1,0:T(8,128)(2,1)}, bf16[1,528,2304]{2,1,0:T(8,128)(2,1)}, u32[]{:S(2)}, u32[]{:S(2)}) collective-permute-start(bf16[1,528,2304]{2,1,0:T(8,128)(2,1)} %get-tuple-element.79), channel_id=1, source_target_pairs={{0,1},{1,0},{2,3},{3,2},{4,5},{5,4},{6,7},{7,6},{8,9},{9,8},{10,11... | collective-permute-start | bytes 7299080 | tf_op jit(solution)/shard_map/ppermute | solution.py:57
  547.6 14.2 %collective-permute-start.50 = (bf16[2,72,1792]{2,1,0:T(8,128)(2,1)}, bf16[2,72,1792]{2,1,0:T(8,128)(2,1)}, u32[]{:S(2)}, u32[]{:S(2)}) collective-permute-start(bf16[2,72,1792]{2,1,0:T(8,128)(2,1)} %pad_maximum_fusion.10), channel_id=1, source_target_pairs={{0,2},{1,3},{2,0},{3,1},{4,6},{5,7},{6,4},{7,5},{8,10},{9,11},{10,... | collective-permute-start | bytes 1548296 | tf_op jit(solution)/shard_map/ppermute | solution.py:57
  550.0 15.0 %collective-permute-start.51 = (bf16[2,72,1792]{2,1,0:T(8,128)(2,1)}, bf16[2,72,1792]{2,1,0:T(8,128)(2,1)}, u32[]{:S(2)}, u32[]{:S(2)}) collective-permute-start(bf16[2,72,1792]{2,1,0:T(8,128)(2,1)} %pad_maximum_fusion.11), channel_id=1, source_target_pairs={{0,4},{1,5},{2,6},{3,7},{4,0},{5,1},{6,2},{7,3},{8,12},{9,13},{10,... | collective-permute-start | bytes 1548296 | tf_op jit(solution)/shard_map/ppermute | solution.py:57
  550.9 24.0 %collective-permute-start.52 = (bf16[2,72,1792]{2,1,0:T(8,128)(2,1)}, bf16[2,72,1792]{2,1,0:T(8,128)(2,1)}, u32[]{:S(2)}, u32[]{:S(2)}) collective-permute-start(bf16[2,72,1792]{2,1,0:T(8,128)(2,1)} %pad_maximum_fusion.12), channel_id=1, source_target_pairs={{0,6},{1,7},{2,4},{3,5},{4,2},{5,3},{6,0},{7,1},{8,14},{9,15},{10,... | collective-permute-start | bytes 1548296 | tf_op jit(solution)/shard_map/ppermute | solution.py:57
  (76 other events, 643.0 us)
Sparse Core Ops, SparseCore 0:
  49.4 91.2 all-gather.2
  142.8 68.9 all-gather.4
  280.2 85.4 reduce-scatter.2
  442.0 66.8 reduce-scatter.4

commit v3 on v2

--- a/solution.py
+++ b/solution.py
@@ -95,17 +95,17 @@
     out_ref[...] = in_ref[...]
 
 
-def copied(value):
+def copied(value, *others):
     rows, width = value.shape
     spec = pl.BlockSpec((rows // 4, width), lambda i: (i, 0))
     return pl.pallas_call(
-        copy_kernel,
+        waiting(copy_kernel, 1, others),
         grid=(4,),
         out_shape=jax.ShapeDtypeStruct(value.shape, value.dtype),
-        in_specs=[spec],
+        in_specs=[spec, *unseen(others)],
         out_specs=spec,
         name="copied",
-    )(value)
+    )(value, *others)
 
 
 def blank(shape, dtype):
@@ -199,8 +199,14 @@
     )(member, *pairs, *others)
 
 
-def pick_rows_kernel(member_ref, first_ref, second_ref, even_ref, odd_ref):
+def pick_rows_kernel(member_ref, first_ref, second_ref, even_ref, odd_ref, squares_ref):
     split = first_ref.shape[-1]
+    squares = jnp.zeros((first_ref.shape[1], LANES), F32)
+    for p in range(MEMBERS):
+        for ref in (first_ref, second_ref):
+            for i in range(ref.shape[-1] // LANES):
+                squares += jnp.square(ref[p, :, pl.ds(i * LANES, LANES)].astype(F32))
+    squares_ref[...] = jnp.sum(squares, axis=0, keepdims=True)
     for p in range(MEMBERS):
         out = (even_ref, odd_ref)[p % 2]
         out[p // 2, :, pl.ds(0, split)] = first_ref[member_ref[0] ^ p]
@@ -211,9 +217,9 @@
     shape = jax.ShapeDtypeStruct((4, first.shape[1], first.shape[2] + second.shape[2]), BF16)
     return pl.pallas_call(
         pick_rows_kernel,
-        out_shape=(shape, shape),
+        out_shape=(shape, shape, jax.ShapeDtypeStruct((1, LANES), F32)),
         in_specs=[pl.BlockSpec(memory_space=pltpu.SMEM)] + in_vmem(2),
-        out_specs=tuple(in_vmem(2)),
+        out_specs=tuple(in_vmem(3)),
         compiler_params=params(),
         name="pick_rows",
     )(member, first, second)
@@ -233,7 +239,7 @@
             for tap in range(taps):
                 for gate in range(3):
                     start = pl.multiple_of(gate * width + (tile * MEMBERS + source) * LANES, LANES)
-                    out_ref[tap, :, pl.ds(start, LANES)] = block_ref[p % 2, :, pl.ds(column, LANES)].astype(F32)
+                    out_ref[tap, :, pl.ds(start, LANES)] = block_ref[p % 2, :, pl.ds(column, LANES)]
                     column += LANES
                 if tile == 0:
                     mixed = block_ref[p % 2, :, pl.ds(column, LANES)].astype(F32)
@@ -243,14 +249,14 @@
                         first = (source % per_tile) * rest
                         part = pltpu.roll(mixed, lax.rem(first - gate * rest + LANES, LANES), 1)
                         inside = (lane >= first) & (lane < first + rest)
-                        old = out_ref[tap, :, pl.ds(start, LANES)]
-                        out_ref[tap, :, pl.ds(start, LANES)] = jnp.where(inside, part, old)
+                        old = out_ref[tap, :, pl.ds(start, LANES)].astype(F32)
+                        out_ref[tap, :, pl.ds(start, LANES)] = jnp.where(inside, part, old).astype(BF16)
 
 
 def place_gradient(pairs, member, shape):
     return pl.pallas_call(
         functools.partial(place_gradient_kernel, shape[2] // 3),
-        out_shape=jax.ShapeDtypeStruct(shape, F32),
+        out_shape=jax.ShapeDtypeStruct(shape, BF16),
         in_specs=[pl.BlockSpec(memory_space=pltpu.SMEM)] + in_vmem(4),
         out_specs=pl.BlockSpec(memory_space=pltpu.VMEM),
         compiler_params=params(),
@@ -334,8 +340,8 @@
 
 def place_channels_kernel(width, member_ref, *refs):
     rest = sizes(width)[1]
-    out_ref = refs[8]
-    rows, _ = out_ref.shape
+    out_ref, tail_ref, all_ref = refs[8:]
+    rows, _ = all_ref.shape
     per_tile = LANES // rest
     lane = lane_index((rows, LANES))
     for p in range(MEMBERS):
@@ -343,27 +349,71 @@
         for tile in range(2):
             block_ref = refs[4 * tile + p // 2]
             start = pl.multiple_of((tile * MEMBERS + source) * LANES, LANES)
-            out_ref[:, pl.ds(start, LANES)] = block_ref[p % 2, :, pl.ds(0, LANES)]
+            all_ref[:, pl.ds(start, LANES)] = block_ref[p % 2, :, pl.ds(0, LANES)]
         start = pl.multiple_of((2 * MEMBERS + source // per_tile) * LANES, LANES)
         first = (source % per_tile) * rest
         part = pltpu.roll(refs[p // 2][p % 2, :, pl.ds(LANES, LANES)].astype(F32), first, 1)
         inside = (lane >= first) & (lane < first + rest)
-        old = out_ref[:, pl.ds(start, LANES)].astype(F32)
-        out_ref[:, pl.ds(start, LANES)] = jnp.where(inside, part, old).astype(BF16)
+        old = all_ref[:, pl.ds(start, LANES)].astype(F32)
+        all_ref[:, pl.ds(start, LANES)] = jnp.where(inside, part, old).astype(BF16)
+    out_ref[...] = all_ref[pl.ds(0, rows - TAIL), :]
+    tail_ref[...] = all_ref[pl.ds(rows - TAIL, TAIL), :]
 
 
 def place_channels(pairs, member, width):
     return pl.pallas_call(
         functools.partial(place_channels_kernel, width),
-        out_shape=jax.ShapeDtypeStruct((pairs[0].shape[1], width), BF16),
+        out_shape=[jax.ShapeDtypeStruct((n, width), BF16) for n in (pairs[0].shape[1] - TAIL, TAIL)],
         in_specs=[pl.BlockSpec(memory_space=pltpu.SMEM)] + in_vmem(8),
-        out_specs=pl.BlockSpec(memory_space=pltpu.VMEM),
+        out_specs=in_vmem(2),
+        scratch_shapes=[pltpu.VMEM((pairs[0].shape[1], width), BF16)],
         compiler_params=params(),
         name="place_channels",
     )(member, *pairs)
 
 
+def bias_columns_kernel(width, place_ref, vectors_ref, out_ref, natural):
+    rest = sizes(width)[1]
+    per_tile = LANES // rest
+    tiles = width // LANES
+    lane = lane_index((1, LANES))
+    for p in range(MEMBERS):
+        source = place_ref[0] ^ p
+        mixed = vectors_ref[pl.ds(p, 1), pl.ds(3 * LANES, LANES)]
+        first = (source % per_tile) * rest
+        for gate in range(3):
+            natural[pl.ds(gate * tiles + source, 1), :] = vectors_ref[pl.ds(p, 1), pl.ds(gate * LANES, LANES)]
+            part = vectors_ref[pl.ds(p, 1), pl.ds((4 + gate) * LANES, LANES)]
+            natural[pl.ds(gate * tiles + MEMBERS + source, 1), :] = part
+            row = pl.ds(gate * tiles + 2 * MEMBERS + source // per_tile, 1)
+            part = pltpu.roll(mixed, lax.rem(first - gate * rest + LANES, LANES), 1)
+            inside = (lane >= first) & (lane < first + rest)
+            natural[row, :] = jnp.where(inside, part, natural[row, :])
+    shift = place_ref[2]
+    for i in range(out_ref.shape[0]):
+        here = pltpu.roll(natural[pl.ds(place_ref[1] + i, 1), :], lax.rem(LANES - shift, LANES), 1)
+        later = pltpu.roll(natural[pl.ds(place_ref[1] + i + 1, 1), :], lax.rem(LANES - shift, LANES), 1)
+        out_ref[pl.ds(i, 1), :] = jnp.where(lane < LANES - shift, here, later)
+
+
+def bias_columns(vectors, here, width, count):
+    rows = -(-count // LANES)
+    start = here.linear * count
+    place = jnp.stack([here.member, start // LANES, start % LANES]).astype(jnp.int32)
+    found = pl.pallas_call(
+        functools.partial(bias_columns_kernel, width),
+        out_shape=jax.ShapeDtypeStruct((rows, LANES), F32),
+        in_specs=[pl.BlockSpec(memory_space=pltpu.SMEM)] + in_vmem(1),
+        out_specs=pl.BlockSpec(memory_space=pltpu.VMEM),
+        scratch_shapes=[pltpu.VMEM((3 * width // LANES + rows + 8, LANES), F32)],
+        compiler_params=params(),
+        name="bias_columns",
+    )(place, vectors)
+    return found.reshape(-1)[:count]
+
+
 UNROLL = 16
+GAP = 8
 
 
 def token_loop(low, high, token, state, reverse):
@@ -418,12 +468,13 @@
     else:
         x = x_refs[0][...].reshape(rows, x_refs[0].shape[2])
     result = dot_f32(x, w_ref[...], ((1,), (0,)))
-    for i in range(2 * count):
-        both[i] = result[:, i * LANES : (i + 1) * LANES]
-    cot_f32[0] = cot_ref[...].reshape(rows, LANES).astype(F32)
-    if tiles == 2:
-        folded = folded_ref[...].reshape(rows, LANES).astype(F32)
-        cot_f32[1] = pltpu.roll(folded, lax.rem(LANES - step * rest, LANES), 1)
+    for p in range(MEMBERS):
+        at = pl.ds(p * (block + GAP), block)
+        for i in range(2 * count):
+            both[i, at, :] = result[p * block : (p + 1) * block, i * LANES : (i + 1) * LANES]
+        cot_f32[0, at, :] = cot_ref[p].astype(F32)
+        if tiles == 2:
+            cot_f32[1, at, :] = pltpu.roll(folded_ref[p].astype(F32), lax.rem(LANES - step * rest, LANES), 1)
 
     @pl.when(step == 0)
     def _():
@@ -437,7 +488,7 @@
 
     def token(k, state):
         sums, earlier = state
-        rows_at = pl.ds(k, MEMBERS, stride=block)
+        rows_at = pl.ds(k, MEMBERS, stride=block + GAP)
         keep = keep_ref[k]
         later = tuple(both[count + i, rows_at, :] for i in range(count))
         gates = [
@@ -518,8 +569,8 @@
             *[pl.BlockSpec((MEMBERS, block, width), lambda i: (0, i, 0)) for _ in whole],
         ),
         scratch_shapes=[
-            pltpu.VMEM((2 * half // LANES, MEMBERS * block, LANES), F32),
-            pltpu.VMEM((tiles, MEMBERS * block, LANES), F32),
+            pltpu.VMEM((2 * half // LANES, MEMBERS * (block + GAP), LANES), F32),
+            pltpu.VMEM((tiles, MEMBERS * (block + GAP), LANES), F32),
             pltpu.VMEM((3 * tiles, MEMBERS, LANES), F32),
             pltpu.VMEM((half // LANES, MEMBERS, LANES), F32),
         ],
@@ -535,11 +586,11 @@
     step = pl.program_id(0)
     block = act_ref.shape[0]
     half = act_ref.shape[2]
-    rows = MEMBERS * block
     lane = lane_index((MEMBERS, LANES))
     which = jnp.where(step < blocks, step, 2 * blocks - 1 - step)
     base = which * block
-    cot_f32[...] = cot_ref[...].reshape(rows, LANES).astype(F32)
+    for p in range(MEMBERS):
+        cot_f32[pl.ds(p * (block + GAP), block), :] = cot_ref[p].astype(F32)
     count = half // LANES
     top = jnp.where(which == blocks - 1, block - TAIL, block)
 
@@ -576,7 +627,7 @@
                 z, u, o = values(k, tile)
                 m = keep * (1.0 - u) * state[tile] + u * z
                 memory[base + k + 1, tile] = m
-                hold[tile, pl.ds(k, MEMBERS, stride=block), :] = o * m
+                hold[tile, pl.ds(k, MEMBERS, stride=block + GAP), :] = o * m
                 new.append(m)
             return tuple(new)
 
@@ -590,14 +641,14 @@
                 rest_of = final_ref[tile]
                 for row in range(3):
                     part = rest_of.astype(BF16).astype(F32)
-                    hold[tile, pl.ds(block - TAIL + row, MEMBERS, stride=block), :] = part
+                    hold[tile, pl.ds(block - TAIL + row, MEMBERS, stride=block + GAP), :] = part
                     rest_of = rest_of - part
                 for row in range(3, TAIL):
-                    hold[tile, pl.ds(block - TAIL + row, MEMBERS, stride=block), :] = jnp.zeros_like(part)
+                    hold[tile, pl.ds(block - TAIL + row, MEMBERS, stride=block + GAP), :] = jnp.zeros_like(part)
 
         for tile in range(tiles):
             for p in range(MEMBERS):
-                part = hold[tile, pl.ds(p * block, block), :].astype(BF16)
+                part = hold[tile, pl.ds(p * (block + GAP), block), :].astype(BF16)
                 (even_ref, odd_ref)[p % 2][p // 2, :, pl.ds(tile * LANES, LANES)] = part
 
     @pl.when(step == blocks)
@@ -611,7 +662,7 @@
     def _():
         def token(k, state):
             arriving, shifted, totals = state
-            rows_at = pl.ds(k, MEMBERS, stride=block)
+            rows_at = pl.ds(k, MEMBERS, stride=block + GAP)
             keep = keep_ref[k]
             new, parts = [], []
             for tile in range(tiles):
@@ -655,10 +706,12 @@
         def _():
             for row in range(block - TAIL, block):
                 for i in range(2 * count):
-                    wide[i, pl.ds(row, MEMBERS, stride=block), :] = jnp.zeros((MEMBERS, LANES), F32)
+                    wide[i, pl.ds(row, MEMBERS, stride=block + GAP), :] = jnp.zeros((MEMBERS, LANES), F32)
 
         for i in range(2 * count):
-            grads_ref[:, :, pl.ds(i * LANES, LANES)] = wide[i].astype(BF16).reshape(MEMBERS, block, LANES)
+            for p in range(MEMBERS):
+                part = wide[i, pl.ds(p * (block + GAP), block), :].astype(BF16)
+                grads_ref[p, :, pl.ds(i * LANES, LANES)] = part
 
 
 def backward(act, keep, cot, enter, arrive, final, tiles, rest, *others):
@@ -694,12 +747,12 @@
         ),
         scratch_shapes=[
             pltpu.VMEM((length, tiles, members, LANES), F32),
-            pltpu.VMEM((members * block, LANES), F32),
-            pltpu.VMEM((2 * half // LANES, members * block, LANES), F32),
-            pltpu.VMEM((tiles, members * block, LANES), F32),
+            pltpu.VMEM((members * (block + GAP), LANES), F32),
+            pltpu.VMEM((2 * half // LANES, members * (block + GAP), LANES), F32),
+            pltpu.VMEM((tiles, members * (block + GAP), LANES), F32),
             pltpu.VMEM((tiles, members, LANES), F32),
             pltpu.VMEM((half // LANES, members, LANES), F32),
-            *[pltpu.VMEM((members * (length - TAIL), LANES), F32) for _ in range(tiles - 1)],
+            *[pltpu.VMEM((members * (length - TAIL + GAP), LANES), F32) for _ in range(tiles - 1)],
         ],
         compiler_params=params(),
         name="backward",
@@ -757,30 +810,56 @@
     )(even, odd)
 
 
-def near_sums_kernel(even_ref, odd_ref, low_ref, high_ref, to_y, to_x):
+def near_sums_kernel(even_ref, odd_ref, low_ref, high_ref, y_low, y_high, x_low, x_high):
     middle = low_ref.shape[0]
     total = even_ref[0].astype(F32) + odd_ref[0].astype(F32)
-    to_y[pl.ds(0, middle), :] = (total[:middle] + low_ref[...].astype(F32)).astype(BF16)
-    to_y[pl.ds(middle, high_ref.shape[0]), :] = total[middle:].astype(BF16)
+    y_low[...] = (total[:middle] + low_ref[...].astype(F32)).astype(BF16)
+    y_high[...] = total[middle:].astype(BF16)
     total = even_ref[1].astype(F32) + odd_ref[1].astype(F32)
-    to_x[pl.ds(0, middle), :] = total[:middle].astype(BF16)
-    to_x[pl.ds(middle, high_ref.shape[0]), :] = (total[middle:] + high_ref[...].astype(F32)).astype(BF16)
+    x_low[...] = total[:middle].astype(BF16)
+    x_high[...] = (total[middle:] + high_ref[...].astype(F32)).astype(BF16)
 
 
 def near_sums(even, odd, low, high):
     _, length, width = even.shape
     block = 384
     spec = pl.BlockSpec((2, length, block), lambda i: (0, 0, i))
-    out = pl.BlockSpec((length, block), lambda i: (0, i))
+    halves = [pl.BlockSpec((part.shape[0], block), lambda i: (0, i)) for part in (low, high)]
     return pl.pallas_call(
         near_sums_kernel,
         grid=(width // block,),
-        out_shape=[jax.ShapeDtypeStruct((length, width), BF16)] * 2,
-        in_specs=[spec, spec] + [pl.BlockSpec((part.shape[0], block), lambda i: (0, i)) for part in (low, high)],
-        out_specs=[out, out],
+        out_shape=[jax.ShapeDtypeStruct(part.shape, BF16) for part in (low, high, low, high)],
+        in_specs=[spec, spec] + halves,
+        out_specs=halves * 2,
         compiler_params=params(),
         name="near_sums",
     )(even, odd, low, high)
+
+
+def last_sum_kernel(even_ref, odd_ref, y_low, x_low, y_high, x_high, next_ref, out_ref):
+    middle = y_low.shape[0]
+    rows = out_ref.shape[0] - middle
+    total = even_ref[0].astype(F32) + odd_ref[0].astype(F32)
+    out_ref[pl.ds(0, middle), :] = (total[:middle] + y_low[...].astype(F32) + x_low[...].astype(F32)).astype(BF16)
+    high = total[middle : middle + rows] + y_high[pl.ds(0, rows), :].astype(F32) + x_high[pl.ds(0, rows), :].astype(F32)
+    row = lax.broadcasted_iota(jnp.int32, high.shape, 0)
+    out_ref[pl.ds(middle, rows), :] = jnp.where(row == rows - 1, high + next_ref[...], high).astype(BF16)
+
+
+def last_sum(even, odd, lows, highs, from_next, tokens):
+    _, length, width = even.shape
+    block = 384
+    spec = pl.BlockSpec((1, length, block), lambda i: (0, 0, i))
+    parts = [*lows, *highs, from_next]
+    return pl.pallas_call(
+        last_sum_kernel,
+        grid=(width // block,),
+        out_shape=jax.ShapeDtypeStruct((tokens, width), BF16),
+        in_specs=[spec, spec] + [pl.BlockSpec((part.shape[0], block), lambda i: (0, i)) for part in parts],
+        out_specs=pl.BlockSpec((tokens, block), lambda i: (0, i)),
+        compiler_params=params(),
+        name="last_sum",
+    )(even, odd, *parts)
 
 
 def adamw(master, gradient, moment_one, moment_two, rate):
@@ -849,14 +928,14 @@
     small = jnp.concatenate(small + [start_state, final_cotangent])
 
     own = inputs[0]
-    own_copy = copied(own)
+    own_copy = copied(own, weight_pairs[3])
     packed_cot = pack_channels(cotangent[0], small, marks, member, own_copy, weight_pairs[3])
-    cot_first, cot_second = here.pair_up(*packed_cot[:2]), here.pair_up(*packed_cot[2:])
+    cot_first = here.pair_up(*packed_cot[:2])
     got_first = here.send_pairs(cot_first)
-    placed = place_weight(weight_got, member, 8 * LANES, *cot_first[1:])
+    placed = place_weight(weight_got, member, 8 * LANES, got_first[1])
     weights = [all_rows(part) for part in placed]
     own_sibling = here.flip(own, 1)
-    sent = after(own_copy, *placed, *got_first[1:])
+    sent = after(own_copy, *got_first[1:])
     middle = (tokens // 32) * 16
     from_y = here.flip(sent, here.member_mask(2))
     from_x = here.flip(sent, here.member_mask(4))
@@ -890,6 +969,8 @@
     bias_all = jnp.take(bias_all, here.high ^ jnp.arange(here.depth), axis=1)
     bias_all = jnp.take(bias_all, every_member, axis=2)
     bias_all = bias_all.reshape(here.wide, here.depth, 2, 4, own_bias).transpose(1, 2, 0, 3, 4).reshape(3, width)
+    cot_second = here.pair_up(packed_cot[2], after(packed_cot[3], behind))
+    got_second = here.send_pairs([after(pair, pieces[7], pieces[9]) for pair in cot_second])
     bias_parts = channel_tiles(bias_all, here.member, rest)
     biases = [
         jnp.concatenate([bias_parts[0].reshape(1, 3 * LANES), widen(bias_parts[2].reshape(1, 3 * rest))], axis=1),
@@ -907,17 +988,23 @@
 
     halfway = (length // 32) * 16
     gradients, outs, hidden_got = [], [], []
+    acts, summaries = [], []
     for chunk in range(2):
-        tiles = 2 - chunk
-        others = (outs[0][4],) if chunk else ()
         source = [x_all] if chunk else pieces
-        act, summary, *whole = forward(source, edges, weights[chunk], biases[chunk], keep, cots[chunk], tiles, rest, *others)
+        act, summary, *whole = forward(source, edges, weights[chunk], biases[chunk], keep, cots[chunk], 2 - chunk, rest)
+        acts.append(act)
+        summaries.append(summary)
         if whole:
-            got_second = here.send_pairs([after(pair, summary) for pair in cot_second])
+            got_second = [after(got, summary) for got in got_second]
             cots.append(jnp.concatenate(got_second, axis=0))
             behind = jnp.pad(edges[:MEMBERS, None], ((0, 0), (0, TAIL - 1), (0, 0)))
             x_all = lax.dynamic_update_slice(whole[0], behind, (0, tokens, 0))
-        every = here.gather_flips(summary[None], here.deep_bits)
+    both_every = here.gather_flips(jnp.concatenate(summaries)[None], here.deep_bits)
+
+    for chunk in range(2):
+        tiles = 2 - chunk
+        act = acts[chunk]
+        every = both_every[:, :6] if chunk == 0 else both_every[:, 6:]
         enters, arrives, ends = [], [], []
         for tile in range(tiles):
             where = (0, 2, 1)[2 * chunk + tile]
@@ -940,67 +1027,62 @@
             enters.append(enter)
             arrives.append(arrive)
             ends.append(state)
-        others = () if chunk else (weights[1], cots[1])
+        others = (outs[0][4],) if chunk else ()
         even, odd, grads, bias_grad, edge_grad = backward(
             act, keep, cots[chunk], jnp.stack(enters), jnp.stack(arrives), jnp.stack(ends), tiles, rest, *others
         )
         half = edge_grad.shape[1]
         edge_grad = jnp.pad(edge_grad.astype(BF16)[:, None], ((0, 0), (0, TAIL - 1), (half, 0)))
         grads = lax.dynamic_update_slice(grads, edge_grad, (0, tokens, 0))
-        hidden_pairs = here.pair_up(even, odd)
-        hidden_got += here.send_pairs(hidden_pairs)
+        hidden_got += here.send_pairs(here.pair_up(even, odd))
         if chunk == 1:
             far_low, far_high = far_sum(*back_pairs(outs[0][2], grads, 3, 1, *hidden_got[1:4]), halfway)
-            grads = after(grads, far_low, gradients[0])
+            grads = after(grads, far_low, *hidden_got[5:])
         flat = grads.reshape(MEMBERS * length, -1)
         local = dot_f32(x_all.reshape(MEMBERS * length, width), flat, ((0,), (0,))).astype(BF16)
         cols = local.shape[-1]
-        ordered = after(local, gradients[0]) if gradients else local
-        summed = lax.psum_scatter(ordered, "seq", scatter_dimension=0, tiled=True, axis_index_groups=deep_groups)
+        local = after(local, gradients[0]) if gradients else local
+        summed = lax.psum_scatter(local, "seq", scatter_dimension=0, tiled=True, axis_index_groups=deep_groups)
         if here.wide > 1:
             summed = summed.reshape(2, here.wide, 4 * own_rows, cols).swapaxes(0, 1).reshape(-1, cols)
             summed = lax.psum_scatter(summed, "stream", scatter_dimension=0, tiled=True, axis_index_groups=wide_groups)
         gradients.append(summed.reshape(MEMBERS, own_rows, cols))
         outs.append((even, odd, grads, jnp.sum(bias_grad, axis=0), local))
 
-    hidden_own = place_channels(hidden_got, member, width)
-    hidden = hidden_own[None, :tokens]
-    whole_final = jnp.sum(hidden_own[tokens : tokens + 3].astype(F32), axis=0, keepdims=True)
-    own_columns = width // here.n_seq
-    final_state = lax.dynamic_slice_in_dim(whole_final, here.seq * own_columns, own_columns, 1)
-
     low_half = here.flip(far_low, here.member_mask(4))
     high_half = here.flip(far_high, here.member_mask(2))
     grads = outs[0][2], outs[1][2]
-    even, odd = back_pairs(*grads, 1, 2, low_half, high_half, outs[1][4], *hidden_got[5:])
-    to_y, to_x = near_sums(even, odd, low_half, high_half)
-    got_y = here.flip(to_y, here.member_mask(2))
-    got_x = here.flip(to_x, here.member_mask(4))
-    even, odd = back_pairs(*grads, 0, 1, to_y, to_x)
-    gradients = [after(gradient, even, got_y, got_x) for gradient in gradients]
-    add_up = lambda rows: sum(part[rows].astype(F32) for part in (even[0], odd[0], got_y, got_x))
-    from_next = lax.ppermute(
-        add_up(slice(tokens, tokens + 1)), "seq", [(i + 1, i) for i in range(here.n_seq - 1)]
-    )
-    last = lax.broadcasted_iota(jnp.int32, (tokens, 1), 0) == tokens - 1
-    input_gradient = (add_up(slice(0, tokens)) + jnp.where(last, from_next, 0.0)).astype(BF16)[None]
-
-    squares = sum(jnp.sum(jnp.square(g.astype(F32))) for g in gradients)
-    vector = jnp.concatenate([outs[0][3], outs[1][3], jnp.broadcast_to(squares, (LANES,))]).reshape(1, -1)
-    vector = here.sum_flips(vector, here.deep_bits + here.wide_bits)
-    vectors = here.gather_flips(vector, here.group_bits)
-    bias_every = jnp.take(vectors[:, :-LANES], every_member, axis=0)
-    gradient_norm = jnp.sqrt(jnp.sum(vectors[:, -1]) + jnp.sum(jnp.square(vectors[:, :-LANES])))
-    tile_a = bias_every[:, : 3 * LANES].reshape(MEMBERS, 3, LANES)
-    tile_b = bias_every[:, 4 * LANES : 7 * LANES].reshape(MEMBERS, 3, LANES)
-    tile_c = bias_every[:, 3 * LANES : 3 * LANES + 3 * rest].reshape(MEMBERS, 3, rest)
-    natural = jnp.concatenate([t.swapaxes(0, 1).reshape(3, -1) for t in (tile_a, tile_b, tile_c)], axis=1)
-    bias_raw = lax.dynamic_slice_in_dim(natural.reshape(-1), here.linear * own_bias, own_bias, 0)
+    even, odd = back_pairs(*grads, 1, 2, low_half, high_half, outs[1][4], gradients[0])
+    y_low, y_high, x_low, x_high = near_sums(even, odd, low_half, high_half)
+    lows = here.flip(y_low, here.member_mask(2)), here.flip(x_low, here.member_mask(4))
+    highs = here.flip(y_high, here.member_mask(2)), here.flip(x_high, here.member_mask(4))
+    hidden_own, final_rows = place_channels(hidden_got, member, width)
+    hidden = hidden_own[None]
+    whole_final = jnp.sum(final_rows[:3].astype(F32), axis=0, keepdims=True)
+    own_columns = width // here.n_seq
+    final_state = lax.dynamic_slice_in_dim(whole_final, here.seq * own_columns, own_columns, 1)
+    even, odd = back_pairs(*grads, 0, 1, y_high, hidden_own)
+    gradients = [after(gradient, even, *highs) for gradient in gradients]
+    *picked, squares = pick_rows(*gradients, member)
+    post_pairs = here.pair_up(*picked)
+    edge_sum = sum(part[tokens - halfway : tokens - halfway + 1].astype(F32) for part in (even[0, halfway:], odd[0, halfway:], *highs))
+    from_next = lax.ppermute(edge_sum, "seq", [(i + 1, i) for i in range(here.n_seq - 1)])
+    received = here.send_pairs(post_pairs)
+
+    vector = jnp.concatenate([outs[0][3], outs[1][3], squares[0]]).reshape(1, -1)
+    vector = here.sum_flips(after(vector, *post_pairs[1:]), here.deep_bits + here.wide_bits)
+    vector = here.gather_flips(vector, here.group_bits[:1])
+    vector = after(vector, *received[1:])
+    from_next = after(from_next, vector)
+    input_gradient = last_sum(even, odd, lows, highs, from_next, tokens)[None]
+    vectors = [vector] + [here.flip(vector, here.member_mask(2 * i)) for i in (1, 2, 3)]
+    vectors = jnp.concatenate(vectors, axis=0)
+    gradient_norm = jnp.sqrt(jnp.sum(vectors[:, -LANES:]) + jnp.sum(jnp.square(vectors[:, :-LANES])))
+    bias_raw = bias_columns(vectors, here, width, own_bias)
 
     clip_factor = jnp.minimum(1.0, CLIP_NORM / (gradient_norm + 1e-06))
-    received = here.exchange(*pick_rows(*gradients, member))
     raw = place_gradient(received, member, weight.shape)
-    weight_gradient = clip_factor * raw
+    weight_gradient = clip_factor * raw.astype(F32)
     bias_gradient = clip_factor * bias_raw
     new_weight, new_first_weight, new_second_weight = adamw(
         weight, weight_gradient, first_weight, second_weight, RATE_WEIGHT

time: 603 us -> 579 us (0.960)
  Pallas kernels: 210 us -> 195 us
  waiting for transfers between devices: 182 us -> 174 us
  local copies, waits for them, and re-layouts: 32.7 us -> 39.7 us
  other arithmetic: 48.6 us -> 42 us
    pallas_call x2, Pallas kernels: 75.7 us -> 60.5 us  [forward(): pl.pallas_call(waiting(functools.partial(forward_kernel, tiles, rest, 2 i...]
    ppermute x51 -> x52, waiting for transfers between devices: 181 us -> 172 us  [flip(): return lax.ppermute(block, AXES, [(n, n ^ mask) for n in range(self.count)])]
    pallas_call x2 -> x4, Pallas kernels: 6.93 us -> 16 us  [the longest x1 7.22 us: last_sum(): pl.pallas_call(last_sum_kernel, grid=(width // block,), out_shape=jax.Sha...]
    pallas_call x2, Pallas kernels: 40.7 us -> 33.1 us  [backward(): pl.pallas_call(waiting(functools.partial(backward_kernel, tiles, rest, bl...]
    unnamed x113 -> x106, local copies, waits for them, and re-layouts: 7.22 us -> 14.8 us
    ppermute x51 -> x52, starting transfers between devices: 50.2 us -> 47.4 us  [flip(): return lax.ppermute(block, AXES, [(n, n ^ mask) for n in range(self.count)])]
  transfers between devices with their start and end apart: 57 -> 58, of which waited for: 28 -> 27; matrix products, arithmetic and copies ran while one was open for 14% -> 13% of each run, Pallas kernels for 25% -> 24%
where the time goes in v3:
time: 579 us; the launch traced here: 574 us
  Pallas kernels  195 us (34%)
  waiting for transfers between devices  174 us (30%)
  starting transfers between devices  54.3 us (9%)
  matrix products  50.8 us (9%)
  other arithmetic  42 us (7%)
  local copies, waits for them, and re-layouts  39.7 us (7%)
  between operations  17.4 us (3%)
    ppermute x52, waiting for transfers between devices, flip(): return lax.ppermute(block, AXES, [(n, n ^ mask) for n in range(self.count)])  172 us
    pallas_call x2, Pallas kernels, forward(): pl.pallas_call(waiting(functools.partial(forward_kernel, tiles, rest, 2 i...  60.5 us
    pallas_call x3, Pallas kernels, input_gradients(): pl.pallas_call(waiting(input_gradient_kernel, 4, others), grid=(count,),...  54.3 us
    dot_general x2, matrix products, dot_f32(): return lax.dot_general(a, b, (dims, ((), ())), preferred_element_type=F32)  50.8 us
    ppermute x52, starting transfers between devices, flip(): return lax.ppermute(block, AXES, [(n, n ^ mask) for n in range(self.count)])  47.4 us
    pallas_call x2, Pallas kernels, backward(): pl.pallas_call(waiting(functools.partial(backward_kernel, tiles, rest, bl...  33.1 us
    unnamed x106, local copies, waits for them, and re-layouts  14.8 us
    another operation x23, other arithmetic, pair_up(): return [jnp.stack([even[i], sibling[i]]) for i in range(4)]  13.1 us
  transfers between devices with their start and end apart: 58, of which 27 were waited for; matrix products, arithmetic and copies ran while one was open for 13% of the time, Pallas kernels for 24%

profile of v3, /device:TPU:0, one launch (start us, length us, event | category | flops | bytes accessed | tf_op | source)
XLA Modules:
  0.0 573.7 jit_solution(2613268872785140565)
XLA Ops:
  7.3 3.9 pack_weight.1
  18.3 3.9 copied.1.refs_3_.refs_0_
  31.8 10.0 %collective-permute-done.15.refs_2_ = bf16[2,72,1792]{2,1,0:T(8,128)(2,1)S(1)} collective-permute-done((bf16[2,72,1792]{2,1,0:T(8,128)(2,1)S(1)}, bf16[2,72,1792]{2,1,0:T(8,128)(2,1)S(1)}, u32[]{:S(2)}, u32[]{:S(2)}) %collective-permute-start.15) | collective-permute-done | bytes 516128 | tf_op jit(solution)/shard_map/ppermute | solution.py:57
  42.8 6.4 %collective-permute-done.3.refs_1_.refs_5_ = bf16[2,688,128]{2,1,0:T(8,128)(2,1)S(1)} collective-permute-done((bf16[2,688,128]{2,1,0:T(8,128)(2,1)S(1)}, bf16[2,688,128]{2,1,0:T(8,128)(2,1)S(1)}, u32[]{:S(2)}, u32[]{:S(2)}) %collective-permute-start.3) | collective-permute-done | bytes 352288 | tf_op jit(solution)/shard_map/ppermute | solution.py:57
  58.3 6.6 %collective-permute-done.4.refs_2_ = bf16[2,688,128]{2,1,0:T(8,128)(2,1)S(1)} collective-permute-done((bf16[2,688,128]{2,1,0:T(8,128)(2,1)S(1)}, bf16[2,688,128]{2,1,0:T(8,128)(2,1)S(1)}, u32[]{:S(2)}, u32[]{:S(2)}) %collective-permute-start.4) | collective-permute-done | bytes 352288 | tf_op jit(solution)/shard_map/ppermute | solution.py:57
  64.9 8.2 %collective-permute-done.5.refs_3_ = bf16[2,688,128]{2,1,0:T(8,128)(2,1)S(1)} collective-permute-done((bf16[2,688,128]{2,1,0:T(8,128)(2,1)S(1)}, bf16[2,688,128]{2,1,0:T(8,128)(2,1)S(1)}, u32[]{:S(2)}, u32[]{:S(2)}) %collective-permute-start.5) | collective-permute-done | bytes 352288 | tf_op jit(solution)/shard_map/ppermute | solution.py:57
  84.4 5.5 collective-permute-start.14
  92.6 34.5 %collective-permute-done.6.refs_2_ = bf16[512,2304]{1,0:T(8,128)(2,1)} collective-permute-done((bf16[512,2304]{1,0:T(8,128)(2,1)}, bf16[512,2304]{1,0:T(8,128)(2,1)}, u32[]{:S(2)}, u32[]{:S(2)}) %collective-permute-start.6) | collective-permute-done | bytes 2359328 | tf_op jit(solution)/shard_map/ppermute | solution.py:57
  135.0 20.4 %collective-permute-done.10.refs_6_ = bf16[256,2304]{1,0:T(8,128)(2,1)} collective-permute-done((bf16[256,2304]{1,0:T(8,128)(2,1)S(1)}, bf16[256,2304]{1,0:T(8,128)(2,1)}, u32[]{:S(2)}, u32[]{:S(2)}) %collective-permute-start.10) | collective-permute-done | bytes 1179680 | tf_op jit(solution)/shard_map/ppermute | solution.py:57
  155.4 3.8 collective-permute-done.12.refs_8_
  172.3 36.2 %forward.2 = (f32[528,8,512]{2,1,0:T(8,128)}, f32[6,8,128]{2,1,0:T(8,128)}, bf16[8,528,2304]{2,1,0:T(8,128)(2,1)}) custom-call(bf16[512,2304]{1,0:T(8,128)(2,1)} %bitcast.165, bf16[512,2304]{1,0:T(8,128)(2,1)} %collective-permute-done.refs_1_, bf16[512,2304]{1,0:T(8,128)(2,1)} %collective-permute-done.6.refs_2_, ...), custom_call_target="tpu_custom_call" | custom-call | tf_op jit(solution)/shard_map/forward/pallas_call | solution.py:549
  215.6 24.3 %forward.3 = (f32[528,8,384]{2,1,0:T(8,128)}, f32[3,8,128]{2,1,0:T(8,128)}) custom-call(bf16[8,528,2304]{2,1,0:T(8,128)(2,1)} %pad_dynamic-update-slice_fusion.refs_0_, bf16[16,2304]{1,0:T(8,128)(2,1)} %pad.38.refs_10_.refs_1_, bf16[2304,768]{1,0:T(8,128)(2,1)} %all-gather.5.cloned.1.call-done.refs_2_.refs_3_, f32[1,384]{1,0:T(1,128)} %bitcast.179, ...), custom_call_target="tpu_custom_call" | custom-call | tf_op jit(solution)/shard_map/forward/pallas_call | solution.py:549
  240.6 4.0 collective-permute-done.24
  245.6 4.4 collective-permute-done.25
  252.5 20.5 %backward.2 = (bf16[4,528,256]{2,1,0:T(8,128)(2,1)}, bf16[4,528,256]{2,1,0:T(8,128)(2,1)}, bf16[8,528,1024]{2,1,0:T(8,128)(2,1)}, f32[8,512]{1,0:T(8,128)}, f32[8,512]{1,0:T(8,128)}) custom-call(f32[528,8,512]{2,1,0:T(8,128)} %get-tuple-element.59.refs_0_, f32[528,8,128]{2,1,0:T(8,128)} %broadcast_in_dim.511.refs_13_.refs_4_.refs_1_, ...), custom_call_target="tpu_custom_call" | custom-call | tf_op jit(solution)/shard_map/backward/pallas_call | solution.py:723
  274.5 28.1 %bitcast_convert_fusion.refs_7_ = bf16[2304,1024]{1,0:T(8,128)(2,1)} fusion(bf16[8,528,2304]{2,1,0:T(8,128)(2,1)} %pad_dynamic-update-slice_fusion.refs_0_, bf16[8,528,1024]{2,1,0:T(8,128)(2,1)} %pad_dynamic-update-slice_fusion.1.refs_0_), kind=kOutput, calls=%fused_computation.2 | convolution fusion | flops 19933691904 | bytes 32833536 | tf_op jit(solution)/shard_map/dot_general | solution.py:37
  311.7 12.6 %backward.3 = (bf16[4,528,128]{2,1,0:T(8,128)(2,1)}, bf16[4,528,128]{2,1,0:T(8,128)(2,1)}, bf16[8,528,768]{2,1,0:T(8,128)(2,1)}, f32[8,384]{1,0:T(8,128)}, f32[8,384]{1,0:T(8,128)}) custom-call(f32[528,8,384]{2,1,0:T(8,128)} %get-tuple-element.68.refs_0_, f32[528,8,128]{2,1,0:T(8,128)} %broadcast_in_dim.511.refs_13_.refs_4_.refs_1_, ...), custom_call_target="tpu_custom_call" | custom-call | tf_op jit(solution)/shard_map/backward/pallas_call | solution.py:723
  325.7 7.7 %collective-permute-done.28.refs_2_.refs_5_ = bf16[2,528,256]{2,1,0:T(8,128)(2,1)S(1)} collective-permute-done((bf16[2,528,256]{2,1,0:T(8,128)(2,1)}, bf16[2,528,256]{2,1,0:T(8,128)(2,1)S(1)}, u32[]{:S(2)}, u32[]{:S(2)}) %collective-permute-start.28) | collective-permute-done | bytes 540704 | tf_op jit(solution)/shard_map/ppermute | solution.py:57
  335.0 15.0 %input_gradient.3 = (bf16[1,528,2304]{2,1,0:T(8,128)(2,1)}, bf16[1,528,2304]{2,1,0:T(8,128)(2,1)}) custom-call(bf16[8,528,1024]{2,1,0:T(8,128)(2,1)} %pad_dynamic-update-slice_fusion.1.refs_0_, bf16[8,528,768]{2,1,0:T(8,128)(2,1)} %pad_dynamic-update-slice_fusion.2.refs_1_.refs_0_, bf16[2304,1024]{1,0:T(8,128)(2,1)} %all-gather.3.cloned.1.call-done.refs_11_.refs_2_, ...), custom_call_target="tpu_custom_call" | custom-call | tf_op jit(solution)/shard_map/input_gradient/pallas_call | solution.py:774
  351.7 4.0 collective-permute-done.30
  363.5 5.5 far_sum.1
  372.8 22.6 %bitcast_convert_fusion.1.refs_0_ = bf16[2304,768]{1,0:T(8,128)(2,1)} fusion(bf16[8,528,2304]{2,1,0:T(8,128)(2,1)} %pad_dynamic-update-slice_fusion.refs_0_, bf16[8,528,768]{2,1,0:T(8,128)(2,1)} %after.27.refs_1_), kind=kOutput, calls=%fused_computation.3 | convolution fusion | flops 14950268928 | bytes 29491200 | tf_op jit(solution)/shard_map/dot_general | solution.py:37
  400.4 24.2 %input_gradient.4 = (bf16[2,528,2304]{2,1,0:T(8,128)(2,1)}, bf16[2,528,2304]{2,1,0:T(8,128)(2,1)}) custom-call(bf16[8,528,1024]{2,1,0:T(8,128)(2,1)} %pad_dynamic-update-slice_fusion.1.refs_0_, bf16[8,528,768]{2,1,0:T(8,128)(2,1)} %after.27.refs_1_, bf16[2304,1024]{1,0:T(8,128)(2,1)} %all-gather.3.cloned.1.call-done.refs_11_.refs_2_, ...), custom_call_target="tpu_custom_call" | custom-call | tf_op jit(solution)/shard_map/input_gradient/pallas_call | solution.py:774
  424.6 8.5 %collective-permute-done.37.odd_ref = bf16[2,528,2304]{2,1,0:T(8,128)(2,1)} collective-permute-done((bf16[2,528,2304]{2,1,0:T(8,128)(2,1)}, bf16[2,528,2304]{2,1,0:T(8,128)(2,1)}, u32[]{:S(2)}, u32[]{:S(2)}) %collective-permute-start.37) | collective-permute-done | bytes 4866080 | tf_op jit(solution)/shard_map/ppermute | solution.py:57
  433.1 7.9 %near_sums.1 = (bf16[256,2304]{1,0:T(8,128)(2,1)}, bf16[272,2304]{1,0:T(8,128)(2,1)}, bf16[256,2304]{1,0:T(8,128)(2,1)}, bf16[272,2304]{1,0:T(8,128)(2,1)}) custom-call(bf16[2,528,2304]{2,1,0:T(8,128)(2,1)} %get-tuple-element.81.even_ref, bf16[2,528,2304]{2,1,0:T(8,128)(2,1)} %collective-permute-done.37.odd_ref, bf16[256,2304]{1,0:T(8,128)(2,1)} %copy-done.9, ...), custom_call_target="tpu_custom_call" | custom-call | tf_op jit(solution)/shard_map/near_sums/pallas_call | solution.py:828
  445.0 4.3 place_channels.1
  449.3 15.0 %input_gradient.5 = (bf16[1,528,2304]{2,1,0:T(8,128)(2,1)}, bf16[1,528,2304]{2,1,0:T(8,128)(2,1)}) custom-call(bf16[8,528,1024]{2,1,0:T(8,128)(2,1)} %pad_dynamic-update-slice_fusion.1.refs_0_, bf16[8,528,768]{2,1,0:T(8,128)(2,1)} %after.27.refs_1_, bf16[2304,1024]{1,0:T(8,128)(2,1)} %all-gather.3.cloned.1.call-done.refs_11_.refs_2_, ...), custom_call_target="tpu_custom_call" | custom-call | tf_op jit(solution)/shard_map/input_gradient/pallas_call | solution.py:774
  464.4 6.5 %collective-permute-done.41.refs_2_.y_high = bf16[272,2304]{1,0:T(8,128)(2,1)S(1)} collective-permute-done((bf16[272,2304]{1,0:T(8,128)(2,1)}, bf16[272,2304]{1,0:T(8,128)(2,1)S(1)}, u32[]{:S(2)}, u32[]{:S(2)}) %collective-permute-start.41) | collective-permute-done | bytes 1253408 | tf_op jit(solution)/shard_map/ppermute | solution.py:57
  497.9 27.0 %collective-permute-done.50.refs_3_ = bf16[2,72,1792]{2,1,0:T(8,128)(2,1)S(1)} collective-permute-done((bf16[2,72,1792]{2,1,0:T(8,128)(2,1)}, bf16[2,72,1792]{2,1,0:T(8,128)(2,1)S(1)}, u32[]{:S(2)}, u32[]{:S(2)}) %collective-permute-start.50) | collective-permute-done | bytes 516128 | tf_op jit(solution)/shard_map/ppermute | solution.py:57
  526.7 7.6 %collective-permute-done.49.refs_2_ = bf16[2,72,1792]{2,1,0:T(8,128)(2,1)S(1)} collective-permute-done((bf16[2,72,1792]{2,1,0:T(8,128)(2,1)}, bf16[2,72,1792]{2,1,0:T(8,128)(2,1)S(1)}, u32[]{:S(2)}, u32[]{:S(2)}) %collective-permute-start.49) | collective-permute-done | bytes 516128 | tf_op jit(solution)/shard_map/ppermute | solution.py:57
  544.1 7.2 %last_sum.1 = bf16[512,2304]{1,0:T(8,128)(2,1)} custom-call(bf16[1,528,2304]{2,1,0:T(8,128)(2,1)} %get-tuple-element.84.refs_1_.even_ref, bf16[1,528,2304]{2,1,0:T(8,128)(2,1)} %copy-done.13, bf16[256,2304]{1,0:T(8,128)(2,1)} %collective-permute-done.39.y_low, bf16[256,2304]{1,0:T(8,128)(2,1)} %collective-permute-done.40.x_low, bf16[272,2304]{1,0:T(8,128)(2,1)} %copy-done.3, ...), custom_call_target="tpu_custom_call" | custom-call | tf_op jit(solution)/shard_map/last_sum/pallas_call | solution.py:854
  556.9 8.9 %multiply_subtract_fusion = (f32[2,72,6912]{2,1,0:T(8,128)}, f32[2,72,6912]{2,1,0:T(8,128)}, f32[2,72,6912]{2,1,0:T(8,128)}, f32[2,72,6912]{2,1,0:T(8,128)}) fusion(f32[2,72,6912]{2,1,0:T(8,128)} %weight_ref.1, f32[2,72,6912]{2,1,0:T(8,128)} %param.20, f32[2,72,6912]{2,1,0:T(8,128)} %param.21, bf16[2,72,6912]{2,1,0:T(8,128)(2,1)S(1)} %copy-done.7, f32[]{:T(128)S(6)} %min.3), kind=kLoop, calls=%fused_computation.6 | loop fusion | flops 16920576 | bytes 29859844 | tf_op jit(solution)/shard_map/sub | solution.py:873
  (368 shorter events, 151.2 us)
Async XLA Ops:
  7.2 163.1 %all-gather.3.cloned.1.call-start = ((), (), s32[]{:S(2)}) async-start(), calls=%async_computation.2 | async-start | bytes 5898240 | tf_op jit(solution)/shard_map/all_gather | solution.py:922
  14.7 27.3 %collective-permute-start.17 = (bf16[2,72,1792]{2,1,0:T(8,128)(2,1)S(1)}, bf16[2,72,1792]{2,1,0:T(8,128)(2,1)}, u32[]{:S(2)}, u32[]{:S(2)}) collective-permute-start(bf16[2,72,1792]{2,1,0:T(8,128)(2,1)S(1)} %pad_maximum_fusion.5.refs_1_.refs_4_), channel_id=1, source_target_pairs={{0,6},{1,7},{2,4},{3,5},{4,2},{5,3},{6,0},{7,1},{8,14},{9,15},{10,... | collective-permute-start | bytes 1548296 | tf_op jit(solution)/shard_map/ppermute | solution.py:57
  29.9 19.4 %collective-permute-start.3 = (bf16[2,688,128]{2,1,0:T(8,128)(2,1)S(1)}, bf16[2,688,128]{2,1,0:T(8,128)(2,1)S(1)}, u32[]{:S(2)}, u32[]{:S(2)}) collective-permute-start(bf16[2,688,128]{2,1,0:T(8,128)(2,1)S(1)} %pad_maximum_fusion.13), channel_id=1, source_target_pairs={{0,2},{1,3},{2,0},{3,1},{4,6},{5,7},{6,4},{7,5},{8,10},{9,11},{10,... | collective-permute-start | bytes 1056776 | tf_op jit(solution)/shard_map/ppermute | solution.py:57
  53.0 162.6 %all-gather.5.cloned.1.call-start = ((), (), s32[]{:S(2)}) async-start(), calls=%async_computation.3 | async-start | bytes 4423680 | tf_op jit(solution)/shard_map/all_gather | solution.py:922
  53.0 113.1 %collective-permute-start = (bf16[512,2304]{1,0:T(8,128)(2,1)}, bf16[512,2304]{1,0:T(8,128)(2,1)}, u32[]{:S(2)}, u32[]{:S(2)}) collective-permute-start(bf16[512,2304]{1,0:T(8,128)(2,1)} %bitcast.164), channel_id=1, source_target_pairs={{0,1},{1,0},{2,3},{3,2},{4,5},{5,4},{6,7},{7,6},{8,9},{9,8},{10,11... | collective-permute-start | bytes 7077896 | tf_op jit(solution)/shard_map/ppermute | solution.py:57
  55.6 17.5 %collective-permute-start.5 = (bf16[2,688,128]{2,1,0:T(8,128)(2,1)S(1)}, bf16[2,688,128]{2,1,0:T(8,128)(2,1)S(1)}, u32[]{:S(2)}, u32[]{:S(2)}) collective-permute-start(bf16[2,688,128]{2,1,0:T(8,128)(2,1)S(1)} %pad_maximum_fusion.15), channel_id=1, source_target_pairs={{0,6},{1,7},{2,4},{3,5},{4,2},{5,3},{6,0},{7,1},{8,14},{9,15},{10,... | collective-permute-start | bytes 1056776 | tf_op jit(solution)/shard_map/ppermute | solution.py:57
  73.9 53.2 %collective-permute-start.6 = (bf16[512,2304]{1,0:T(8,128)(2,1)}, bf16[512,2304]{1,0:T(8,128)(2,1)}, u32[]{:S(2)}, u32[]{:S(2)}) collective-permute-start(bf16[512,2304]{1,0:T(8,128)(2,1)} %after.17), channel_id=1, source_target_pairs={{0,2},{1,3},{2,0},{3,1},{4,6},{5,7},{6,4},{7,5},{8,10},{9,11},{10,... | collective-permute-start | bytes 7077896 | tf_op jit(solution)/shard_map/ppermute | solution.py:57
  74.2 55.8 %collective-permute-start.8 = (bf16[512,2304]{1,0:T(8,128)(2,1)}, bf16[512,2304]{1,0:T(8,128)(2,1)}, u32[]{:S(2)}, u32[]{:S(2)}) collective-permute-start(bf16[512,2304]{1,0:T(8,128)(2,1)} %after.17), channel_id=1, source_target_pairs={{0,4},{1,5},{2,6},{3,7},{4,0},{5,1},{6,2},{7,3},{8,12},{9,13},{10,... | collective-permute-start | bytes 7077896 | tf_op jit(solution)/shard_map/ppermute | solution.py:57
  79.7 315.6 %reduce-scatter.3.cloned.1.call-start = ((), (), s32[]{:S(2)}) async-start(), calls=%async_computation.4 | async-start | bytes 5898240 | tf_op jit(solution)/shard_map/reduce_scatter | solution.py:1045
  92.6 41.9 %collective-permute-start.20 = (bf16[4,528,128]{2,1,0:T(8,128)(2,1)}, bf16[4,528,128]{2,1,0:T(8,128)(2,1)}, u32[]{:S(2)}, u32[]{:S(2)}) collective-permute-start(bf16[4,528,128]{2,1,0:T(8,128)(2,1)} %after.18), channel_id=1, source_target_pairs={{0,1},{1,0},{2,3},{3,2},{4,5},{5,4},{6,7},{7,6},{8,9},{9,8},{10,11... | collective-permute-start | bytes 1622024 | tf_op jit(solution)/shard_map/ppermute | solution.py:57
  128.5 26.9 %collective-permute-start.10 = (bf16[256,2304]{1,0:T(8,128)(2,1)S(1)}, bf16[256,2304]{1,0:T(8,128)(2,1)}, u32[]{:S(2)}, u32[]{:S(2)}) collective-permute-start(bf16[256,2304]{1,0:T(8,128)(2,1)S(1)} %slice.974), channel_id=1, source_target_pairs={{0,4},{1,5},{2,6},{3,7},{4,0},{5,1},{6,2},{7,3},{8,12},{9,13},{10,... | collective-permute-start | bytes 3538952 | tf_op jit(solution)/shard_map/ppermute | solution.py:57
  132.4 26.8 %collective-permute-start.12 = (bf16[256,2304]{1,0:T(8,128)(2,1)}, bf16[256,2304]{1,0:T(8,128)(2,1)}, u32[]{:S(2)}, u32[]{:S(2)}) collective-permute-start(bf16[256,2304]{1,0:T(8,128)(2,1)} %slice.975), channel_id=1, source_target_pairs={{0,2},{1,3},{2,0},{3,1},{4,6},{5,7},{6,4},{7,5},{8,10},{9,11},{10,... | collective-permute-start | bytes 3538952 | tf_op jit(solution)/shard_map/ppermute | solution.py:57
  134.5 35.9 %collective-permute-start.7 = (bf16[512,2304]{1,0:T(8,128)(2,1)}, bf16[512,2304]{1,0:T(8,128)(2,1)}, u32[]{:S(2)}, u32[]{:S(2)}) collective-permute-start(bf16[512,2304]{1,0:T(8,128)(2,1)} %collective-permute-done.6.refs_2_), channel_id=1, source_target_pairs={{0,1},{1,0},{2,3},{3,2},{4,5},{5,4},{6,7},{7,6},{8,9},{9,8},{10,11... | collective-permute-start | bytes 7077896 | tf_op jit(solution)/shard_map/ppermute | solution.py:57
  134.5 35.9 %collective-permute-start.9 = (bf16[512,2304]{1,0:T(8,128)(2,1)}, bf16[512,2304]{1,0:T(8,128)(2,1)}, u32[]{:S(2)}, u32[]{:S(2)}) collective-permute-start(bf16[512,2304]{1,0:T(8,128)(2,1)} %collective-permute-done.8.refs_4_), channel_id=1, source_target_pairs={{0,1},{1,0},{2,3},{3,2},{4,5},{5,4},{6,7},{7,6},{8,9},{9,8},{10,11... | collective-permute-start | bytes 7077896 | tf_op jit(solution)/shard_map/ppermute | solution.py:57
  165.3 43.2 %collective-permute-start.21 = (bf16[2,528,128]{2,1,0:T(8,128)(2,1)}, bf16[2,528,128]{2,1,0:T(8,128)(2,1)S(1)}, u32[]{:S(2)}, u32[]{:S(2)}) collective-permute-start(bf16[2,528,128]{2,1,0:T(8,128)(2,1)} %after.21), channel_id=1, source_target_pairs={{0,2},{1,3},{2,0},{3,1},{4,6},{5,7},{6,4},{7,5},{8,10},{9,11},{10,... | collective-permute-start | bytes 811016 | tf_op jit(solution)/shard_map/ppermute | solution.py:57
  165.8 43.4 %collective-permute-start.22 = (bf16[2,528,128]{2,1,0:T(8,128)(2,1)}, bf16[2,528,128]{2,1,0:T(8,128)(2,1)S(1)}, u32[]{:S(2)}, u32[]{:S(2)}) collective-permute-start(bf16[2,528,128]{2,1,0:T(8,128)(2,1)} %after.23), channel_id=1, source_target_pairs={{0,4},{1,5},{2,6},{3,7},{4,0},{5,1},{6,2},{7,3},{8,12},{9,13},{10,... | collective-permute-start | bytes 811016 | tf_op jit(solution)/shard_map/ppermute | solution.py:57
  166.2 43.7 %collective-permute-start.23 = (bf16[2,528,128]{2,1,0:T(8,128)(2,1)}, bf16[2,528,128]{2,1,0:T(8,128)(2,1)S(1)}, u32[]{:S(2)}, u32[]{:S(2)}) collective-permute-start(bf16[2,528,128]{2,1,0:T(8,128)(2,1)} %after.25), channel_id=1, source_target_pairs={{0,6},{1,7},{2,4},{3,5},{4,2},{5,3},{6,0},{7,1},{8,14},{9,15},{10,... | collective-permute-start | bytes 811016 | tf_op jit(solution)/shard_map/ppermute | solution.py:57
  302.6 170.0 %reduce-scatter.5.cloned.1.call-start = ((), (), s32[]{:S(2)}) async-start(), calls=%async_computation.5 | async-start | bytes 4423680 | tf_op jit(solution)/shard_map/reduce_scatter | solution.py:1045
  306.5 19.2 %collective-permute-start.29 = (bf16[2,528,256]{2,1,0:T(8,128)(2,1)S(1)}, bf16[2,528,256]{2,1,0:T(8,128)(2,1)S(1)}, u32[]{:S(2)}, u32[]{:S(2)}) collective-permute-start(bf16[2,528,256]{2,1,0:T(8,128)(2,1)S(1)} %pad_maximum_fusion.4), channel_id=1, source_target_pairs={{0,6},{1,7},{2,4},{3,5},{4,2},{5,3},{6,0},{7,1},{8,14},{9,15},{10,... | collective-permute-start | bytes 1622024 | tf_op jit(solution)/shard_map/ppermute | solution.py:57
  309.8 23.6 %collective-permute-start.28 = (bf16[2,528,256]{2,1,0:T(8,128)(2,1)}, bf16[2,528,256]{2,1,0:T(8,128)(2,1)S(1)}, u32[]{:S(2)}, u32[]{:S(2)}) collective-permute-start(bf16[2,528,256]{2,1,0:T(8,128)(2,1)} %pad_maximum_fusion.3), channel_id=1, source_target_pairs={{0,4},{1,5},{2,6},{3,7},{4,0},{5,1},{6,2},{7,3},{8,12},{9,13},{10,... | collective-permute-start | bytes 1622024 | tf_op jit(solution)/shard_map/ppermute | solution.py:57
  310.4 23.0 %collective-permute-start.27 = (bf16[2,528,256]{2,1,0:T(8,128)(2,1)S(1)}, bf16[2,528,256]{2,1,0:T(8,128)(2,1)S(1)}, u32[]{:S(2)}, u32[]{:S(2)}) collective-permute-start(bf16[2,528,256]{2,1,0:T(8,128)(2,1)S(1)} %pad_maximum_fusion.2), channel_id=1, source_target_pairs={{0,2},{1,3},{2,0},{3,1},{4,6},{5,7},{6,4},{7,5},{8,10},{9,11},{10,... | collective-permute-start | bytes 1622024 | tf_op jit(solution)/shard_map/ppermute | solution.py:57
  369.0 30.4 %collective-permute-start.36 = (bf16[272,2304]{1,0:T(8,128)(2,1)}, bf16[272,2304]{1,0:T(8,128)(2,1)S(1)}, u32[]{:S(2)}, u32[]{:S(2)}) collective-permute-start(bf16[272,2304]{1,0:T(8,128)(2,1)} %get-tuple-element.80), channel_id=1, source_target_pairs={{0,2},{1,3},{2,0},{3,1},{4,6},{5,7},{6,4},{7,5},{8,10},{9,11},{10,... | collective-permute-start | bytes 3760136 | tf_op jit(solution)/shard_map/ppermute | solution.py:57
  369.5 27.5 %collective-permute-start.35 = (bf16[256,2304]{1,0:T(8,128)(2,1)}, bf16[256,2304]{1,0:T(8,128)(2,1)S(1)}, u32[]{:S(2)}, u32[]{:S(2)}) collective-permute-start(bf16[256,2304]{1,0:T(8,128)(2,1)} %get-tuple-element.79.refs_1_), channel_id=1, source_target_pairs={{0,4},{1,5},{2,6},{3,7},{4,0},{5,1},{6,2},{7,3},{8,12},{9,13},{10,... | collective-permute-start | bytes 3538952 | tf_op jit(solution)/shard_map/ppermute | solution.py:57
  441.0 29.9 %collective-permute-start.41 = (bf16[272,2304]{1,0:T(8,128)(2,1)}, bf16[272,2304]{1,0:T(8,128)(2,1)S(1)}, u32[]{:S(2)}, u32[]{:S(2)}) collective-permute-start(bf16[272,2304]{1,0:T(8,128)(2,1)} %get-tuple-element.83.refs_4_), channel_id=1, source_target_pairs={{0,2},{1,3},{2,0},{3,1},{4,6},{5,7},{6,4},{7,5},{8,10},{9,11},{10,... | collective-permute-start | bytes 3760136 | tf_op jit(solution)/shard_map/ppermute | solution.py:57
  442.0 29.6 %collective-permute-start.42 = (bf16[272,2304]{1,0:T(8,128)(2,1)}, bf16[272,2304]{1,0:T(8,128)(2,1)S(1)}, u32[]{:S(2)}, u32[]{:S(2)}) collective-permute-start(bf16[272,2304]{1,0:T(8,128)(2,1)} %get-tuple-element.88), channel_id=1, source_target_pairs={{0,4},{1,5},{2,6},{3,7},{4,0},{5,1},{6,2},{7,3},{8,12},{9,13},{10,... | collective-permute-start | bytes 3760136 | tf_op jit(solution)/shard_map/ppermute | solution.py:57
  475.9 19.7 %collective-permute-start.38 = (bf16[1,528,2304]{2,1,0:T(8,128)(2,1)}, bf16[1,528,2304]{2,1,0:T(8,128)(2,1)S(1)}, u32[]{:S(2)}, u32[]{:S(2)}) collective-permute-start(bf16[1,528,2304]{2,1,0:T(8,128)(2,1)} %get-tuple-element.85), channel_id=1, source_target_pairs={{0,1},{1,0},{2,3},{3,2},{4,5},{5,4},{6,7},{7,6},{8,9},{9,8},{10,11... | collective-permute-start | bytes 7299080 | tf_op jit(solution)/shard_map/ppermute | solution.py:57
  483.2 60.9 %collective-permute-start.39 = (bf16[256,2304]{1,0:T(8,128)(2,1)}, bf16[256,2304]{1,0:T(8,128)(2,1)}, u32[]{:S(2)}, u32[]{:S(2)}) collective-permute-start(bf16[256,2304]{1,0:T(8,128)(2,1)} %get-tuple-element.86), channel_id=1, source_target_pairs={{0,2},{1,3},{2,0},{3,1},{4,6},{5,7},{6,4},{7,5},{8,10},{9,11},{10,... | collective-permute-start | bytes 3538952 | tf_op jit(solution)/shard_map/ppermute | solution.py:57
  484.5 59.6 %collective-permute-start.40 = (bf16[256,2304]{1,0:T(8,128)(2,1)}, bf16[256,2304]{1,0:T(8,128)(2,1)}, u32[]{:S(2)}, u32[]{:S(2)}) collective-permute-start(bf16[256,2304]{1,0:T(8,128)(2,1)} %get-tuple-element.87), channel_id=1, source_target_pairs={{0,4},{1,5},{2,6},{3,7},{4,0},{5,1},{6,2},{7,3},{8,12},{9,13},{10,... | collective-permute-start | bytes 3538952 | tf_op jit(solution)/shard_map/ppermute | solution.py:57
  493.6 31.3 %collective-permute-start.50 = (bf16[2,72,1792]{2,1,0:T(8,128)(2,1)}, bf16[2,72,1792]{2,1,0:T(8,128)(2,1)S(1)}, u32[]{:S(2)}, u32[]{:S(2)}) collective-permute-start(bf16[2,72,1792]{2,1,0:T(8,128)(2,1)} %pad_maximum_fusion.11.refs_3_), channel_id=1, source_target_pairs={{0,6},{1,7},{2,4},{3,5},{4,2},{5,3},{6,0},{7,1},{8,14},{9,15},{10,... | collective-permute-start | bytes 1548296 | tf_op jit(solution)/shard_map/ppermute | solution.py:57
  495.6 38.7 %collective-permute-start.49 = (bf16[2,72,1792]{2,1,0:T(8,128)(2,1)}, bf16[2,72,1792]{2,1,0:T(8,128)(2,1)S(1)}, u32[]{:S(2)}, u32[]{:S(2)}) collective-permute-start(bf16[2,72,1792]{2,1,0:T(8,128)(2,1)} %pad_maximum_fusion.10.refs_2_), channel_id=1, source_target_pairs={{0,4},{1,5},{2,6},{3,7},{4,0},{5,1},{6,2},{7,3},{8,12},{9,13},{10,... | collective-permute-start | bytes 1548296 | tf_op jit(solution)/shard_map/ppermute | solution.py:57
  496.1 38.2 %collective-permute-start.48 = (bf16[2,72,1792]{2,1,0:T(8,128)(2,1)}, bf16[2,72,1792]{2,1,0:T(8,128)(2,1)}, u32[]{:S(2)}, u32[]{:S(2)}) collective-permute-start(bf16[2,72,1792]{2,1,0:T(8,128)(2,1)} %pad_maximum_fusion.9.refs_1_), channel_id=1, source_target_pairs={{0,2},{1,3},{2,0},{3,1},{4,6},{5,7},{6,4},{7,5},{8,10},{9,11},{10,... | collective-permute-start | bytes 1548296 | tf_op jit(solution)/shard_map/ppermute | solution.py:57
  535.1 16.2 %collective-permute-start.51 = (f32[2,1024]{1,0:T(2,128)}, f32[2,1024]{1,0:T(2,128)S(1)}, u32[]{:S(2)}, u32[]{:S(2)}) collective-permute-start(f32[2,1024]{1,0:T(2,128)} %after.32.refs_1_), channel_id=1, source_target_pairs={{0,2},{1,3},{2,0},{3,1},{4,6},{5,7},{6,4},{7,5},{8,10},{9,11},{10,... | collective-permute-start | bytes 24584 | tf_op jit(solution)/shard_map/ppermute | solution.py:57
  (76 other events, 674.4 us)
Sparse Core Ops, SparseCore 0:
  53.1 91.2 all-gather.2
  146.5 69.0 all-gather.4
  302.7 83.6 reduce-scatter.2
  395.5 64.6 reduce-scatter.4

commit v4 on v3

--- a/solution.py
+++ b/solution.py
@@ -60,11 +60,17 @@
         return (p & 3) | ((p >> 2) * self.n_stream)
 
     def gather_flips(self, block, bits):
+        if len(bits) == 2:
+            parts = [self.flip(block, mask) for mask in (bits[0], bits[1], bits[0] | bits[1])]
+            return jnp.concatenate([block, *parts], axis=0)
         for bit in bits:
             block = jnp.concatenate([block, self.flip(block, bit)], axis=0)
         return block
 
     def sum_flips(self, value, bits):
+        if len(bits) == 2:
+            parts = [self.flip(value, mask) for mask in (bits[0], bits[1], bits[0] | bits[1])]
+            return (value + parts[0]) + (parts[1] + parts[2])
         for bit in bits:
             value = value + self.flip(value, bit)
         return value
@@ -773,15 +779,16 @@
     shape = jax.ShapeDtypeStruct((count, length, width), BF16)
     return pl.pallas_call(
         waiting(input_gradient_kernel, 4, others),
-        grid=(count,),
+        grid=(3, count),
         out_shape=(shape, shape),
         in_specs=[
-            pl.BlockSpec((2, length, first.shape[2]), lambda i: (start + i, 0, 0)),
-            pl.BlockSpec((2, length, second.shape[2]), lambda i: (start + i, 0, 0)),
-            *in_vmem(2),
+            pl.BlockSpec((2, length, first.shape[2]), lambda n, i: (start + i, 0, 0)),
+            pl.BlockSpec((2, length, second.shape[2]), lambda n, i: (start + i, 0, 0)),
+            pl.BlockSpec((width // 3, first.shape[2]), lambda n, i: (n, 0)),
+            pl.BlockSpec((width // 3, second.shape[2]), lambda n, i: (n, 0)),
             *unseen(others),
         ],
-        out_specs=(pl.BlockSpec((1, length, width), lambda i: (i, 0, 0)),) * 2,
+        out_specs=(pl.BlockSpec((1, length, width // 3), lambda n, i: (i, 0, n)),) * 2,
         compiler_params=params(),
         name="input_gradient",
     )(first, second, w_first, w_second, *others)
@@ -811,26 +818,29 @@
 
 
 def near_sums_kernel(even_ref, odd_ref, low_ref, high_ref, y_low, y_high, x_low, x_high):
-    middle = low_ref.shape[0]
+    middle, cut = low_ref.shape[0], y_low.shape[0]
+    assert cut == middle
     total = even_ref[0].astype(F32) + odd_ref[0].astype(F32)
-    y_low[...] = (total[:middle] + low_ref[...].astype(F32)).astype(BF16)
+    first = total[:middle] + low_ref[...].astype(F32)
+    y_low[...] = first[:cut].astype(BF16)
     y_high[...] = total[middle:].astype(BF16)
     total = even_ref[1].astype(F32) + odd_ref[1].astype(F32)
-    x_low[...] = total[:middle].astype(BF16)
+    x_low[...] = total[:cut].astype(BF16)
     x_high[...] = (total[middle:] + high_ref[...].astype(F32)).astype(BF16)
 
 
-def near_sums(even, odd, low, high):
+def near_sums(even, odd, low, high, cut):
     _, length, width = even.shape
     block = 384
     spec = pl.BlockSpec((2, length, block), lambda i: (0, 0, i))
-    halves = [pl.BlockSpec((part.shape[0], block), lambda i: (0, i)) for part in (low, high)]
+    halves = [pl.BlockSpec((rows, block), lambda i: (0, i)) for rows in (low.shape[0], high.shape[0])]
+    parts = [cut, length - cut]
     return pl.pallas_call(
         near_sums_kernel,
         grid=(width // block,),
-        out_shape=[jax.ShapeDtypeStruct(part.shape, BF16) for part in (low, high, low, high)],
+        out_shape=[jax.ShapeDtypeStruct((rows, width), BF16) for rows in parts * 2],
         in_specs=[spec, spec] + halves,
-        out_specs=halves * 2,
+        out_specs=[pl.BlockSpec((rows, block), lambda i: (0, i)) for rows in parts * 2],
         compiler_params=params(),
         name="near_sums",
     )(even, odd, low, high)
@@ -932,7 +942,7 @@
     packed_cot = pack_channels(cotangent[0], small, marks, member, own_copy, weight_pairs[3])
     cot_first = here.pair_up(*packed_cot[:2])
     got_first = here.send_pairs(cot_first)
-    placed = place_weight(weight_got, member, 8 * LANES, got_first[1])
+    placed = place_weight(weight_got, member, 8 * LANES, *cot_first[1:])
     weights = [all_rows(part) for part in placed]
     own_sibling = here.flip(own, 1)
     sent = after(own_copy, *got_first[1:])
@@ -1053,8 +1063,7 @@
     high_half = here.flip(far_high, here.member_mask(2))
     grads = outs[0][2], outs[1][2]
     even, odd = back_pairs(*grads, 1, 2, low_half, high_half, outs[1][4], gradients[0])
-    y_low, y_high, x_low, x_high = near_sums(even, odd, low_half, high_half)
-    lows = here.flip(y_low, here.member_mask(2)), here.flip(x_low, here.member_mask(4))
+    y_low, y_high, x_low, x_high = near_sums(even, odd, low_half, high_half, halfway)
     highs = here.flip(y_high, here.member_mask(2)), here.flip(x_high, here.member_mask(4))
     hidden_own, final_rows = place_channels(hidden_got, member, width)
     hidden = hidden_own[None]
@@ -1065,7 +1074,8 @@
     gradients = [after(gradient, even, *highs) for gradient in gradients]
     *picked, squares = pick_rows(*gradients, member)
     post_pairs = here.pair_up(*picked)
-    edge_sum = sum(part[tokens - halfway : tokens - halfway + 1].astype(F32) for part in (even[0, halfway:], odd[0, halfway:], *highs))
+    edge_parts = even[0, tokens : tokens + 1], odd[0, tokens : tokens + 1], *(part[-TAIL : 1 - TAIL] for part in highs)
+    edge_sum = sum(part.astype(F32) for part in edge_parts)
     from_next = lax.ppermute(edge_sum, "seq", [(i + 1, i) for i in range(here.n_seq - 1)])
     received = here.send_pairs(post_pairs)
 
@@ -1073,6 +1083,8 @@
     vector = here.sum_flips(after(vector, *post_pairs[1:]), here.deep_bits + here.wide_bits)
     vector = here.gather_flips(vector, here.group_bits[:1])
     vector = after(vector, *received[1:])
+    y_low, x_low = after(y_low, *received[1:]), after(x_low, *received[1:])
+    lows = here.flip(y_low, here.member_mask(2)), here.flip(x_low, here.member_mask(4))
     from_next = after(from_next, vector)
     input_gradient = last_sum(even, odd, lows, highs, from_next, tokens)[None]
     vectors = [vector] + [here.flip(vector, here.member_mask(2 * i)) for i in (1, 2, 3)]

time: 579 us -> 560 us (0.967)
  waiting for transfers between devices: 174 us -> 146 us
    ppermute x52 -> x55, waiting for transfers between devices: 172 us -> 145 us  [flip(): return lax.ppermute(block, AXES, [(n, n ^ mask) for n in range(self.count)])]
    ppermute x52 -> x55, starting transfers between devices: 47.4 us -> 53.7 us  [flip(): return lax.ppermute(block, AXES, [(n, n ^ mask) for n in range(self.count)])]
    unnamed x106 -> x136, local copies, waits for them, and re-layouts: 14.8 us -> 16.2 us
  transfers between devices with their start and end apart: 58 -> 61, of which waited for: 27 -> 28; matrix products, arithmetic and copies ran while one was open for 13% -> 17% of each run, Pallas kernels for 24% -> 23%
where the time goes in v4:
time: 560 us; the launch traced here: 554 us
  Pallas kernels  192 us (34%)
  waiting for transfers between devices  146 us (26%)
  starting transfers between devices  58.5 us (10%)
  matrix products  50.3 us (9%)
  local copies, waits for them, and re-layouts  45.3 us (8%)
  other arithmetic  45 us (8%)
  between operations  17.5 us (3%)
    ppermute x55, waiting for transfers between devices, flip(): return lax.ppermute(block, AXES, [(n, n ^ mask) for n in range(self.count)])  145 us
    pallas_call x2, Pallas kernels, forward(): pl.pallas_call(waiting(functools.partial(forward_kernel, tiles, rest, 2 i...  60.5 us
    ppermute x55, starting transfers between devices, flip(): return lax.ppermute(block, AXES, [(n, n ^ mask) for n in range(self.count)])  53.7 us
    pallas_call x3, Pallas kernels, input_gradients(): pl.pallas_call(waiting(input_gradient_kernel, 4, others), grid=(3, count)...  50.9 us
    dot_general x2, matrix products, dot_f32(): return lax.dot_general(a, b, (dims, ((), ())), preferred_element_type=F32)  50.3 us
    pallas_call x2, Pallas kernels, backward(): pl.pallas_call(waiting(functools.partial(backward_kernel, tiles, rest, bl...  33.3 us
    another operation x23, other arithmetic, pair_up(): return [jnp.stack([even[i], sibling[i]]) for i in range(4)]  16.2 us
    unnamed x136, local copies, waits for them, and re-layouts  16.2 us
  transfers between devices with their start and end apart: 61, of which 28 were waited for; matrix products, arithmetic and copies ran while one was open for 17% of the time, Pallas kernels for 23%

profile of v4, /device:TPU:0, one launch (start us, length us, event | category | flops | bytes accessed | tf_op | source)
XLA Modules:
  0.0 554.4 jit_solution(7387112821902868600)
XLA Ops:
  7.3 3.9 pack_weight.1
  18.3 3.9 copied.1.refs_3_.refs_0_
  22.1 3.6 pack_channels.1
  31.1 10.6 %collective-permute-done.15.refs_2_ = bf16[2,72,1792]{2,1,0:T(8,128)(2,1)S(1)} collective-permute-done((bf16[2,72,1792]{2,1,0:T(8,128)(2,1)S(1)}, bf16[2,72,1792]{2,1,0:T(8,128)(2,1)S(1)}, u32[]{:S(2)}, u32[]{:S(2)}) %collective-permute-start.15) | collective-permute-done | bytes 516128 | tf_op jit(solution)/shard_map/ppermute | solution.py:57
  51.6 5.0 collective-permute-done.3.refs_1_
  58.8 6.1 %collective-permute-done.5.refs_3_ = bf16[2,688,128]{2,1,0:T(8,128)(2,1)S(1)} collective-permute-done((bf16[2,688,128]{2,1,0:T(8,128)(2,1)S(1)}, bf16[2,688,128]{2,1,0:T(8,128)(2,1)S(1)}, u32[]{:S(2)}, u32[]{:S(2)}) %collective-permute-start.5) | collective-permute-done | bytes 352288 | tf_op jit(solution)/shard_map/ppermute | solution.py:57
  71.9 3.7 collective-permute-start.20
  85.7 32.3 %collective-permute-done.6.refs_2_ = bf16[512,2304]{1,0:T(8,128)(2,1)} collective-permute-done((bf16[512,2304]{1,0:T(8,128)(2,1)}, bf16[512,2304]{1,0:T(8,128)(2,1)}, u32[]{:S(2)}, u32[]{:S(2)}) %collective-permute-start.6) | collective-permute-done | bytes 2359328 | tf_op jit(solution)/shard_map/ppermute | solution.py:57
  132.0 13.3 %collective-permute-done.10.refs_6_ = bf16[256,2304]{1,0:T(8,128)(2,1)S(1)} collective-permute-done((bf16[256,2304]{1,0:T(8,128)(2,1)S(1)}, bf16[256,2304]{1,0:T(8,128)(2,1)S(1)}, u32[]{:S(2)}, u32[]{:S(2)}) %collective-permute-start.10) | collective-permute-done | bytes 1179680 | tf_op jit(solution)/shard_map/ppermute | solution.py:57
  164.8 36.2 %forward.2 = (f32[528,8,512]{2,1,0:T(8,128)}, f32[6,8,128]{2,1,0:T(8,128)}, bf16[8,528,2304]{2,1,0:T(8,128)(2,1)}) custom-call(bf16[512,2304]{1,0:T(8,128)(2,1)} %bitcast.166, bf16[512,2304]{1,0:T(8,128)(2,1)} %collective-permute-done.refs_1_, bf16[512,2304]{1,0:T(8,128)(2,1)} %collective-permute-done.6.refs_2_, ...), custom_call_target="tpu_custom_call" | custom-call | tf_op jit(solution)/shard_map/forward/pallas_call | solution.py:555
  207.7 24.3 %forward.3 = (f32[528,8,384]{2,1,0:T(8,128)}, f32[3,8,128]{2,1,0:T(8,128)}) custom-call(bf16[8,528,2304]{2,1,0:T(8,128)(2,1)} %pad_dynamic-update-slice_fusion.refs_0_, bf16[16,2304]{1,0:T(8,128)(2,1)} %pad.38.refs_10_.refs_1_, bf16[2304,768]{1,0:T(8,128)(2,1)} %all-gather.5.cloned.1.call-done.refs_2_.refs_3_, f32[1,384]{1,0:T(1,128)} %bitcast.178, ...), custom_call_target="tpu_custom_call" | custom-call | tf_op jit(solution)/shard_map/forward/pallas_call | solution.py:555
  243.7 20.7 %backward.2 = (bf16[4,528,256]{2,1,0:T(8,128)(2,1)}, bf16[4,528,256]{2,1,0:T(8,128)(2,1)}, bf16[8,528,1024]{2,1,0:T(8,128)(2,1)}, f32[8,512]{1,0:T(8,128)}, f32[8,512]{1,0:T(8,128)}) custom-call(f32[528,8,512]{2,1,0:T(8,128)} %get-tuple-element.59.refs_0_, f32[528,8,128]{2,1,0:T(8,128)} %broadcast_in_dim.511.refs_13_.refs_4_.refs_1_, ...), custom_call_target="tpu_custom_call" | custom-call | tf_op jit(solution)/shard_map/backward/pallas_call | solution.py:729
  265.9 28.1 %bitcast_convert_fusion.refs_7_ = bf16[2304,1024]{1,0:T(8,128)(2,1)} fusion(bf16[8,528,2304]{2,1,0:T(8,128)(2,1)} %pad_dynamic-update-slice_fusion.refs_0_, bf16[8,528,1024]{2,1,0:T(8,128)(2,1)} %pad_dynamic-update-slice_fusion.1.refs_0_), kind=kOutput, calls=%fused_computation.2 | convolution fusion | flops 19933691904 | bytes 32833536 | tf_op jit(solution)/shard_map/dot_general | solution.py:37
  303.1 12.6 %backward.3 = (bf16[4,528,128]{2,1,0:T(8,128)(2,1)}, bf16[4,528,128]{2,1,0:T(8,128)(2,1)}, bf16[8,528,768]{2,1,0:T(8,128)(2,1)}, f32[8,384]{1,0:T(8,128)}, f32[8,384]{1,0:T(8,128)}) custom-call(f32[528,8,384]{2,1,0:T(8,128)} %get-tuple-element.68.refs_0_, f32[528,8,128]{2,1,0:T(8,128)} %broadcast_in_dim.511.refs_13_.refs_4_.refs_1_, ...), custom_call_target="tpu_custom_call" | custom-call | tf_op jit(solution)/shard_map/backward/pallas_call | solution.py:729
  317.2 7.6 %collective-permute-done.30.refs_2_.refs_5_ = bf16[2,528,256]{2,1,0:T(8,128)(2,1)S(1)} collective-permute-done((bf16[2,528,256]{2,1,0:T(8,128)(2,1)}, bf16[2,528,256]{2,1,0:T(8,128)(2,1)S(1)}, u32[]{:S(2)}, u32[]{:S(2)}) %collective-permute-start.30) | collective-permute-done | bytes 540704 | tf_op jit(solution)/shard_map/ppermute | solution.py:57
  326.4 13.5 %input_gradient.3 = (bf16[1,528,2304]{2,1,0:T(8,128)(2,1)}, bf16[1,528,2304]{2,1,0:T(8,128)(2,1)}) custom-call(bf16[8,528,1024]{2,1,0:T(8,128)(2,1)} %pad_dynamic-update-slice_fusion.1.refs_0_, bf16[8,528,768]{2,1,0:T(8,128)(2,1)} %pad_dynamic-update-slice_fusion.2.refs_1_.refs_0_, bf16[2304,1024]{1,0:T(8,128)(2,1)} %all-gather.3.cloned.1.call-done.refs_11_.refs_2_, ...), custom_call_target="tpu_custom_call" | custom-call | tf_op jit(solution)/shard_map/input_gradient/pallas_call | solution.py:780
  341.6 4.0 collective-permute-done.32
  353.4 5.4 far_sum.1
  362.7 22.2 %bitcast_convert_fusion.1.refs_0_ = bf16[2304,768]{1,0:T(8,128)(2,1)} fusion(bf16[8,528,2304]{2,1,0:T(8,128)(2,1)} %pad_dynamic-update-slice_fusion.refs_0_, bf16[8,528,768]{2,1,0:T(8,128)(2,1)} %after.29.refs_1_), kind=kOutput, calls=%fused_computation.3 | convolution fusion | flops 14950268928 | bytes 29491200 | tf_op jit(solution)/shard_map/dot_general | solution.py:37
  390.3 23.8 %input_gradient.4 = (bf16[2,528,2304]{2,1,0:T(8,128)(2,1)}, bf16[2,528,2304]{2,1,0:T(8,128)(2,1)}) custom-call(bf16[8,528,1024]{2,1,0:T(8,128)(2,1)} %pad_dynamic-update-slice_fusion.1.refs_0_, bf16[8,528,768]{2,1,0:T(8,128)(2,1)} %after.29.refs_1_, bf16[2304,1024]{1,0:T(8,128)(2,1)} %all-gather.3.cloned.1.call-done.refs_11_.refs_2_, ...), custom_call_target="tpu_custom_call" | custom-call | tf_op jit(solution)/shard_map/input_gradient/pallas_call | solution.py:780
  414.2 8.4 %collective-permute-done.39.odd_ref = bf16[2,528,2304]{2,1,0:T(8,128)(2,1)} collective-permute-done((bf16[2,528,2304]{2,1,0:T(8,128)(2,1)}, bf16[2,528,2304]{2,1,0:T(8,128)(2,1)}, u32[]{:S(2)}, u32[]{:S(2)}) %collective-permute-start.39) | collective-permute-done | bytes 4866080 | tf_op jit(solution)/shard_map/ppermute | solution.py:57
  422.6 7.9 %near_sums.1 = (bf16[256,2304]{1,0:T(8,128)(2,1)}, bf16[272,2304]{1,0:T(8,128)(2,1)}, bf16[256,2304]{1,0:T(8,128)(2,1)}, bf16[272,2304]{1,0:T(8,128)(2,1)}) custom-call(bf16[2,528,2304]{2,1,0:T(8,128)(2,1)} %get-tuple-element.81.even_ref, bf16[2,528,2304]{2,1,0:T(8,128)(2,1)} %collective-permute-done.39.odd_ref, bf16[256,2304]{1,0:T(8,128)(2,1)} %copy-done.12, ...), custom_call_target="tpu_custom_call" | custom-call | tf_op jit(solution)/shard_map/near_sums/pallas_call | solution.py:838
  434.0 4.2 place_channels.1
  438.2 13.6 %input_gradient.5 = (bf16[1,528,2304]{2,1,0:T(8,128)(2,1)}, bf16[1,528,2304]{2,1,0:T(8,128)(2,1)}) custom-call(bf16[8,528,1024]{2,1,0:T(8,128)(2,1)} %pad_dynamic-update-slice_fusion.1.refs_0_, bf16[8,528,768]{2,1,0:T(8,128)(2,1)} %after.29.refs_1_, bf16[2304,1024]{1,0:T(8,128)(2,1)} %all-gather.3.cloned.1.call-done.refs_11_.refs_2_, ...), custom_call_target="tpu_custom_call" | custom-call | tf_op jit(solution)/shard_map/input_gradient/pallas_call | solution.py:780
  451.8 8.6 %collective-permute-done.41.refs_2_.y_high = bf16[272,2304]{1,0:T(8,128)(2,1)S(1)} collective-permute-done((bf16[272,2304]{1,0:T(8,128)(2,1)}, bf16[272,2304]{1,0:T(8,128)(2,1)S(1)}, u32[]{:S(2)}, u32[]{:S(2)}) %collective-permute-start.41) | collective-permute-done | bytes 1253408 | tf_op jit(solution)/shard_map/ppermute | solution.py:57
  485.3 8.6 %collective-permute-done.46.refs_3_ = bf16[2,72,1792]{2,1,0:T(8,128)(2,1)S(1)} collective-permute-done((bf16[2,72,1792]{2,1,0:T(8,128)(2,1)S(1)}, bf16[2,72,1792]{2,1,0:T(8,128)(2,1)S(1)}, u32[]{:S(2)}, u32[]{:S(2)}) %collective-permute-start.46) | collective-permute-done | bytes 516128 | tf_op jit(solution)/shard_map/ppermute | solution.py:57
  493.9 8.9 %collective-permute-done.45.refs_2_ = bf16[2,72,1792]{2,1,0:T(8,128)(2,1)S(1)} collective-permute-done((bf16[2,72,1792]{2,1,0:T(8,128)(2,1)S(1)}, bf16[2,72,1792]{2,1,0:T(8,128)(2,1)S(1)}, u32[]{:S(2)}, u32[]{:S(2)}) %collective-permute-start.45) | collective-permute-done | bytes 516128 | tf_op jit(solution)/shard_map/ppermute | solution.py:57
  509.9 3.5 place_gradient.1
  516.9 8.9 %multiply_subtract_fusion = (f32[2,72,6912]{2,1,0:T(8,128)}, f32[2,72,6912]{2,1,0:T(8,128)}, f32[2,72,6912]{2,1,0:T(8,128)}, f32[2,72,6912]{2,1,0:T(8,128)}) fusion(f32[2,72,6912]{2,1,0:T(8,128)} %weight_ref.1, f32[2,72,6912]{2,1,0:T(8,128)} %param.20, f32[2,72,6912]{2,1,0:T(8,128)} %param.21, bf16[2,72,6912]{2,1,0:T(8,128)(2,1)S(1)} %copy-done.8, f32[]{:T(128)S(6)} %min.3), kind=kLoop, calls=%fused_computation.6 | loop fusion | flops 16920576 | bytes 29859844 | tf_op jit(solution)/shard_map/sub | solution.py:883
  528.7 7.0 %collective-permute-done.48.x_low = bf16[256,2304]{1,0:T(8,128)(2,1)S(1)} collective-permute-done((bf16[256,2304]{1,0:T(8,128)(2,1)}, bf16[256,2304]{1,0:T(8,128)(2,1)S(1)}, u32[]{:S(2)}, u32[]{:S(2)}) %collective-permute-start.48) | collective-permute-done | bytes 1179680 | tf_op jit(solution)/shard_map/ppermute | solution.py:57
  535.7 4.0 collective-permute-done.47.y_low
  539.7 6.8 %last_sum.1 = bf16[512,2304]{1,0:T(8,128)(2,1)} custom-call(bf16[1,528,2304]{2,1,0:T(8,128)(2,1)} %get-tuple-element.84.refs_1_.even_ref, bf16[1,528,2304]{2,1,0:T(8,128)(2,1)} %collective-permute-done.40.odd_ref, bf16[256,2304]{1,0:T(8,128)(2,1)} %collective-permute-done.47.y_low, bf16[256,2304]{1,0:T(8,128)(2,1)} %copy-done.26, ...), custom_call_target="tpu_custom_call" | custom-call | tf_op jit(solution)/shard_map/last_sum/pallas_call | solution.py:864
  (403 shorter events, 165.7 us)
Async XLA Ops:
  7.2 155.6 %all-gather.3.cloned.1.call-start = ((), (), s32[]{:S(2)}) async-start(), calls=%async_computation.2 | async-start | bytes 5898240 | tf_op jit(solution)/shard_map/all_gather | solution.py:932
  14.7 28.1 %collective-permute-start.17 = (bf16[2,72,1792]{2,1,0:T(8,128)(2,1)S(1)}, bf16[2,72,1792]{2,1,0:T(8,128)(2,1)}, u32[]{:S(2)}, u32[]{:S(2)}) collective-permute-start(bf16[2,72,1792]{2,1,0:T(8,128)(2,1)S(1)} %pad_maximum_fusion.5.refs_1_.refs_4_), channel_id=1, source_target_pairs={{0,6},{1,7},{2,4},{3,5},{4,2},{5,3},{6,0},{7,1},{8,14},{9,15},{10,... | collective-permute-start | bytes 1548296 | tf_op jit(solution)/shard_map/ppermute | solution.py:57
  26.0 15.8 %collective-permute-start.15 = (bf16[2,72,1792]{2,1,0:T(8,128)(2,1)S(1)}, bf16[2,72,1792]{2,1,0:T(8,128)(2,1)S(1)}, u32[]{:S(2)}, u32[]{:S(2)}) collective-permute-start(bf16[2,72,1792]{2,1,0:T(8,128)(2,1)S(1)} %pad_maximum_fusion.7), channel_id=1, source_target_pairs={{0,2},{1,3},{2,0},{3,1},{4,6},{5,7},{6,4},{7,5},{8,10},{9,11},{10,... | collective-permute-start | bytes 1548296 | tf_op jit(solution)/shard_map/ppermute | solution.py:57
  45.8 161.9 %all-gather.5.cloned.1.call-start = ((), (), s32[]{:S(2)}) async-start(), calls=%async_computation.3 | async-start | bytes 4423680 | tf_op jit(solution)/shard_map/all_gather | solution.py:932
  49.1 15.8 %collective-permute-start.5 = (bf16[2,688,128]{2,1,0:T(8,128)(2,1)S(1)}, bf16[2,688,128]{2,1,0:T(8,128)(2,1)S(1)}, u32[]{:S(2)}, u32[]{:S(2)}) collective-permute-start(bf16[2,688,128]{2,1,0:T(8,128)(2,1)S(1)} %copy-done.24), channel_id=1, source_target_pairs={{0,6},{1,7},{2,4},{3,5},{4,2},{5,3},{6,0},{7,1},{8,14},{9,15},{10,... | collective-permute-start | bytes 1056776 | tf_op jit(solution)/shard_map/ppermute | solution.py:57
  51.5 333.3 %reduce-scatter.3.cloned.1.call-start = ((), (), s32[]{:S(2)}) async-start(), calls=%async_computation.4 | async-start | bytes 5898240 | tf_op jit(solution)/shard_map/reduce_scatter | solution.py:1055
  65.6 52.4 %collective-permute-start.6 = (bf16[512,2304]{1,0:T(8,128)(2,1)}, bf16[512,2304]{1,0:T(8,128)(2,1)}, u32[]{:S(2)}, u32[]{:S(2)}) collective-permute-start(bf16[512,2304]{1,0:T(8,128)(2,1)} %after.19), channel_id=1, source_target_pairs={{0,2},{1,3},{2,0},{3,1},{4,6},{5,7},{6,4},{7,5},{8,10},{9,11},{10,... | collective-permute-start | bytes 7077896 | tf_op jit(solution)/shard_map/ppermute | solution.py:57
  67.3 53.9 %collective-permute-start.8 = (bf16[512,2304]{1,0:T(8,128)(2,1)}, bf16[512,2304]{1,0:T(8,128)(2,1)}, u32[]{:S(2)}, u32[]{:S(2)}) collective-permute-start(bf16[512,2304]{1,0:T(8,128)(2,1)} %after.19), channel_id=1, source_target_pairs={{0,4},{1,5},{2,6},{3,7},{4,0},{5,1},{6,2},{7,3},{8,12},{9,13},{10,... | collective-permute-start | bytes 7077896 | tf_op jit(solution)/shard_map/ppermute | solution.py:57
  79.3 80.5 %collective-permute-start = (bf16[512,2304]{1,0:T(8,128)(2,1)}, bf16[512,2304]{1,0:T(8,128)(2,1)}, u32[]{:S(2)}, u32[]{:S(2)}) collective-permute-start(bf16[512,2304]{1,0:T(8,128)(2,1)} %bitcast.165), channel_id=1, source_target_pairs={{0,1},{1,0},{2,3},{3,2},{4,5},{5,4},{6,7},{7,6},{8,9},{9,8},{10,11... | collective-permute-start | bytes 7077896 | tf_op jit(solution)/shard_map/ppermute | solution.py:57
  85.5 44.5 %collective-permute-start.21 = (bf16[4,528,128]{2,1,0:T(8,128)(2,1)}, bf16[4,528,128]{2,1,0:T(8,128)(2,1)}, u32[]{:S(2)}, u32[]{:S(2)}) collective-permute-start(bf16[4,528,128]{2,1,0:T(8,128)(2,1)} %after.20), channel_id=1, source_target_pairs={{0,1},{1,0},{2,3},{3,2},{4,5},{5,4},{6,7},{7,6},{8,9},{9,8},{10,11... | collective-permute-start | bytes 1622024 | tf_op jit(solution)/shard_map/ppermute | solution.py:57
  119.4 26.0 %collective-permute-start.10 = (bf16[256,2304]{1,0:T(8,128)(2,1)S(1)}, bf16[256,2304]{1,0:T(8,128)(2,1)S(1)}, u32[]{:S(2)}, u32[]{:S(2)}) collective-permute-start(bf16[256,2304]{1,0:T(8,128)(2,1)S(1)} %slice.968), channel_id=1, source_target_pairs={{0,4},{1,5},{2,6},{3,7},{4,0},{5,1},{6,2},{7,3},{8,12},{9,13},{10,... | collective-permute-start | bytes 3538952 | tf_op jit(solution)/shard_map/ppermute | solution.py:57
  122.5 25.8 %collective-permute-start.12 = (bf16[256,2304]{1,0:T(8,128)(2,1)S(1)}, bf16[256,2304]{1,0:T(8,128)(2,1)}, u32[]{:S(2)}, u32[]{:S(2)}) collective-permute-start(bf16[256,2304]{1,0:T(8,128)(2,1)S(1)} %slice.969), channel_id=1, source_target_pairs={{0,2},{1,3},{2,0},{3,1},{4,6},{5,7},{6,4},{7,5},{8,10},{9,11},{10,... | collective-permute-start | bytes 3538952 | tf_op jit(solution)/shard_map/ppermute | solution.py:57
  130.1 32.7 %collective-permute-start.7 = (bf16[512,2304]{1,0:T(8,128)(2,1)}, bf16[512,2304]{1,0:T(8,128)(2,1)}, u32[]{:S(2)}, u32[]{:S(2)}) collective-permute-start(bf16[512,2304]{1,0:T(8,128)(2,1)} %collective-permute-done.6.refs_2_), channel_id=1, source_target_pairs={{0,1},{1,0},{2,3},{3,2},{4,5},{5,4},{6,7},{7,6},{8,9},{9,8},{10,11... | collective-permute-start | bytes 7077896 | tf_op jit(solution)/shard_map/ppermute | solution.py:57
  130.1 32.7 %collective-permute-start.9 = (bf16[512,2304]{1,0:T(8,128)(2,1)}, bf16[512,2304]{1,0:T(8,128)(2,1)}, u32[]{:S(2)}, u32[]{:S(2)}) collective-permute-start(bf16[512,2304]{1,0:T(8,128)(2,1)} %collective-permute-done.8.refs_4_), channel_id=1, source_target_pairs={{0,1},{1,0},{2,3},{3,2},{4,5},{5,4},{6,7},{7,6},{8,9},{9,8},{10,11... | collective-permute-start | bytes 7077896 | tf_op jit(solution)/shard_map/ppermute | solution.py:57
  157.7 43.3 %collective-permute-start.22 = (bf16[2,528,128]{2,1,0:T(8,128)(2,1)}, bf16[2,528,128]{2,1,0:T(8,128)(2,1)S(1)}, u32[]{:S(2)}, u32[]{:S(2)}) collective-permute-start(bf16[2,528,128]{2,1,0:T(8,128)(2,1)} %after.23), channel_id=1, source_target_pairs={{0,2},{1,3},{2,0},{3,1},{4,6},{5,7},{6,4},{7,5},{8,10},{9,11},{10,... | collective-permute-start | bytes 811016 | tf_op jit(solution)/shard_map/ppermute | solution.py:57
  159.2 42.5 %collective-permute-start.23 = (bf16[2,528,128]{2,1,0:T(8,128)(2,1)}, bf16[2,528,128]{2,1,0:T(8,128)(2,1)S(1)}, u32[]{:S(2)}, u32[]{:S(2)}) collective-permute-start(bf16[2,528,128]{2,1,0:T(8,128)(2,1)} %after.25), channel_id=1, source_target_pairs={{0,4},{1,5},{2,6},{3,7},{4,0},{5,1},{6,2},{7,3},{8,12},{9,13},{10,... | collective-permute-start | bytes 811016 | tf_op jit(solution)/shard_map/ppermute | solution.py:57
  159.8 42.6 %collective-permute-start.24 = (bf16[2,528,128]{2,1,0:T(8,128)(2,1)}, bf16[2,528,128]{2,1,0:T(8,128)(2,1)S(1)}, u32[]{:S(2)}, u32[]{:S(2)}) collective-permute-start(bf16[2,528,128]{2,1,0:T(8,128)(2,1)} %after.27), channel_id=1, source_target_pairs={{0,6},{1,7},{2,4},{3,5},{4,2},{5,3},{6,0},{7,1},{8,14},{9,15},{10,... | collective-permute-start | bytes 811016 | tf_op jit(solution)/shard_map/ppermute | solution.py:57
  294.1 168.2 %reduce-scatter.5.cloned.1.call-start = ((), (), s32[]{:S(2)}) async-start(), calls=%async_computation.5 | async-start | bytes 4423680 | tf_op jit(solution)/shard_map/reduce_scatter | solution.py:1055
  297.9 19.3 %collective-permute-start.31 = (bf16[2,528,256]{2,1,0:T(8,128)(2,1)S(1)}, bf16[2,528,256]{2,1,0:T(8,128)(2,1)S(1)}, u32[]{:S(2)}, u32[]{:S(2)}) collective-permute-start(bf16[2,528,256]{2,1,0:T(8,128)(2,1)S(1)} %pad_maximum_fusion.4), channel_id=1, source_target_pairs={{0,6},{1,7},{2,4},{3,5},{4,2},{5,3},{6,0},{7,1},{8,14},{9,15},{10,... | collective-permute-start | bytes 1622024 | tf_op jit(solution)/shard_map/ppermute | solution.py:57
  300.3 24.5 %collective-permute-start.30 = (bf16[2,528,256]{2,1,0:T(8,128)(2,1)}, bf16[2,528,256]{2,1,0:T(8,128)(2,1)S(1)}, u32[]{:S(2)}, u32[]{:S(2)}) collective-permute-start(bf16[2,528,256]{2,1,0:T(8,128)(2,1)} %pad_maximum_fusion.3), channel_id=1, source_target_pairs={{0,4},{1,5},{2,6},{3,7},{4,0},{5,1},{6,2},{7,3},{8,12},{9,13},{10,... | collective-permute-start | bytes 1622024 | tf_op jit(solution)/shard_map/ppermute | solution.py:57
  301.8 23.0 %collective-permute-start.29 = (bf16[2,528,256]{2,1,0:T(8,128)(2,1)S(1)}, bf16[2,528,256]{2,1,0:T(8,128)(2,1)S(1)}, u32[]{:S(2)}, u32[]{:S(2)}) collective-permute-start(bf16[2,528,256]{2,1,0:T(8,128)(2,1)S(1)} %pad_maximum_fusion.2), channel_id=1, source_target_pairs={{0,2},{1,3},{2,0},{3,1},{4,6},{5,7},{6,4},{7,5},{8,10},{9,11},{10,... | collective-permute-start | bytes 1622024 | tf_op jit(solution)/shard_map/ppermute | solution.py:57
  358.8 30.5 %collective-permute-start.38 = (bf16[272,2304]{1,0:T(8,128)(2,1)}, bf16[272,2304]{1,0:T(8,128)(2,1)S(1)}, u32[]{:S(2)}, u32[]{:S(2)}) collective-permute-start(bf16[272,2304]{1,0:T(8,128)(2,1)} %get-tuple-element.80), channel_id=1, source_target_pairs={{0,2},{1,3},{2,0},{3,1},{4,6},{5,7},{6,4},{7,5},{8,10},{9,11},{10,... | collective-permute-start | bytes 3760136 | tf_op jit(solution)/shard_map/ppermute | solution.py:57
  359.4 27.5 %collective-permute-start.37 = (bf16[256,2304]{1,0:T(8,128)(2,1)}, bf16[256,2304]{1,0:T(8,128)(2,1)S(1)}, u32[]{:S(2)}, u32[]{:S(2)}) collective-permute-start(bf16[256,2304]{1,0:T(8,128)(2,1)} %get-tuple-element.79.refs_1_), channel_id=1, source_target_pairs={{0,4},{1,5},{2,6},{3,7},{4,0},{5,1},{6,2},{7,3},{8,12},{9,13},{10,... | collective-permute-start | bytes 3538952 | tf_op jit(solution)/shard_map/ppermute | solution.py:57
  430.5 29.9 %collective-permute-start.41 = (bf16[272,2304]{1,0:T(8,128)(2,1)}, bf16[272,2304]{1,0:T(8,128)(2,1)S(1)}, u32[]{:S(2)}, u32[]{:S(2)}) collective-permute-start(bf16[272,2304]{1,0:T(8,128)(2,1)} %get-tuple-element.83.refs_4_), channel_id=1, source_target_pairs={{0,2},{1,3},{2,0},{3,1},{4,6},{5,7},{6,4},{7,5},{8,10},{9,11},{10,... | collective-permute-start | bytes 3760136 | tf_op jit(solution)/shard_map/ppermute | solution.py:57
  431.7 29.5 %collective-permute-start.42 = (bf16[272,2304]{1,0:T(8,128)(2,1)}, bf16[272,2304]{1,0:T(8,128)(2,1)S(1)}, u32[]{:S(2)}, u32[]{:S(2)}) collective-permute-start(bf16[272,2304]{1,0:T(8,128)(2,1)} %get-tuple-element.87), channel_id=1, source_target_pairs={{0,4},{1,5},{2,6},{3,7},{4,0},{5,1},{6,2},{7,3},{8,12},{9,13},{10,... | collective-permute-start | bytes 3760136 | tf_op jit(solution)/shard_map/ppermute | solution.py:57
  465.6 17.0 %collective-permute-start.40 = (bf16[1,528,2304]{2,1,0:T(8,128)(2,1)}, bf16[1,528,2304]{2,1,0:T(8,128)(2,1)}, u32[]{:S(2)}, u32[]{:S(2)}) collective-permute-start(bf16[1,528,2304]{2,1,0:T(8,128)(2,1)} %get-tuple-element.85), channel_id=1, source_target_pairs={{0,1},{1,0},{2,3},{3,2},{4,5},{5,4},{6,7},{7,6},{8,9},{9,8},{10,11... | collective-permute-start | bytes 7299080 | tf_op jit(solution)/shard_map/ppermute | solution.py:57
  478.3 15.6 %collective-permute-start.46 = (bf16[2,72,1792]{2,1,0:T(8,128)(2,1)S(1)}, bf16[2,72,1792]{2,1,0:T(8,128)(2,1)S(1)}, u32[]{:S(2)}, u32[]{:S(2)}) collective-permute-start(bf16[2,72,1792]{2,1,0:T(8,128)(2,1)S(1)} %copy-done.23), channel_id=1, source_target_pairs={{0,6},{1,7},{2,4},{3,5},{4,2},{5,3},{6,0},{7,1},{8,14},{9,15},{10,... | collective-permute-start | bytes 1548296 | tf_op jit(solution)/shard_map/ppermute | solution.py:57
  479.7 23.0 %collective-permute-start.45 = (bf16[2,72,1792]{2,1,0:T(8,128)(2,1)S(1)}, bf16[2,72,1792]{2,1,0:T(8,128)(2,1)S(1)}, u32[]{:S(2)}, u32[]{:S(2)}) collective-permute-start(bf16[2,72,1792]{2,1,0:T(8,128)(2,1)S(1)} %copy-done.22), channel_id=1, source_target_pairs={{0,4},{1,5},{2,6},{3,7},{4,0},{5,1},{6,2},{7,3},{8,12},{9,13},{10,... | collective-permute-start | bytes 1548296 | tf_op jit(solution)/shard_map/ppermute | solution.py:57
  480.7 22.5 %collective-permute-start.44 = (bf16[2,72,1792]{2,1,0:T(8,128)(2,1)}, bf16[2,72,1792]{2,1,0:T(8,128)(2,1)S(1)}, u32[]{:S(2)}, u32[]{:S(2)}) collective-permute-start(bf16[2,72,1792]{2,1,0:T(8,128)(2,1)} %pad_maximum_fusion.9.refs_1_), channel_id=1, source_target_pairs={{0,2},{1,3},{2,0},{3,1},{4,6},{5,7},{6,4},{7,5},{8,10},{9,11},{10,... | collective-permute-start | bytes 1548296 | tf_op jit(solution)/shard_map/ppermute | solution.py:57
  483.4 30.0 %collective-permute-start.49 = (f32[1,2304]{1,0:T(1,128)S(1)}, f32[1,2304]{1,0:T(1,128)S(1)}, u32[]{:S(2)}, u32[]{:S(2)}) collective-permute-start(f32[1,2304]{1,0:T(1,128)S(1)} %fusion.3), channel_id=1, source_target_pairs={{4,0},{8,4},{12,8},{16,12},{20,16},{24,20},{28,24},{5,1},{9,5},{13... | collective-permute-start | bytes 27656 | tf_op jit(solution)/shard_map/ppermute | solution.py:1079
  508.7 27.0 %collective-permute-start.48 = (bf16[256,2304]{1,0:T(8,128)(2,1)}, bf16[256,2304]{1,0:T(8,128)(2,1)S(1)}, u32[]{:S(2)}, u32[]{:S(2)}) collective-permute-start(bf16[256,2304]{1,0:T(8,128)(2,1)} %after.34), channel_id=1, source_target_pairs={{0,4},{1,5},{2,6},{3,7},{4,0},{5,1},{6,2},{7,3},{8,12},{9,13},{10,... | collective-permute-start | bytes 3538952 | tf_op jit(solution)/shard_map/ppermute | solution.py:57
  513.4 26.3 %collective-permute-start.47 = (bf16[256,2304]{1,0:T(8,128)(2,1)}, bf16[256,2304]{1,0:T(8,128)(2,1)}, u32[]{:S(2)}, u32[]{:S(2)}) collective-permute-start(bf16[256,2304]{1,0:T(8,128)(2,1)} %after.33), channel_id=1, source_target_pairs={{0,2},{1,3},{2,0},{3,1},{4,6},{5,7},{6,4},{7,5},{8,10},{9,11},{10,... | collective-permute-start | bytes 3538952 | tf_op jit(solution)/shard_map/ppermute | solution.py:57
  (94 other events, 685.8 us)
Sparse Core Ops, SparseCore 0:
  45.9 91.0 all-gather.2
  138.6 69.0 all-gather.4
  294.2 84.3 reduce-scatter.2
  385.0 65.2 reduce-scatter.4

commit v5 on v4

--- a/solution.py
+++ b/solution.py
@@ -846,30 +846,47 @@
     )(even, odd, low, high)
 
 
-def last_sum_kernel(even_ref, odd_ref, y_low, x_low, y_high, x_high, next_ref, out_ref):
-    middle = y_low.shape[0]
-    rows = out_ref.shape[0] - middle
+def high_sum_kernel(even_ref, odd_ref, y_high, x_high, next_ref, out_ref):
+    rows = out_ref.shape[0]
+    here = pl.ds(rows, rows)
+    total = even_ref[0, here, :].astype(F32) + odd_ref[0, here, :].astype(F32)
+    total = total + y_high[pl.ds(0, rows), :].astype(F32) + x_high[pl.ds(0, rows), :].astype(F32)
+    row = lax.broadcasted_iota(jnp.int32, total.shape, 0)
+    out_ref[...] = jnp.where(row == rows - 1, total + next_ref[...], total).astype(BF16)
+
+
+def low_sum_kernel(even_ref, odd_ref, y_low, x_low, _, out_ref):
     total = even_ref[0].astype(F32) + odd_ref[0].astype(F32)
-    out_ref[pl.ds(0, middle), :] = (total[:middle] + y_low[...].astype(F32) + x_low[...].astype(F32)).astype(BF16)
-    high = total[middle : middle + rows] + y_high[pl.ds(0, rows), :].astype(F32) + x_high[pl.ds(0, rows), :].astype(F32)
-    row = lax.broadcasted_iota(jnp.int32, high.shape, 0)
-    out_ref[pl.ds(middle, rows), :] = jnp.where(row == rows - 1, high + next_ref[...], high).astype(BF16)
+    out_ref[...] = (total + y_low[...].astype(F32) + x_low[...].astype(F32)).astype(BF16)
 
 
 def last_sum(even, odd, lows, highs, from_next, tokens):
     _, length, width = even.shape
-    block = 384
-    spec = pl.BlockSpec((1, length, block), lambda i: (0, 0, i))
-    parts = [*lows, *highs, from_next]
-    return pl.pallas_call(
-        last_sum_kernel,
+    block, rows = 384, tokens // 2
+    assert lows[0].shape[0] == rows
+    shape = jax.ShapeDtypeStruct((tokens, width), BF16)
+    columns = lambda part: pl.BlockSpec((part.shape[0], block), lambda i: (0, i))
+    whole = pl.BlockSpec((1, length, block), lambda i: (0, 0, i))
+    half = pl.BlockSpec((1, rows, block), lambda i: (0, 0, i))
+    done = pl.pallas_call(
+        high_sum_kernel,
         grid=(width // block,),
-        out_shape=jax.ShapeDtypeStruct((tokens, width), BF16),
-        in_specs=[spec, spec] + [pl.BlockSpec((part.shape[0], block), lambda i: (0, i)) for part in parts],
-        out_specs=pl.BlockSpec((tokens, block), lambda i: (0, i)),
-        compiler_params=params(),
-        name="last_sum",
-    )(even, odd, *parts)
+        out_shape=shape,
+        in_specs=[whole, whole, *map(columns, (*highs, from_next))],
+        out_specs=pl.BlockSpec((rows, block), lambda i: (1, i)),
+        compiler_params=params(),
+        name="high_sum",
+    )(even, odd, *highs, from_next)
+    return pl.pallas_call(
+        low_sum_kernel,
+        grid=(width // block,),
+        out_shape=shape,
+        in_specs=[half, half, *map(columns, lows), pl.BlockSpec(memory_space=pl.ANY)],
+        out_specs=pl.BlockSpec((rows, block), lambda i: (0, i)),
+        input_output_aliases={4: 0},
+        compiler_params=params(),
+        name="low_sum",
+    )(even, odd, *lows, done)
 
 
 def adamw(master, gradient, moment_one, moment_two, rate):

time: 560 us -> 561 us (level)
  waiting for transfers between devices: 146 us -> 140 us
    ppermute x55, waiting for transfers between devices: 145 us -> 138 us  [flip(): return lax.ppermute(block, AXES, [(n, n ^ mask) for n in range(self.count)])]
    pallas_call x1 -> x2, Pallas kernels: 6.78 us -> 11.3 us  [the longest x1 5.93 us: last_sum(): pl.pallas_call(high_sum_kernel, grid=(width // block,), out_shape=shape,...]
    unnamed x136 -> x132, local copies, waits for them, and re-layouts: 16.2 us -> 16.3 us
  transfers between devices with their start and end apart: 61 -> 61, of which waited for: 28 -> 27; matrix products, arithmetic and copies ran while one was open for 17% -> 18% of each run, Pallas kernels for 23% -> 24%
where the time goes in v5:
time: 561 us; the launch traced here: 555 us
  Pallas kernels  196 us (35%)
  waiting for transfers between devices  140 us (25%)
  starting transfers between devices  58.5 us (10%)
  matrix products  50.4 us (9%)
  local copies, waits for them, and re-layouts  46.9 us (8%)
  other arithmetic  46.2 us (8%)
  between operations  17.5 us (3%)
    ppermute x55, waiting for transfers between devices, flip(): return lax.ppermute(block, AXES, [(n, n ^ mask) for n in range(self.count)])  138 us
    pallas_call x2, Pallas kernels, forward(): pl.pallas_call(waiting(functools.partial(forward_kernel, tiles, rest, 2 i...  60.5 us
    ppermute x55, starting transfers between devices, flip(): return lax.ppermute(block, AXES, [(n, n ^ mask) for n in range(self.count)])  53.6 us
    pallas_call x3, Pallas kernels, input_gradients(): pl.pallas_call(waiting(input_gradient_kernel, 4, others), grid=(3, count)...  51 us
    dot_general x2, matrix products, dot_f32(): return lax.dot_general(a, b, (dims, ((), ())), preferred_element_type=F32)  50.4 us
    pallas_call x2, Pallas kernels, backward(): pl.pallas_call(waiting(functools.partial(backward_kernel, tiles, rest, bl...  33.2 us
    another operation x23, other arithmetic, pair_up(): return [jnp.stack([even[i], sibling[i]]) for i in range(4)]  17.2 us
    unnamed x132, local copies, waits for them, and re-layouts  16.3 us
  transfers between devices with their start and end apart: 61, of which 27 were waited for; matrix products, arithmetic and copies ran while one was open for 18% of the time, Pallas kernels for 24%

profile of v5, /device:TPU:0, one launch (start us, length us, event | category | flops | bytes accessed | tf_op | source)
XLA Modules:
  0.0 555.4 jit_solution(14573975081948163034)
XLA Ops:
  7.3 3.9 pack_weight.1
  18.3 3.9 copied.1.refs_3_.refs_0_
  22.1 3.6 pack_channels.1
  31.1 10.6 %collective-permute-done.15.refs_2_ = bf16[2,72,1792]{2,1,0:T(8,128)(2,1)S(1)} collective-permute-done((bf16[2,72,1792]{2,1,0:T(8,128)(2,1)S(1)}, bf16[2,72,1792]{2,1,0:T(8,128)(2,1)S(1)}, u32[]{:S(2)}, u32[]{:S(2)}) %collective-permute-start.15) | collective-permute-done | bytes 516128 | tf_op jit(solution)/shard_map/ppermute | solution.py:57
  51.5 5.1 collective-permute-done.3.refs_1_
  58.8 6.1 %collective-permute-done.5.refs_3_ = bf16[2,688,128]{2,1,0:T(8,128)(2,1)S(1)} collective-permute-done((bf16[2,688,128]{2,1,0:T(8,128)(2,1)S(1)}, bf16[2,688,128]{2,1,0:T(8,128)(2,1)S(1)}, u32[]{:S(2)}, u32[]{:S(2)}) %collective-permute-start.5) | collective-permute-done | bytes 352288 | tf_op jit(solution)/shard_map/ppermute | solution.py:57
  71.9 3.7 collective-permute-start.20
  85.7 32.3 %collective-permute-done.6.refs_2_ = bf16[512,2304]{1,0:T(8,128)(2,1)} collective-permute-done((bf16[512,2304]{1,0:T(8,128)(2,1)}, bf16[512,2304]{1,0:T(8,128)(2,1)}, u32[]{:S(2)}, u32[]{:S(2)}) %collective-permute-start.6) | collective-permute-done | bytes 2359328 | tf_op jit(solution)/shard_map/ppermute | solution.py:57
  132.1 13.3 %collective-permute-done.10.refs_6_ = bf16[256,2304]{1,0:T(8,128)(2,1)S(1)} collective-permute-done((bf16[256,2304]{1,0:T(8,128)(2,1)S(1)}, bf16[256,2304]{1,0:T(8,128)(2,1)S(1)}, u32[]{:S(2)}, u32[]{:S(2)}) %collective-permute-start.10) | collective-permute-done | bytes 1179680 | tf_op jit(solution)/shard_map/ppermute | solution.py:57
  164.7 36.2 %forward.2 = (f32[528,8,512]{2,1,0:T(8,128)}, f32[6,8,128]{2,1,0:T(8,128)}, bf16[8,528,2304]{2,1,0:T(8,128)(2,1)}) custom-call(bf16[512,2304]{1,0:T(8,128)(2,1)} %bitcast.166, bf16[512,2304]{1,0:T(8,128)(2,1)} %collective-permute-done.refs_1_, bf16[512,2304]{1,0:T(8,128)(2,1)} %collective-permute-done.6.refs_2_, ...), custom_call_target="tpu_custom_call" | custom-call | tf_op jit(solution)/shard_map/forward/pallas_call | solution.py:555
  207.7 24.3 %forward.3 = (f32[528,8,384]{2,1,0:T(8,128)}, f32[3,8,128]{2,1,0:T(8,128)}) custom-call(bf16[8,528,2304]{2,1,0:T(8,128)(2,1)} %pad_dynamic-update-slice_fusion.refs_0_, bf16[16,2304]{1,0:T(8,128)(2,1)} %pad.38.refs_10_.refs_1_, bf16[2304,768]{1,0:T(8,128)(2,1)} %all-gather.5.cloned.1.call-done.refs_2_.refs_3_, f32[1,384]{1,0:T(1,128)} %bitcast.178, ...), custom_call_target="tpu_custom_call" | custom-call | tf_op jit(solution)/shard_map/forward/pallas_call | solution.py:555
  243.7 20.6 %backward.2 = (bf16[4,528,256]{2,1,0:T(8,128)(2,1)}, bf16[4,528,256]{2,1,0:T(8,128)(2,1)}, bf16[8,528,1024]{2,1,0:T(8,128)(2,1)}, f32[8,512]{1,0:T(8,128)}, f32[8,512]{1,0:T(8,128)}) custom-call(f32[528,8,512]{2,1,0:T(8,128)} %get-tuple-element.59.refs_0_, f32[528,8,128]{2,1,0:T(8,128)} %broadcast_in_dim.511.refs_13_.refs_4_.refs_1_, ...), custom_call_target="tpu_custom_call" | custom-call | tf_op jit(solution)/shard_map/backward/pallas_call | solution.py:729
  265.9 28.2 %bitcast_convert_fusion.refs_7_ = bf16[2304,1024]{1,0:T(8,128)(2,1)} fusion(bf16[8,528,2304]{2,1,0:T(8,128)(2,1)} %pad_dynamic-update-slice_fusion.refs_0_, bf16[8,528,1024]{2,1,0:T(8,128)(2,1)} %pad_dynamic-update-slice_fusion.1.refs_0_), kind=kOutput, calls=%fused_computation.2 | convolution fusion | flops 19933691904 | bytes 32833536 | tf_op jit(solution)/shard_map/dot_general | solution.py:37
  303.2 12.6 %backward.3 = (bf16[4,528,128]{2,1,0:T(8,128)(2,1)}, bf16[4,528,128]{2,1,0:T(8,128)(2,1)}, bf16[8,528,768]{2,1,0:T(8,128)(2,1)}, f32[8,384]{1,0:T(8,128)}, f32[8,384]{1,0:T(8,128)}) custom-call(f32[528,8,384]{2,1,0:T(8,128)} %get-tuple-element.68.refs_0_, f32[528,8,128]{2,1,0:T(8,128)} %broadcast_in_dim.511.refs_13_.refs_4_.refs_1_, ...), custom_call_target="tpu_custom_call" | custom-call | tf_op jit(solution)/shard_map/backward/pallas_call | solution.py:729
  317.2 7.7 %collective-permute-done.30.refs_2_.refs_5_ = bf16[2,528,256]{2,1,0:T(8,128)(2,1)S(1)} collective-permute-done((bf16[2,528,256]{2,1,0:T(8,128)(2,1)}, bf16[2,528,256]{2,1,0:T(8,128)(2,1)S(1)}, u32[]{:S(2)}, u32[]{:S(2)}) %collective-permute-start.30) | collective-permute-done | bytes 540704 | tf_op jit(solution)/shard_map/ppermute | solution.py:57
  326.5 13.5 %input_gradient.3 = (bf16[1,528,2304]{2,1,0:T(8,128)(2,1)}, bf16[1,528,2304]{2,1,0:T(8,128)(2,1)}) custom-call(bf16[8,528,1024]{2,1,0:T(8,128)(2,1)} %pad_dynamic-update-slice_fusion.1.refs_0_, bf16[8,528,768]{2,1,0:T(8,128)(2,1)} %pad_dynamic-update-slice_fusion.2.refs_1_.refs_0_, bf16[2304,1024]{1,0:T(8,128)(2,1)} %all-gather.3.cloned.1.call-done.refs_11_.refs_2_, ...), custom_call_target="tpu_custom_call" | custom-call | tf_op jit(solution)/shard_map/input_gradient/pallas_call | solution.py:780
  341.7 4.0 collective-permute-done.32
  353.5 5.4 far_sum.1
  362.8 22.2 %bitcast_convert_fusion.1.refs_0_ = bf16[2304,768]{1,0:T(8,128)(2,1)} fusion(bf16[8,528,2304]{2,1,0:T(8,128)(2,1)} %pad_dynamic-update-slice_fusion.refs_0_, bf16[8,528,768]{2,1,0:T(8,128)(2,1)} %after.29.refs_1_), kind=kOutput, calls=%fused_computation.3 | convolution fusion | flops 14950268928 | bytes 29491200 | tf_op jit(solution)/shard_map/dot_general | solution.py:37
  390.4 23.9 %input_gradient.4 = (bf16[2,528,2304]{2,1,0:T(8,128)(2,1)}, bf16[2,528,2304]{2,1,0:T(8,128)(2,1)}) custom-call(bf16[8,528,1024]{2,1,0:T(8,128)(2,1)} %pad_dynamic-update-slice_fusion.1.refs_0_, bf16[8,528,768]{2,1,0:T(8,128)(2,1)} %after.29.refs_1_, bf16[2304,1024]{1,0:T(8,128)(2,1)} %all-gather.3.cloned.1.call-done.refs_11_.refs_2_, ...), custom_call_target="tpu_custom_call" | custom-call | tf_op jit(solution)/shard_map/input_gradient/pallas_call | solution.py:780
  414.4 8.4 %collective-permute-done.39.odd_ref = bf16[2,528,2304]{2,1,0:T(8,128)(2,1)} collective-permute-done((bf16[2,528,2304]{2,1,0:T(8,128)(2,1)}, bf16[2,528,2304]{2,1,0:T(8,128)(2,1)}, u32[]{:S(2)}, u32[]{:S(2)}) %collective-permute-start.39) | collective-permute-done | bytes 4866080 | tf_op jit(solution)/shard_map/ppermute | solution.py:57
  422.8 7.8 %near_sums.1 = (bf16[256,2304]{1,0:T(8,128)(2,1)}, bf16[272,2304]{1,0:T(8,128)(2,1)}, bf16[256,2304]{1,0:T(8,128)(2,1)}, bf16[272,2304]{1,0:T(8,128)(2,1)}) custom-call(bf16[2,528,2304]{2,1,0:T(8,128)(2,1)} %get-tuple-element.81.even_ref, bf16[2,528,2304]{2,1,0:T(8,128)(2,1)} %collective-permute-done.39.odd_ref, bf16[256,2304]{1,0:T(8,128)(2,1)} %copy-done.12, ...), custom_call_target="tpu_custom_call" | custom-call | tf_op jit(solution)/shard_map/near_sums/pallas_call | solution.py:838
  434.0 4.2 place_channels.1
  438.3 13.5 %input_gradient.5 = (bf16[1,528,2304]{2,1,0:T(8,128)(2,1)}, bf16[1,528,2304]{2,1,0:T(8,128)(2,1)}) custom-call(bf16[8,528,1024]{2,1,0:T(8,128)(2,1)} %pad_dynamic-update-slice_fusion.1.refs_0_, bf16[8,528,768]{2,1,0:T(8,128)(2,1)} %after.29.refs_1_, bf16[2304,1024]{1,0:T(8,128)(2,1)} %all-gather.3.cloned.1.call-done.refs_11_.refs_2_, ...), custom_call_target="tpu_custom_call" | custom-call | tf_op jit(solution)/shard_map/input_gradient/pallas_call | solution.py:780
  451.8 8.7 %collective-permute-done.41.refs_2_.y_high = bf16[272,2304]{1,0:T(8,128)(2,1)S(1)} collective-permute-done((bf16[272,2304]{1,0:T(8,128)(2,1)}, bf16[272,2304]{1,0:T(8,128)(2,1)S(1)}, u32[]{:S(2)}, u32[]{:S(2)}) %collective-permute-start.41) | collective-permute-done | bytes 1253408 | tf_op jit(solution)/shard_map/ppermute | solution.py:57
  486.5 8.7 %collective-permute-done.46.refs_3_ = bf16[2,72,1792]{2,1,0:T(8,128)(2,1)S(1)} collective-permute-done((bf16[2,72,1792]{2,1,0:T(8,128)(2,1)}, bf16[2,72,1792]{2,1,0:T(8,128)(2,1)S(1)}, u32[]{:S(2)}, u32[]{:S(2)}) %collective-permute-start.46) | collective-permute-done | bytes 516128 | tf_op jit(solution)/shard_map/ppermute | solution.py:57
  495.2 8.7 %collective-permute-done.45.refs_2_ = bf16[2,72,1792]{2,1,0:T(8,128)(2,1)S(1)} collective-permute-done((bf16[2,72,1792]{2,1,0:T(8,128)(2,1)}, bf16[2,72,1792]{2,1,0:T(8,128)(2,1)S(1)}, u32[]{:S(2)}, u32[]{:S(2)}) %collective-permute-start.45) | collective-permute-done | bytes 516128 | tf_op jit(solution)/shard_map/ppermute | solution.py:57
  511.3 3.5 place_gradient.1
  515.6 5.9 %high_sum.1._ = bf16[512,2304]{1,0:T(8,128)(2,1)} custom-call(bf16[1,528,2304]{2,1,0:T(8,128)(2,1)} %get-tuple-element.84.refs_1_.even_ref, bf16[1,528,2304]{2,1,0:T(8,128)(2,1)} %copy-done.5, bf16[272,2304]{1,0:T(8,128)(2,1)} %copy-done.3, bf16[272,2304]{1,0:T(8,128)(2,1)} %copy-done.4, f32[1,2304]{1,0:T(1,128)} %after.37.next_ref), custom_call_target="tpu_custom_call" | custom-call | tf_op jit(solution)/shard_map/high_sum/pallas_call | solution.py:871
  524.2 8.9 %multiply_subtract_fusion = (f32[2,72,6912]{2,1,0:T(8,128)}, f32[2,72,6912]{2,1,0:T(8,128)}, f32[2,72,6912]{2,1,0:T(8,128)}, f32[2,72,6912]{2,1,0:T(8,128)}) fusion(f32[2,72,6912]{2,1,0:T(8,128)} %weight_ref.1, f32[2,72,6912]{2,1,0:T(8,128)} %param.20, f32[2,72,6912]{2,1,0:T(8,128)} %param.21, bf16[2,72,6912]{2,1,0:T(8,128)(2,1)S(1)} %copy-done.8, f32[]{:T(128)S(6)} %min.3), kind=kLoop, calls=%fused_computation.6 | loop fusion | flops 16920576 | bytes 29859844 | tf_op jit(solution)/shard_map/sub | solution.py:900
  537.2 3.9 collective-permute-done.47.y_low
  542.1 5.3 low_sum.1
  (400 shorter events, 169.4 us)
Async XLA Ops:
  7.2 155.5 %all-gather.3.cloned.1.call-start = ((), (), s32[]{:S(2)}) async-start(), calls=%async_computation.2 | async-start | bytes 5898240 | tf_op jit(solution)/shard_map/all_gather | solution.py:949
  14.7 28.1 %collective-permute-start.17 = (bf16[2,72,1792]{2,1,0:T(8,128)(2,1)S(1)}, bf16[2,72,1792]{2,1,0:T(8,128)(2,1)}, u32[]{:S(2)}, u32[]{:S(2)}) collective-permute-start(bf16[2,72,1792]{2,1,0:T(8,128)(2,1)S(1)} %pad_maximum_fusion.5.refs_1_.refs_4_), channel_id=1, source_target_pairs={{0,6},{1,7},{2,4},{3,5},{4,2},{5,3},{6,0},{7,1},{8,14},{9,15},{10,... | collective-permute-start | bytes 1548296 | tf_op jit(solution)/shard_map/ppermute | solution.py:57
  45.8 161.9 %all-gather.5.cloned.1.call-start = ((), (), s32[]{:S(2)}) async-start(), calls=%async_computation.3 | async-start | bytes 4423680 | tf_op jit(solution)/shard_map/all_gather | solution.py:949
  49.1 15.8 %collective-permute-start.5 = (bf16[2,688,128]{2,1,0:T(8,128)(2,1)S(1)}, bf16[2,688,128]{2,1,0:T(8,128)(2,1)S(1)}, u32[]{:S(2)}, u32[]{:S(2)}) collective-permute-start(bf16[2,688,128]{2,1,0:T(8,128)(2,1)S(1)} %copy-done.22), channel_id=1, source_target_pairs={{0,6},{1,7},{2,4},{3,5},{4,2},{5,3},{6,0},{7,1},{8,14},{9,15},{10,... | collective-permute-start | bytes 1056776 | tf_op jit(solution)/shard_map/ppermute | solution.py:57
  51.5 333.5 %reduce-scatter.3.cloned.1.call-start = ((), (), s32[]{:S(2)}) async-start(), calls=%async_computation.4 | async-start | bytes 5898240 | tf_op jit(solution)/shard_map/reduce_scatter | solution.py:1072
  65.7 52.4 %collective-permute-start.6 = (bf16[512,2304]{1,0:T(8,128)(2,1)}, bf16[512,2304]{1,0:T(8,128)(2,1)}, u32[]{:S(2)}, u32[]{:S(2)}) collective-permute-start(bf16[512,2304]{1,0:T(8,128)(2,1)} %after.19), channel_id=1, source_target_pairs={{0,2},{1,3},{2,0},{3,1},{4,6},{5,7},{6,4},{7,5},{8,10},{9,11},{10,... | collective-permute-start | bytes 7077896 | tf_op jit(solution)/shard_map/ppermute | solution.py:57
  67.3 53.9 %collective-permute-start.8 = (bf16[512,2304]{1,0:T(8,128)(2,1)}, bf16[512,2304]{1,0:T(8,128)(2,1)}, u32[]{:S(2)}, u32[]{:S(2)}) collective-permute-start(bf16[512,2304]{1,0:T(8,128)(2,1)} %after.19), channel_id=1, source_target_pairs={{0,4},{1,5},{2,6},{3,7},{4,0},{5,1},{6,2},{7,3},{8,12},{9,13},{10,... | collective-permute-start | bytes 7077896 | tf_op jit(solution)/shard_map/ppermute | solution.py:57
  79.3 80.5 %collective-permute-start = (bf16[512,2304]{1,0:T(8,128)(2,1)}, bf16[512,2304]{1,0:T(8,128)(2,1)}, u32[]{:S(2)}, u32[]{:S(2)}) collective-permute-start(bf16[512,2304]{1,0:T(8,128)(2,1)} %bitcast.165), channel_id=1, source_target_pairs={{0,1},{1,0},{2,3},{3,2},{4,5},{5,4},{6,7},{7,6},{8,9},{9,8},{10,11... | collective-permute-start | bytes 7077896 | tf_op jit(solution)/shard_map/ppermute | solution.py:57
  85.5 44.5 %collective-permute-start.21 = (bf16[4,528,128]{2,1,0:T(8,128)(2,1)}, bf16[4,528,128]{2,1,0:T(8,128)(2,1)}, u32[]{:S(2)}, u32[]{:S(2)}) collective-permute-start(bf16[4,528,128]{2,1,0:T(8,128)(2,1)} %after.20), channel_id=1, source_target_pairs={{0,1},{1,0},{2,3},{3,2},{4,5},{5,4},{6,7},{7,6},{8,9},{9,8},{10,11... | collective-permute-start | bytes 1622024 | tf_op jit(solution)/shard_map/ppermute | solution.py:57
  119.4 26.0 %collective-permute-start.10 = (bf16[256,2304]{1,0:T(8,128)(2,1)S(1)}, bf16[256,2304]{1,0:T(8,128)(2,1)S(1)}, u32[]{:S(2)}, u32[]{:S(2)}) collective-permute-start(bf16[256,2304]{1,0:T(8,128)(2,1)S(1)} %slice.968), channel_id=1, source_target_pairs={{0,4},{1,5},{2,6},{3,7},{4,0},{5,1},{6,2},{7,3},{8,12},{9,13},{10,... | collective-permute-start | bytes 3538952 | tf_op jit(solution)/shard_map/ppermute | solution.py:57
  122.5 25.8 %collective-permute-start.12 = (bf16[256,2304]{1,0:T(8,128)(2,1)S(1)}, bf16[256,2304]{1,0:T(8,128)(2,1)}, u32[]{:S(2)}, u32[]{:S(2)}) collective-permute-start(bf16[256,2304]{1,0:T(8,128)(2,1)S(1)} %slice.969), channel_id=1, source_target_pairs={{0,2},{1,3},{2,0},{3,1},{4,6},{5,7},{6,4},{7,5},{8,10},{9,11},{10,... | collective-permute-start | bytes 3538952 | tf_op jit(solution)/shard_map/ppermute | solution.py:57
  130.1 32.6 %collective-permute-start.7 = (bf16[512,2304]{1,0:T(8,128)(2,1)}, bf16[512,2304]{1,0:T(8,128)(2,1)}, u32[]{:S(2)}, u32[]{:S(2)}) collective-permute-start(bf16[512,2304]{1,0:T(8,128)(2,1)} %collective-permute-done.6.refs_2_), channel_id=1, source_target_pairs={{0,1},{1,0},{2,3},{3,2},{4,5},{5,4},{6,7},{7,6},{8,9},{9,8},{10,11... | collective-permute-start | bytes 7077896 | tf_op jit(solution)/shard_map/ppermute | solution.py:57
  130.1 32.6 %collective-permute-start.9 = (bf16[512,2304]{1,0:T(8,128)(2,1)}, bf16[512,2304]{1,0:T(8,128)(2,1)}, u32[]{:S(2)}, u32[]{:S(2)}) collective-permute-start(bf16[512,2304]{1,0:T(8,128)(2,1)} %collective-permute-done.8.refs_4_), channel_id=1, source_target_pairs={{0,1},{1,0},{2,3},{3,2},{4,5},{5,4},{6,7},{7,6},{8,9},{9,8},{10,11... | collective-permute-start | bytes 7077896 | tf_op jit(solution)/shard_map/ppermute | solution.py:57
  157.6 43.3 %collective-permute-start.22 = (bf16[2,528,128]{2,1,0:T(8,128)(2,1)}, bf16[2,528,128]{2,1,0:T(8,128)(2,1)S(1)}, u32[]{:S(2)}, u32[]{:S(2)}) collective-permute-start(bf16[2,528,128]{2,1,0:T(8,128)(2,1)} %after.23), channel_id=1, source_target_pairs={{0,2},{1,3},{2,0},{3,1},{4,6},{5,7},{6,4},{7,5},{8,10},{9,11},{10,... | collective-permute-start | bytes 811016 | tf_op jit(solution)/shard_map/ppermute | solution.py:57
  159.2 42.5 %collective-permute-start.23 = (bf16[2,528,128]{2,1,0:T(8,128)(2,1)}, bf16[2,528,128]{2,1,0:T(8,128)(2,1)S(1)}, u32[]{:S(2)}, u32[]{:S(2)}) collective-permute-start(bf16[2,528,128]{2,1,0:T(8,128)(2,1)} %after.25), channel_id=1, source_target_pairs={{0,4},{1,5},{2,6},{3,7},{4,0},{5,1},{6,2},{7,3},{8,12},{9,13},{10,... | collective-permute-start | bytes 811016 | tf_op jit(solution)/shard_map/ppermute | solution.py:57
  159.8 42.6 %collective-permute-start.24 = (bf16[2,528,128]{2,1,0:T(8,128)(2,1)}, bf16[2,528,128]{2,1,0:T(8,128)(2,1)S(1)}, u32[]{:S(2)}, u32[]{:S(2)}) collective-permute-start(bf16[2,528,128]{2,1,0:T(8,128)(2,1)} %after.27), channel_id=1, source_target_pairs={{0,6},{1,7},{2,4},{3,5},{4,2},{5,3},{6,0},{7,1},{8,14},{9,15},{10,... | collective-permute-start | bytes 811016 | tf_op jit(solution)/shard_map/ppermute | solution.py:57
  294.1 168.3 %reduce-scatter.5.cloned.1.call-start = ((), (), s32[]{:S(2)}) async-start(), calls=%async_computation.5 | async-start | bytes 4423680 | tf_op jit(solution)/shard_map/reduce_scatter | solution.py:1072
  298.0 19.2 %collective-permute-start.31 = (bf16[2,528,256]{2,1,0:T(8,128)(2,1)S(1)}, bf16[2,528,256]{2,1,0:T(8,128)(2,1)S(1)}, u32[]{:S(2)}, u32[]{:S(2)}) collective-permute-start(bf16[2,528,256]{2,1,0:T(8,128)(2,1)S(1)} %pad_maximum_fusion.4), channel_id=1, source_target_pairs={{0,6},{1,7},{2,4},{3,5},{4,2},{5,3},{6,0},{7,1},{8,14},{9,15},{10,... | collective-permute-start | bytes 1622024 | tf_op jit(solution)/shard_map/ppermute | solution.py:57
  300.4 24.5 %collective-permute-start.30 = (bf16[2,528,256]{2,1,0:T(8,128)(2,1)}, bf16[2,528,256]{2,1,0:T(8,128)(2,1)S(1)}, u32[]{:S(2)}, u32[]{:S(2)}) collective-permute-start(bf16[2,528,256]{2,1,0:T(8,128)(2,1)} %pad_maximum_fusion.3), channel_id=1, source_target_pairs={{0,4},{1,5},{2,6},{3,7},{4,0},{5,1},{6,2},{7,3},{8,12},{9,13},{10,... | collective-permute-start | bytes 1622024 | tf_op jit(solution)/shard_map/ppermute | solution.py:57
  301.9 23.0 %collective-permute-start.29 = (bf16[2,528,256]{2,1,0:T(8,128)(2,1)S(1)}, bf16[2,528,256]{2,1,0:T(8,128)(2,1)S(1)}, u32[]{:S(2)}, u32[]{:S(2)}) collective-permute-start(bf16[2,528,256]{2,1,0:T(8,128)(2,1)S(1)} %pad_maximum_fusion.2), channel_id=1, source_target_pairs={{0,2},{1,3},{2,0},{3,1},{4,6},{5,7},{6,4},{7,5},{8,10},{9,11},{10,... | collective-permute-start | bytes 1622024 | tf_op jit(solution)/shard_map/ppermute | solution.py:57
  358.9 30.5 %collective-permute-start.38 = (bf16[272,2304]{1,0:T(8,128)(2,1)}, bf16[272,2304]{1,0:T(8,128)(2,1)S(1)}, u32[]{:S(2)}, u32[]{:S(2)}) collective-permute-start(bf16[272,2304]{1,0:T(8,128)(2,1)} %get-tuple-element.80), channel_id=1, source_target_pairs={{0,2},{1,3},{2,0},{3,1},{4,6},{5,7},{6,4},{7,5},{8,10},{9,11},{10,... | collective-permute-start | bytes 3760136 | tf_op jit(solution)/shard_map/ppermute | solution.py:57
  359.5 27.5 %collective-permute-start.37 = (bf16[256,2304]{1,0:T(8,128)(2,1)}, bf16[256,2304]{1,0:T(8,128)(2,1)S(1)}, u32[]{:S(2)}, u32[]{:S(2)}) collective-permute-start(bf16[256,2304]{1,0:T(8,128)(2,1)} %get-tuple-element.79.refs_1_), channel_id=1, source_target_pairs={{0,4},{1,5},{2,6},{3,7},{4,0},{5,1},{6,2},{7,3},{8,12},{9,13},{10,... | collective-permute-start | bytes 3538952 | tf_op jit(solution)/shard_map/ppermute | solution.py:57
  430.6 29.9 %collective-permute-start.41 = (bf16[272,2304]{1,0:T(8,128)(2,1)}, bf16[272,2304]{1,0:T(8,128)(2,1)S(1)}, u32[]{:S(2)}, u32[]{:S(2)}) collective-permute-start(bf16[272,2304]{1,0:T(8,128)(2,1)} %get-tuple-element.83.refs_4_), channel_id=1, source_target_pairs={{0,2},{1,3},{2,0},{3,1},{4,6},{5,7},{6,4},{7,5},{8,10},{9,11},{10,... | collective-permute-start | bytes 3760136 | tf_op jit(solution)/shard_map/ppermute | solution.py:57
  431.9 29.5 %collective-permute-start.42 = (bf16[272,2304]{1,0:T(8,128)(2,1)}, bf16[272,2304]{1,0:T(8,128)(2,1)S(1)}, u32[]{:S(2)}, u32[]{:S(2)}) collective-permute-start(bf16[272,2304]{1,0:T(8,128)(2,1)} %get-tuple-element.87), channel_id=1, source_target_pairs={{0,4},{1,5},{2,6},{3,7},{4,0},{5,1},{6,2},{7,3},{8,12},{9,13},{10,... | collective-permute-start | bytes 3760136 | tf_op jit(solution)/shard_map/ppermute | solution.py:57
  465.7 17.9 %collective-permute-start.40 = (bf16[1,528,2304]{2,1,0:T(8,128)(2,1)}, bf16[1,528,2304]{2,1,0:T(8,128)(2,1)S(1)}, u32[]{:S(2)}, u32[]{:S(2)}) collective-permute-start(bf16[1,528,2304]{2,1,0:T(8,128)(2,1)} %get-tuple-element.85), channel_id=1, source_target_pairs={{0,1},{1,0},{2,3},{3,2},{4,5},{5,4},{6,7},{7,6},{8,9},{9,8},{10,11... | collective-permute-start | bytes 7299080 | tf_op jit(solution)/shard_map/ppermute | solution.py:57
  479.3 15.8 %collective-permute-start.46 = (bf16[2,72,1792]{2,1,0:T(8,128)(2,1)}, bf16[2,72,1792]{2,1,0:T(8,128)(2,1)S(1)}, u32[]{:S(2)}, u32[]{:S(2)}) collective-permute-start(bf16[2,72,1792]{2,1,0:T(8,128)(2,1)} %pad_maximum_fusion.11.refs_3_), channel_id=1, source_target_pairs={{0,6},{1,7},{2,4},{3,5},{4,2},{5,3},{6,0},{7,1},{8,14},{9,15},{10,... | collective-permute-start | bytes 1548296 | tf_op jit(solution)/shard_map/ppermute | solution.py:57
  480.8 23.1 %collective-permute-start.45 = (bf16[2,72,1792]{2,1,0:T(8,128)(2,1)}, bf16[2,72,1792]{2,1,0:T(8,128)(2,1)S(1)}, u32[]{:S(2)}, u32[]{:S(2)}) collective-permute-start(bf16[2,72,1792]{2,1,0:T(8,128)(2,1)} %pad_maximum_fusion.10.refs_2_), channel_id=1, source_target_pairs={{0,4},{1,5},{2,6},{3,7},{4,0},{5,1},{6,2},{7,3},{8,12},{9,13},{10,... | collective-permute-start | bytes 1548296 | tf_op jit(solution)/shard_map/ppermute | solution.py:57
  481.7 22.8 %collective-permute-start.44 = (bf16[2,72,1792]{2,1,0:T(8,128)(2,1)}, bf16[2,72,1792]{2,1,0:T(8,128)(2,1)}, u32[]{:S(2)}, u32[]{:S(2)}) collective-permute-start(bf16[2,72,1792]{2,1,0:T(8,128)(2,1)} %pad_maximum_fusion.9.refs_1_), channel_id=1, source_target_pairs={{0,2},{1,3},{2,0},{3,1},{4,6},{5,7},{6,4},{7,5},{8,10},{9,11},{10,... | collective-permute-start | bytes 1548296 | tf_op jit(solution)/shard_map/ppermute | solution.py:57
  484.6 30.2 %collective-permute-start.49 = (f32[1,2304]{1,0:T(1,128)S(1)}, f32[1,2304]{1,0:T(1,128)S(1)}, u32[]{:S(2)}, u32[]{:S(2)}) collective-permute-start(f32[1,2304]{1,0:T(1,128)S(1)} %fusion.3), channel_id=1, source_target_pairs={{4,0},{8,4},{12,8},{16,12},{20,16},{24,20},{28,24},{5,1},{9,5},{13... | collective-permute-start | bytes 27656 | tf_op jit(solution)/shard_map/ppermute | solution.py:1096
  504.7 16.9 %collective-permute-start.54 = (f32[2,1024]{1,0:T(2,128)}, f32[2,1024]{1,0:T(2,128)S(1)}, u32[]{:S(2)}, u32[]{:S(2)}) collective-permute-start(f32[2,1024]{1,0:T(2,128)} %after.36.refs_1_), channel_id=1, source_target_pairs={{0,2},{1,3},{2,0},{3,1},{4,6},{5,7},{6,4},{7,5},{8,10},{9,11},{10,... | collective-permute-start | bytes 24584 | tf_op jit(solution)/shard_map/ppermute | solution.py:57
  510.1 27.1 %collective-permute-start.48 = (bf16[256,2304]{1,0:T(8,128)(2,1)}, bf16[256,2304]{1,0:T(8,128)(2,1)}, u32[]{:S(2)}, u32[]{:S(2)}) collective-permute-start(bf16[256,2304]{1,0:T(8,128)(2,1)} %after.34), channel_id=1, source_target_pairs={{0,4},{1,5},{2,6},{3,7},{4,0},{5,1},{6,2},{7,3},{8,12},{9,13},{10,... | collective-permute-start | bytes 3538952 | tf_op jit(solution)/shard_map/ppermute | solution.py:57
  514.8 26.3 %collective-permute-start.47 = (bf16[256,2304]{1,0:T(8,128)(2,1)}, bf16[256,2304]{1,0:T(8,128)(2,1)S(1)}, u32[]{:S(2)}, u32[]{:S(2)}) collective-permute-start(bf16[256,2304]{1,0:T(8,128)(2,1)} %after.33), channel_id=1, source_target_pairs={{0,2},{1,3},{2,0},{3,1},{4,6},{5,7},{6,4},{7,5},{8,10},{9,11},{10,... | collective-permute-start | bytes 3538952 | tf_op jit(solution)/shard_map/ppermute | solution.py:57
  (92 other events, 723.0 us)
Sparse Core Ops, SparseCore 0:
  45.9 91.0 all-gather.2
  138.6 69.0 all-gather.4
  294.2 84.3 reduce-scatter.2
  385.1 65.4 reduce-scatter.4
